TPU v7x, 32 devices: a whole 2x2x4 slice. The times are simulated.
32 devices in a mesh: ctx: 16 (over z, x, core), wa: 2 (over y).
Axes of the slice: x: 2, y: 2, z: 4, core: 2. Of those that a mesh axis runs over, the one named last changes fastest.
Arguments:
- tokens: bfloat16 [2, 2048, 1536], P('wa', 'ctx'), may hold values from -6 to 6
- doc_starts: int32 [2, 16], P('wa'), may hold values from 0 to 2047, as said below
- routes: int32 [2, 2048, 6], P('wa', 'ctx'), may hold values from 0 to 15, all different within a row; in each aligned block of 128 rows (0 to 127, 128 to 255, ..., all dimensions but the last counted through in order) at most 96 rows name the same one
- valid: int32 [2, 2048], P('wa', 'ctx'), may hold values from 0 to 1, as said below
- teacher: bfloat16 [2, 2048, 1536], P('wa', 'ctx'), may hold values from -6 to 6
- out_grad: bfloat16 [2, 2048, 1536], P('wa', 'ctx'), may hold values from -6 to 6
- norm1_gain: bfloat16 [1536], P('wa'), may hold values from 0.5 to 1.5
- w_query: bfloat16 [1536, 1536], P('wa'), may hold values from -0.21875 to 0.21875
- w_key: bfloat16 [1536, 512], P('wa'), may hold values from -0.21875 to 0.21875
- w_value: bfloat16 [1536, 512], P('wa'), may hold values from -0.15625 to 0.15625
- w_out: bfloat16 [1536, 1536], P('wa'), may hold values from -3.5 to 3.5
- norm2_gain: bfloat16 [1536], P('wa'), may hold values from 0.5 to 1.5
- w_router: bfloat16 [1536, 16], P('wa'), may hold values from -0.078125 to 0.078125
- shared_gate: bfloat16 [1536, 1024], P('wa'), may hold values from -0.15625 to 0.15625
- shared_up: bfloat16 [1536, 1024], P('wa'), may hold values from -0.15625 to 0.15625
- shared_down: bfloat16 [1024, 1536], P('wa'), may hold values from -0.1875 to 0.1875
- expert_gate: bfloat16 [16, 1536, 512], P('ctx', 'wa'), may hold values from -0.15625 to 0.15625
- expert_up: bfloat16 [16, 1536, 512], P('ctx', 'wa'), may hold values from -0.15625 to 0.15625
- expert_down: bfloat16 [16, 512, 1536], P('ctx', 'wa'), may hold values from -1 to 1
Outputs:
- loss: float32 [], replicated
- output: bfloat16 [2, 2048, 1536], P('wa', 'ctx')
- input_grad: float32 [2, 2048, 1536], P('wa', 'ctx')
- norm1_gain_grad: float32 [1536], P('wa')
- w_query_grad: float32 [1536, 1536], P('wa')
- w_key_grad: float32 [1536, 512], P('wa')
- w_value_grad: float32 [1536, 512], P('wa')
- w_out_grad: float32 [1536, 1536], P('wa')
- norm2_gain_grad: float32 [1536], P('wa')
- w_router_grad: float32 [1536, 16], P('wa')
- shared_gate_grad: float32 [1536, 1024], P('wa')
- shared_up_grad: float32 [1536, 1024], P('wa')
- shared_down_grad: float32 [1024, 1536], P('wa')
- expert_gate_grad: float32 [16, 1536, 512], P('ctx', 'wa')
- expert_up_grad: float32 [16, 1536, 512], P('ctx', 'wa')
- expert_down_grad: float32 [16, 512, 1536], P('ctx', 'wa')
Inputs may be any that keep to these rules, and one draw needn't show every extreme that they name: `doc_starts`: each row lists the first positions of 16 documents that together cover the 2048 positions of a packed sequence, increasing from 0. The longest document has exactly 1088 positions and is the first or the last of its row. `routes`: each row names 6 different experts. Among the 128 rows that one device holds, no expert is named more than 96 times, and in every draw some expert is named exactly 96 times by one device's rows. `valid`: rows whose index in the stored order is a multiple of 128 are 1.
All inputs are finite; a program needn't handle non-finite values.
Results may differ from a plain program's by a relative error of at most 0.023.
Values may be sent and summed in bfloat16 or wider, within the bound.
A program may use at most 384 MiB of HBM per device.

v0:
```python
import math

import jax
import jax.numpy as jnp
from jax import lax
from jax.sharding import PartitionSpec as P

D = 1536
H = 12
KVH = 4
HD = 128


EPSILON = 1e-05
MASKED_SCORE = -1e30


def keep_state(state_in):
    return state_in


def stored_position(stored_rows, local_rows, ctx_count):
    half_rows = local_rows // 2
    owner_rank = stored_rows // local_rows
    within_rows = stored_rows % local_rows
    first_half = owner_rank * half_rows + within_rows
    second_half = (2 * ctx_count - 1 - owner_rank) * half_rows + within_rows - half_rows
    return jnp.where(within_rows < half_rows, first_half, second_half)


def document_of(positions, doc_first):
    return jnp.sum((doc_first[None, :] <= positions[:, None]).astype(jnp.int32), axis=1) - 1


def matmul(left, right):
    return jnp.dot(left, right, preferred_element_type=jnp.float32)


def contract_rows(left, right):
    return lax.dot_general(
        left, right, (((0,), (0,)), ((), ())), preferred_element_type=jnp.float32
    )


def contract_cols(left, right):
    return lax.dot_general(
        left, right, (((1,), (1,)), ((), ())), preferred_element_type=jnp.float32
    )


def norm_forward(values, gain):
    inverse = lax.rsqrt(jnp.mean(values * values, axis=1, keepdims=True) + EPSILON)
    return (inverse, values * inverse * gain)


def norm_backward(values, inverse, gain, grad_normed):
    scaled = grad_normed * gain
    inner_sum = jnp.sum(scaled * values, axis=1, keepdims=True)
    grad_values = (
        inverse * scaled - values * (inverse * inverse * inverse) * inner_sum / values.shape[1]
    )
    grad_gain = jnp.sum(grad_normed * values * inverse, axis=0)
    return (grad_values, grad_gain)


def silu_grads(grad_hidden, gate_act, up_activation):
    sigmoid_gate = jax.nn.sigmoid(gate_act)
    grad_gate = grad_hidden * up_activation * sigmoid_gate * (1.0 + gate_act * (1.0 - sigmoid_gate))
    grad_up = grad_hidden * gate_act * sigmoid_gate
    return (grad_gate.astype(jnp.bfloat16), grad_up.astype(jnp.bfloat16))


def slot_tables(route_rows, experts, capacity):
    pair_count = route_rows.shape[0] * route_rows.shape[1]
    flat_routes = route_rows.reshape(pair_count)
    one_hot = (flat_routes[:, None] == jnp.arange(experts, dtype=jnp.int32)[None, :]).astype(
        jnp.int32
    )
    slot_rank = jnp.sum((jnp.cumsum(one_hot, axis=0) - 1) * one_hot, axis=1)
    slot_index = flat_routes * capacity + slot_rank
    pair_table = (
        jnp.full((experts * capacity,), pair_count, jnp.int32)
        .at[slot_index]
        .set(jnp.arange(pair_count, dtype=jnp.int32))
    )
    return (slot_index, pair_table)


def visible_pairs(query_pos, query_doc, key_pos, key_doc):
    return (key_pos[None, :] <= query_pos[:, None]) & (key_doc[None, :] == query_doc[:, None])


def block_scores(query_heads, key_part, score_scale):
    return (
        jnp.einsum("tagd,sad->agts", query_heads, key_part, preferred_element_type=jnp.float32)
        * score_scale
    )


def block_probs(query_heads, key_part, visible, log_total, score_scale):
    scores = block_scores(query_heads, key_part, score_scale)
    return jnp.where(visible, jnp.exp(jnp.where(visible, scores, MASKED_SCORE) - log_total), 0.0)


def attend_forward(
    query_heads,
    key_all,
    value_all,
    query_pos,
    query_doc,
    key_pos_all,
    key_doc_all,
    key_width,
    score_scale,
):
    local_rows, kv_heads, groups, head_dim = query_heads.shape
    key_turns = key_all.shape[0] // key_width

    def key_step(block_index, carry_state):
        first_row = block_index * key_width
        key_pos = lax.dynamic_slice_in_dim(key_pos_all, first_row, key_width, 0)
        key_doc = lax.dynamic_slice_in_dim(key_doc_all, first_row, key_width, 0)
        visible = visible_pairs(query_pos, query_doc, key_pos, key_doc)

        def compute(state_in):
            peak_in, total_in, accum_in = state_in
            key_part = lax.dynamic_slice_in_dim(key_all, first_row, key_width, 0).reshape(
                key_width, kv_heads, head_dim
            )
            value_part = lax.dynamic_slice_in_dim(value_all, first_row, key_width, 0).reshape(
                key_width, kv_heads, head_dim
            )
            scores = block_scores(query_heads, key_part, score_scale)
            masked = jnp.where(visible, scores, MASKED_SCORE)
            new_peak = jnp.maximum(peak_in, jnp.max(masked, axis=3, keepdims=True))
            shrink = jnp.exp(peak_in - new_peak)
            weights = jnp.where(visible, jnp.exp(masked - new_peak), 0.0)
            new_total = total_in * shrink + jnp.sum(weights, axis=3, keepdims=True)
            new_accum = accum_in * shrink + jnp.einsum(
                "agts,sad->agtd",
                weights.astype(jnp.bfloat16),
                value_part,
                preferred_element_type=jnp.float32,
            )
            return (new_peak, new_total, new_accum)

        return lax.cond(jnp.any(visible), compute, keep_state, carry_state)

    initial = (
        jnp.full((kv_heads, groups, local_rows, 1), MASKED_SCORE, jnp.float32),
        jnp.zeros((kv_heads, groups, local_rows, 1), jnp.float32),
        jnp.zeros((kv_heads, groups, local_rows, head_dim), jnp.float32),
    )
    row_peak, totals, accumulated = lax.fori_loop(0, key_turns, key_step, initial)
    log_total = row_peak + jnp.log(totals)
    attn_heads = jnp.transpose(accumulated / totals, (2, 0, 1, 3))
    return (log_total, attn_heads.reshape(local_rows, kv_heads * groups * head_dim))


def attend_query_grads(
    query_heads,
    grad_heads,
    key_all,
    value_all,
    log_total,
    delta,
    query_pos,
    query_doc,
    key_pos_all,
    key_doc_all,
    key_width,
    score_scale,
):
    local_rows, kv_heads, groups, head_dim = query_heads.shape

    def key_step(block_index, accumulated):
        first_row = block_index * key_width
        key_pos = lax.dynamic_slice_in_dim(key_pos_all, first_row, key_width, 0)
        key_doc = lax.dynamic_slice_in_dim(key_doc_all, first_row, key_width, 0)
        visible = visible_pairs(query_pos, query_doc, key_pos, key_doc)

        def compute(state_in):
            key_part = lax.dynamic_slice_in_dim(key_all, first_row, key_width, 0).reshape(
                key_width, kv_heads, head_dim
            )
            value_part = lax.dynamic_slice_in_dim(value_all, first_row, key_width, 0).reshape(
                key_width, kv_heads, head_dim
            )
            probs = block_probs(query_heads, key_part, visible, log_total, score_scale)
            grad_probs = jnp.einsum(
                "tagd,sad->agts", grad_heads, value_part, preferred_element_type=jnp.float32
            )
            grad_scores = (probs * (grad_probs - delta)).astype(jnp.bfloat16)
            return state_in + jnp.einsum(
                "agts,sad->tagd", grad_scores, key_part, preferred_element_type=jnp.float32
            )

        return lax.cond(jnp.any(visible), compute, keep_state, accumulated)

    result = lax.fori_loop(
        0, key_all.shape[0] // key_width, key_step, jnp.zeros(query_heads.shape, jnp.float32)
    )
    return result * score_scale


def key_value_grads(
    query_heads,
    grad_heads,
    log_total,
    delta,
    query_pos,
    query_doc,
    key_part,
    value_part,
    key_pos,
    key_doc,
    score_scale,
):
    key_count = key_part.shape[0]
    kv_width = key_part.shape[1] * key_part.shape[2]
    visible = visible_pairs(query_pos, query_doc, key_pos, key_doc)

    def compute(unused):
        probs = block_probs(query_heads, key_part, visible, log_total, score_scale)
        grad_probs = jnp.einsum(
            "tagd,sad->agts", grad_heads, value_part, preferred_element_type=jnp.float32
        )
        grad_scores = (probs * (grad_probs - delta)).astype(jnp.bfloat16)
        grad_keys = (
            jnp.einsum(
                "agts,tagd->sad", grad_scores, query_heads, preferred_element_type=jnp.float32
            )
            * score_scale
        )
        grad_values = jnp.einsum(
            "agts,tagd->sad",
            probs.astype(jnp.bfloat16),
            grad_heads,
            preferred_element_type=jnp.float32,
        )
        return jnp.concatenate(
            [grad_keys.reshape(key_count, kv_width), grad_values.reshape(key_count, kv_width)],
            axis=1,
        )

    def nothing(unused):
        return jnp.zeros((key_count, 2 * kv_width), jnp.float32)

    return lax.cond(jnp.any(visible), compute, nothing, 0)


def per_device(
    tokens,
    doc_starts,
    routes,
    valid,
    teacher,
    out_grad,
    norm1_gain,
    w_query,
    w_key,
    w_value,
    w_out,
    norm2_gain,
    w_router,
    shared_gate,
    shared_up,
    shared_down,
    expert_gate,
    expert_up,
    expert_down,
):
    ctx_count = lax.axis_size("ctx")
    ctx_rank = lax.axis_index("ctx")
    wa_count = lax.axis_size("wa")
    local_rows = tokens.shape[1]
    seq_len = local_rows * ctx_count
    key_width = min(seq_len, 1024)
    groups = H // KVH
    kv_width = KVH * HD
    score_scale = HD ** (-0.5)
    topk_count = routes.shape[2]
    experts = w_router.shape[1]
    capacity = max(2, 2 * local_rows * topk_count // experts)
    (
        gain_one,
        weight_query,
        weight_key,
        weight_value,
        weight_out,
        gain_two,
        weight_router,
        weight_sgate,
        weight_sup,
        weight_sdown,
    ) = (
        lax.all_gather(norm1_gain, "wa", axis=0, tiled=True),
        lax.all_gather(w_query, "wa", axis=0, tiled=True),
        lax.all_gather(w_key, "wa", axis=0, tiled=True),
        lax.all_gather(w_value, "wa", axis=0, tiled=True),
        lax.all_gather(w_out, "wa", axis=0, tiled=True),
        lax.all_gather(norm2_gain, "wa", axis=0, tiled=True),
        lax.all_gather(w_router, "wa", axis=0, tiled=True),
        lax.all_gather(shared_gate, "wa", axis=0, tiled=True),
        lax.all_gather(shared_up, "wa", axis=0, tiled=True),
        lax.all_gather(shared_down, "wa", axis=0, tiled=True),
    )
    expert_gate_weight, expert_up_weight, expert_down_weight = (
        lax.all_gather(expert_gate, "wa", axis=1, tiled=True),
        lax.all_gather(expert_up, "wa", axis=1, tiled=True),
        lax.all_gather(expert_down, "wa", axis=1, tiled=True),
    )
    gain_one_f = gain_one.astype(jnp.float32)
    gain_two_f = gain_two.astype(jnp.float32)
    resident_experts = expert_gate_weight.shape[0]
    doc_first = doc_starts[0]
    own_rows = ctx_rank * local_rows + jnp.arange(local_rows, dtype=jnp.int32)
    query_pos = stored_position(own_rows, local_rows, ctx_count)
    query_doc = document_of(query_pos, doc_first)
    key_pos_all = stored_position(jnp.arange(seq_len, dtype=jnp.int32), local_rows, ctx_count)
    key_doc_all = document_of(key_pos_all, doc_first)
    residual_stream = tokens[0].astype(jnp.float32)
    inverse_one, normed = norm_forward(residual_stream, gain_one_f)
    normed_one = normed.astype(jnp.bfloat16)
    queries = matmul(normed_one, weight_query).astype(jnp.bfloat16)
    key_rows = matmul(normed_one, weight_key).astype(jnp.bfloat16)
    value_rows = matmul(normed_one, weight_value).astype(jnp.bfloat16)
    key_all, value_all = (
        lax.all_gather(key_rows, "ctx", axis=0, tiled=True),
        lax.all_gather(value_rows, "ctx", axis=0, tiled=True),
    )
    query_heads = queries.reshape(local_rows, KVH, groups, HD)
    log_total, attn_f32 = attend_forward(
        query_heads,
        key_all,
        value_all,
        query_pos,
        query_doc,
        key_pos_all,
        key_doc_all,
        key_width,
        score_scale,
    )
    attn_low = attn_f32.astype(jnp.bfloat16)
    hidden_one = residual_stream + matmul(attn_low, weight_out)
    inverse_two, normed = norm_forward(hidden_one, gain_two_f)
    normed_two = normed.astype(jnp.bfloat16)
    logits = matmul(normed_two, weight_router)
    route_rows = routes[0]
    choose = (route_rows[:, :, None] == jnp.arange(experts, dtype=jnp.int32)[None, None, :]).astype(
        jnp.float32
    )
    picked_logits = jnp.sum(choose * logits[:, None, :], axis=2)
    gates = jax.nn.softmax(picked_logits, axis=1)
    shared_g_act = matmul(normed_two, weight_sgate)
    shared_u_act = matmul(normed_two, weight_sup)
    shared_hidden = (jax.nn.silu(shared_g_act) * shared_u_act).astype(jnp.bfloat16)
    shared_out = matmul(shared_hidden, weight_sdown)
    slot_index, pair_table = slot_tables(route_rows, experts, capacity)
    padded = jnp.concatenate([normed_two, jnp.zeros((1, D), jnp.bfloat16)], axis=0)
    sent_rows = padded[pair_table // topk_count].reshape(experts, capacity, D)
    arrived_tokens = lax.all_to_all(
        sent_rows, "ctx", split_axis=0, concat_axis=0, tiled=True
    ).reshape(ctx_count, resident_experts, capacity, D)
    gate_act = jnp.einsum(
        "rqel,qlo->rqeo", arrived_tokens, expert_gate_weight, preferred_element_type=jnp.float32
    )
    up_activation = jnp.einsum(
        "rqel,qlo->rqeo", arrived_tokens, expert_up_weight, preferred_element_type=jnp.float32
    )
    hidden_exp = (jax.nn.silu(gate_act) * up_activation).astype(jnp.bfloat16)
    expert_out = jnp.einsum(
        "sacf,afd->sacd", hidden_exp, expert_down_weight, preferred_element_type=jnp.float32
    ).astype(jnp.bfloat16)
    returned = lax.all_to_all(
        expert_out.reshape(experts, capacity, D), "ctx", split_axis=0, concat_axis=0, tiled=True
    ).reshape(experts * capacity, D)
    picked = returned[slot_index].reshape(local_rows, topk_count, D).astype(jnp.float32)
    routed = jnp.einsum("tk,tkd->td", gates, picked)
    produced = hidden_one + shared_out + routed
    output = produced.astype(jnp.bfloat16)[None]
    valid_rows = valid[0].astype(jnp.float32)
    errors = produced - teacher[0].astype(jnp.float32)
    local_error = jnp.sum(valid_rows[:, None] * errors * errors)
    local_valid = jnp.sum(valid_rows)
    valid_total, error_total = lax.psum((local_valid, local_error), ("ctx", "wa"))
    loss_value = error_total / (valid_total * D)
    tokens_all = wa_count * seq_len
    grad_out = (
        out_grad[0].astype(jnp.float32)
        + 2.0 * tokens_all / valid_total * valid_rows[:, None] * errors
    )
    grad_low = grad_out.astype(jnp.bfloat16)
    grad_shared_hidden = contract_cols(grad_low, weight_sdown)
    grad_sgate, grad_sup = silu_grads(grad_shared_hidden, shared_g_act, shared_u_act)
    grad_normed = contract_cols(grad_sgate, weight_sgate) + contract_cols(grad_sup, weight_sup)
    grad_picked = (gates[:, :, None] * grad_out[:, None, :]).astype(jnp.bfloat16)
    pair_padded = jnp.concatenate(
        [grad_picked.reshape(local_rows * topk_count, D), jnp.zeros((1, D), jnp.bfloat16)], axis=0
    )
    grad_sent = pair_padded[pair_table].reshape(experts, capacity, D)
    grad_received = lax.all_to_all(
        grad_sent, "ctx", split_axis=0, concat_axis=0, tiled=True
    ).reshape(ctx_count, resident_experts, capacity, D)
    grad_gates = jnp.einsum("td,tkd->tk", grad_out, picked)
    grad_selected = gates * (grad_gates - jnp.sum(gates * grad_gates, axis=1, keepdims=True))
    grad_logits = jnp.einsum("tk,tke->te", grad_selected, choose).astype(jnp.bfloat16)
    grad_normed = grad_normed + contract_cols(grad_logits, weight_router)
    grad_hidden_exp = jnp.einsum(
        "sacd,afd->sacf", grad_received, expert_down_weight, preferred_element_type=jnp.float32
    )
    grad_gate_act, gradient_up_activation = silu_grads(grad_hidden_exp, gate_act, up_activation)
    grad_expert_down = jnp.einsum(
        "sacf,sacd->afd", hidden_exp, grad_received, preferred_element_type=jnp.float32
    )
    grad_expert_gate = jnp.einsum(
        "sacd,sacf->adf", arrived_tokens, grad_gate_act, preferred_element_type=jnp.float32
    )
    grad_expert_up = jnp.einsum(
        "sacd,sacf->adf", arrived_tokens, gradient_up_activation, preferred_element_type=jnp.float32
    )
    grad_rows_exp = (
        jnp.einsum(
            "ezrj,zoj->ezro", grad_gate_act, expert_gate_weight, preferred_element_type=jnp.float32
        )
        + jnp.einsum(
            "ezrj,zoj->ezro",
            gradient_up_activation,
            expert_up_weight,
            preferred_element_type=jnp.float32,
        )
    ).astype(jnp.bfloat16)
    grad_back = lax.all_to_all(
        grad_rows_exp.reshape(experts, capacity, D), "ctx", split_axis=0, concat_axis=0, tiled=True
    ).reshape(experts * capacity, D)
    grad_normed = grad_normed + jnp.sum(
        grad_back[slot_index].reshape(local_rows, topk_count, D).astype(jnp.float32), axis=1
    )
    expert_gate_sum, expert_up_sum, expert_down_sum = (
        lax.psum_scatter(
            grad_expert_gate.astype(jnp.bfloat16), "wa", scatter_dimension=1, tiled=True
        ).astype(jnp.float32),
        lax.psum_scatter(
            grad_expert_up.astype(jnp.bfloat16), "wa", scatter_dimension=1, tiled=True
        ).astype(jnp.float32),
        lax.psum_scatter(
            grad_expert_down.astype(jnp.bfloat16), "wa", scatter_dimension=1, tiled=True
        ).astype(jnp.float32),
    )
    grad_hidden_norm, grad_gain_two = norm_backward(
        hidden_one, inverse_two, gain_two_f, grad_normed
    )
    grad_hidden_one = grad_out + grad_hidden_norm
    grad_attn_in = grad_hidden_one.astype(jnp.bfloat16)
    grad_attn_low = contract_cols(grad_attn_in, weight_out).astype(jnp.bfloat16)
    grad_heads = grad_attn_low.reshape(local_rows, KVH, groups, HD)
    delta = jnp.einsum(
        "tagd,tagd->agt",
        grad_heads.astype(jnp.float32),
        attn_f32.reshape(local_rows, KVH, groups, HD),
    )[:, :, :, None]
    grad_query_low = (
        attend_query_grads(
            query_heads,
            grad_heads,
            key_all,
            value_all,
            log_total,
            delta,
            query_pos,
            query_doc,
            key_pos_all,
            key_doc_all,
            key_width,
            score_scale,
        )
        .reshape(local_rows, H * HD)
        .astype(jnp.bfloat16)
    )
    sub_rows = math.gcd(local_rows * lax.axis_size("ctx"), key_width)

    def one_piece(piece_index):
        piece_first = piece_index * sub_rows
        key_part = lax.dynamic_slice_in_dim(key_all, piece_first, sub_rows, 0).reshape(
            sub_rows, KVH, HD
        )
        value_part = lax.dynamic_slice_in_dim(value_all, piece_first, sub_rows, 0).reshape(
            sub_rows, KVH, HD
        )
        key_pos = lax.dynamic_slice_in_dim(key_pos_all, piece_first, sub_rows, 0)
        key_doc = lax.dynamic_slice_in_dim(key_doc_all, piece_first, sub_rows, 0)
        return key_value_grads(
            query_heads,
            grad_heads,
            log_total,
            delta,
            query_pos,
            query_doc,
            key_part,
            value_part,
            key_pos,
            key_doc,
            score_scale,
        )

    pieces = lax.map(
        one_piece, jnp.arange(local_rows * lax.axis_size("ctx") // sub_rows, dtype=jnp.int32)
    )
    key_value_grad = lax.psum_scatter(
        pieces.reshape(local_rows * lax.axis_size("ctx"), 2 * kv_width),
        "ctx",
        scatter_dimension=0,
        tiled=True,
    )
    grad_key_low = key_value_grad[:, :kv_width].astype(jnp.bfloat16)
    grad_value_low = key_value_grad[:, kv_width:].astype(jnp.bfloat16)
    grad_normed_one = (
        contract_cols(grad_query_low, weight_query)
        + contract_cols(grad_key_low, weight_key)
        + contract_cols(grad_value_low, weight_value)
    )
    grad_residual_norm, grad_gain_one = norm_backward(
        residual_stream, inverse_one, gain_one_f, grad_normed_one
    )
    grad_input = grad_hidden_one + grad_residual_norm
    grad_weight_out = contract_rows(attn_low, grad_attn_in)
    grad_router = contract_rows(normed_two, grad_logits)
    grad_shared_down = contract_rows(shared_hidden, grad_low)
    grad_shared_gate = contract_rows(normed_two, grad_sgate)
    grad_shared_up = contract_rows(normed_two, grad_sup)
    grad_weight_query = contract_rows(normed_one, grad_query_low)
    grad_weight_key = contract_rows(normed_one, grad_key_low)
    grad_weight_value = contract_rows(normed_one, grad_value_low)
    (
        shard_gain_one,
        shard_query,
        shard_key,
        shard_value,
        shard_out,
        shard_gain_two,
        shard_router,
        shard_sgate,
        shard_sup,
        shard_sdown,
    ) = (
        lax.psum_scatter(
            grad_gain_one.astype(jnp.bfloat16), "wa", scatter_dimension=0, tiled=True
        ).astype(jnp.float32),
        lax.psum_scatter(
            grad_weight_query.astype(jnp.bfloat16), "wa", scatter_dimension=0, tiled=True
        ).astype(jnp.float32),
        lax.psum_scatter(
            grad_weight_key.astype(jnp.bfloat16), "wa", scatter_dimension=0, tiled=True
        ).astype(jnp.float32),
        lax.psum_scatter(
            grad_weight_value.astype(jnp.bfloat16), "wa", scatter_dimension=0, tiled=True
        ).astype(jnp.float32),
        lax.psum_scatter(
            grad_weight_out.astype(jnp.bfloat16), "wa", scatter_dimension=0, tiled=True
        ).astype(jnp.float32),
        lax.psum_scatter(
            grad_gain_two.astype(jnp.bfloat16), "wa", scatter_dimension=0, tiled=True
        ).astype(jnp.float32),
        lax.psum_scatter(
            grad_router.astype(jnp.bfloat16), "wa", scatter_dimension=0, tiled=True
        ).astype(jnp.float32),
        lax.psum_scatter(
            grad_shared_gate.astype(jnp.bfloat16), "wa", scatter_dimension=0, tiled=True
        ).astype(jnp.float32),
        lax.psum_scatter(
            grad_shared_up.astype(jnp.bfloat16), "wa", scatter_dimension=0, tiled=True
        ).astype(jnp.float32),
        lax.psum_scatter(
            grad_shared_down.astype(jnp.bfloat16), "wa", scatter_dimension=0, tiled=True
        ).astype(jnp.float32),
    )
    (
        total_gain_one,
        total_query,
        total_key,
        total_value,
        total_out,
        total_gain_two,
        total_router,
        total_sgate,
        total_sup,
        total_sdown,
    ) = lax.psum(
        (
            shard_gain_one,
            shard_query,
            shard_key,
            shard_value,
            shard_out,
            shard_gain_two,
            shard_router,
            shard_sgate,
            shard_sup,
            shard_sdown,
        ),
        "ctx",
    )
    return (
        loss_value,
        output,
        grad_input[None],
        total_gain_one,
        total_query,
        total_key,
        total_value,
        total_out,
        total_gain_two,
        total_router,
        total_sgate,
        total_sup,
        total_sdown,
        expert_gate_sum,
        expert_up_sum,
        expert_down_sum,
    )


def solution(mesh):
    return jax.shard_map(
        per_device,
        mesh=mesh,
        in_specs=(
            P("wa", "ctx", None),
            P("wa", None),
            P("wa", "ctx", None),
            P("wa", "ctx"),
            P("wa", "ctx", None),
            P("wa", "ctx", None),
            P("wa"),
            P("wa", None),
            P("wa", None),
            P("wa", None),
            P("wa", None),
            P("wa"),
            P("wa", None),
            P("wa", None),
            P("wa", None),
            P("wa", None),
            P("ctx", "wa", None),
            P("ctx", "wa", None),
            P("ctx", "wa", None),
        ),
        out_specs=(
            P(),
            P("wa", "ctx", None),
            P("wa", "ctx", None),
            P("wa"),
            P("wa", None),
            P("wa", None),
            P("wa", None),
            P("wa", None),
            P("wa"),
            P("wa", None),
            P("wa", None),
            P("wa", None),
            P("wa", None),
            P("ctx", "wa", None),
            P("ctx", "wa", None),
            P("ctx", "wa", None),
        ),
        check_vma=False,
    )
```

profile of v0, /device:TPU:1, one launch (start us, length us, event | category | flops | bytes accessed | tf_op | source)
XLA Modules:
  0.0 1936.5 jit_solution(5795369531038442761)
XLA Ops:
  41.5 26.2 %all-gather.21.cloned.1.call-done = bf16[1536,512]{1,0:T(8,128)(2,1)} async-done(((bf16[768,512]{1,0:T(8,128)(2,1)}), bf16[1536,512]{1,0:T(8,128)(2,1)}) %all-gather.21.cloned.1.call-update) | async-done | bytes 1572880 | tf_op jit(solution)/shard_map/all_gather | solution.py:300
  82.5 49.5 %all-gather.19.cloned.1.call-done = bf16[1536,1536]{1,0:T(8,128)(2,1)} async-done(((bf16[768,1536]{1,0:T(8,128)(2,1)}), bf16[1536,1536]{1,0:T(8,128)(2,1)}) %all-gather.19.cloned.1.call-update) | async-done | bytes 4718608 | tf_op jit(solution)/shard_map/all_gather | solution.py:298
  136.1 40.3 %all-gather.17.cloned.1.call-done = bf16[2048,512]{1,0:T(8,128)(2,1)} async-done(((bf16[128,512]{1,0:T(8,128)(2,1)}), bf16[2048,512]{1,0:T(8,128)(2,1)}) %all-gather.17.cloned.1.call-update) | async-done | bytes 2097168 | tf_op jit(solution)/shard_map/all_gather | solution.py:329
  179.3 39.9 %all-gather.23.cloned.1.call-done = bf16[2048,512]{1,0:T(8,128)(2,1)} async-done(((bf16[128,512]{1,0:T(8,128)(2,1)}), bf16[2048,512]{1,0:T(8,128)(2,1)}) %all-gather.23.cloned.1.call-update) | async-done | bytes 2097168 | tf_op jit(solution)/shard_map/all_gather | solution.py:330
  248.0 33.6 %all-gather.25.cloned.1.call-done = bf16[1536,1536]{1,0:T(8,128)(2,1)} async-done(((bf16[768,1536]{1,0:T(8,128)(2,1)}), bf16[1536,1536]{1,0:T(8,128)(2,1)}) %all-gather.25.cloned.1.call-update) | async-done | bytes 4718608 | tf_op jit(solution)/shard_map/all_gather | solution.py:301
  301.1 26.6 %all-gather.33.cloned.1.call-done = bf16[1,1536,512]{2,1,0:T(8,128)(2,1)} async-done(((bf16[1,768,512]{2,1,0:T(8,128)(2,1)}), bf16[1,1536,512]{2,1,0:T(8,128)(2,1)}) %all-gather.33.cloned.1.call-update) | async-done | bytes 1572880 | tf_op jit(solution)/shard_map/all_gather | solution.py:309
  327.8 57.8 %all-to-all-done = bf16[16,96,1536]{2,1,0:T(8,128)(2,1)} async-done(((bf16[16,96,1536]{2,1,0:T(8,128)(2,1)}), bf16[16,96,1536]{2,1,0:T(8,128)(2,1)}, u32[]{:S(2)}, u32[]{:S(2)}) %all-to-all-start) | async-done | bytes 4718624 | tf_op jit(solution)/shard_map/all_to_all | solution.py:362
  438.2 40.1 %all-gather.29.cloned.1.call-done = bf16[1536,1024]{1,0:T(8,128)(2,1)} async-done(((bf16[768,1024]{1,0:T(8,128)(2,1)}), bf16[1536,1024]{1,0:T(8,128)(2,1)}) %all-gather.29.cloned.1.call-update) | async-done | bytes 3145744 | tf_op jit(solution)/shard_map/all_gather | solution.py:305
  481.6 34.2 %all-to-all-done.1 = bf16[16,96,1536]{2,1,0:T(8,128)(2,1)} async-done(((bf16[16,96,1536]{2,1,0:T(8,128)(2,1)}), bf16[16,96,1536]{2,1,0:T(8,128)(2,1)}, u32[]{:S(2)}, u32[]{:S(2)}) %all-to-all-start.1) | async-done | bytes 4718624 | tf_op jit(solution)/shard_map/all_to_all | solution.py:375
  532.6 55.9 %all-reduce.4 = (f32[]{:T(128)}, f32[]{:T(128)}) all-reduce(f32[]{:T(128)} %get-tuple-element.1006, f32[]{:T(128)} %convert_reduce_fusion.4), channel_id=1, replica_groups=mesh['ctx'=16,'wa'=2] {'ctx','wa'}, use_global_device_ids=true, to_apply=%region_19.20 | all-reduce | flops 2 | bytes 16 | tf_op jit(solution)/shard_map/psum | solution.py:386
  610.6 110.6 %all_to_all.20 = bf16[16,96,1536]{2,1,0:T(8,128)(2,1)S(1)} all-to-all(bf16[16,96,1536]{2,1,0:T(8,128)(2,1)} %bitcast.426), channel_id=1, replica_groups=mesh['ctx'=16,'wa'=2] {'ctx'}, dimensions={0} | all-to-all | bytes 9437184 | tf_op jit(solution)/shard_map/all_to_all | solution.py:402
  747.8 76.5 %all-to-all-done.3 = bf16[16,96,1536]{2,1,0:T(8,128)(2,1)} async-done(((bf16[16,96,1536]{2,1,0:T(8,128)(2,1)}), bf16[16,96,1536]{2,1,0:T(8,128)(2,1)}, u32[]{:S(2)}, u32[]{:S(2)}) %all-to-all-start.3) | async-done | bytes 4718624 | tf_op jit(solution)/shard_map/all_to_all | solution.py:433
  853.8 70.8 %while.48 = (s32[]{:T(128)}, f32[2,1024,1024]{2,1,0:T(8,128)}, s32[2]{0:T(128)S(1)}, s32[2048]{0:T(1024)S(1)}, s32[2048]{0:T(1024)}, /*index=5*/s32[128]{0:T(128...) while((s32[]{:T(128)}, f32[2,1024,1024]{2,1,0:T(8,128)}, ...), condition=%wide.region_34.35_spmd.clone, body=%wide.region_30.34_spmd.clone.sunk | while | flops 1631587840 | bytes 64926152 | solution.py:506
  963.6 34.4 %while.47 = (s32[]{:T(128)}, f32[128,4,3,128]{0,3,2,1:T(8,128)}, s32[2048]{0:T(1024)S(1)}, s32[2048]{0:T(1024)}, s32[128]{0:T(128)}, /*index=5*/bf16[2048,512]{0...) while((s32[]{:T(128)}, f32[128,4,3,128]{0,3,2,1:T(8,128)}, ...), condition=%wide.region_29.30_spmd.clone, body=%wide.region_25.29_spmd.clone.sunk | while | flops 1219694080 | bytes 22583116 | solution.py:200
  1004.0 40.8 %reduce-scatter.13.cloned.1.call-done = f32[128,1024]{1,0:T(8,128)} async-done(((f32[2048,1024]{1,0:T(8,128)}), f32[128,1024]{1,0:T(8,128)}) %reduce-scatter.13.cloned.1.call-update) | async-done | bytes 524304 | tf_op jit(solution)/shard_map/reduce_scatter | solution.py:509
  1056.5 46.5 %reduce-scatter.25.cloned.1.call-done = bf16[768,1024]{1,0:T(8,128)(2,1)} async-done(((bf16[1536,1024]{1,0:T(8,128)(2,1)}), bf16[768,1024]{1,0:T(8,128)(2,1)}) %reduce-scatter.25.cloned.1.call-update) | async-done | bytes 1572880 | tf_op jit(solution)/shard_map/reduce_scatter | solution.py:567
  1103.0 46.1 %reduce-scatter.27.cloned.1.call-done = bf16[768,1024]{1,0:T(8,128)(2,1)} async-done(((bf16[1536,1024]{1,0:T(8,128)(2,1)}), bf16[768,1024]{1,0:T(8,128)(2,1)}) %reduce-scatter.27.cloned.1.call-update) | async-done | bytes 1572880 | tf_op jit(solution)/shard_map/reduce_scatter | solution.py:570
  1149.1 46.0 %reduce-scatter.29.cloned.1.call-done = bf16[512,1536]{1,0:T(8,128)(2,1)} async-done(((bf16[1024,1536]{1,0:T(8,128)(2,1)}), bf16[512,1536]{1,0:T(8,128)(2,1)}) %reduce-scatter.29.cloned.1.call-update) | async-done | bytes 1572880 | tf_op jit(solution)/shard_map/reduce_scatter | solution.py:573
  1195.2 28.3 %reduce-scatter.35.cloned.1.call-done = bf16[1,256,1536]{2,1,0:T(8,128)(2,1)} async-done(((bf16[1,512,1536]{2,1,0:T(8,128)(2,1)}), bf16[1,256,1536]{2,1,0:T(8,128)(2,1)}) %reduce-scatter.35.cloned.1.call-update) | async-done | bytes 786448 | tf_op jit(solution)/shard_map/reduce_scatter | solution.py:446
  1225.9 26.5 %reduce-scatter.31.cloned.1.call-done = bf16[1,768,512]{2,1,0:T(8,128)(2,1)} async-done(((bf16[1,1536,512]{2,1,0:T(8,128)(2,1)}), bf16[1,768,512]{2,1,0:T(8,128)(2,1)}) %reduce-scatter.31.cloned.1.call-update) | async-done | bytes 786448 | tf_op jit(solution)/shard_map/reduce_scatter | solution.py:440
  1287.2 56.4 %reduce-scatter.21.cloned.1.call-done = bf16[768,1536]{1,0:T(8,128)(2,1)} async-done(((bf16[1536,1536]{1,0:T(8,128)(2,1)}), bf16[768,1536]{1,0:T(8,128)(2,1)}) %reduce-scatter.21.cloned.1.call-update) | async-done | bytes 2359312 | tf_op jit(solution)/shard_map/reduce_scatter | solution.py:558
  1343.6 63.0 %reduce-scatter.15.cloned.1.call-done = bf16[768,1536]{1,0:T(8,128)(2,1)} async-done(((bf16[1536,1536]{1,0:T(8,128)(2,1)}), bf16[768,1536]{1,0:T(8,128)(2,1)}) %reduce-scatter.15.cloned.1.call-update) | async-done | bytes 2359312 | tf_op jit(solution)/shard_map/reduce_scatter | solution.py:549
  1435.6 28.9 %reduce-scatter.19.cloned.1.call-done = bf16[768,512]{1,0:T(8,128)(2,1)} async-done(((bf16[1536,512]{1,0:T(8,128)(2,1)}), bf16[768,512]{1,0:T(8,128)(2,1)}) %reduce-scatter.19.cloned.1.call-update) | async-done | bytes 786448 | tf_op jit(solution)/shard_map/reduce_scatter | solution.py:555
  1464.5 463.9 %all-reduce.8 = (f32[768]{0:T(1024)}, f32[768,1536]{1,0:T(8,128)}, f32[768,512]{1,0:T(8,128)}, f32[768,512]{1,0:T(8,128)}, f32[768,1536]{1,0:T(8,128)}, /*index=...) all-reduce(f32[768]{0:T(1024)} %dynamic-slice_convert_fusion.1, ...), channel_id=1, replica_groups=mesh['ctx'=16,'wa'=2] {'ctx'}, use_global_device_ids=true, to_apply=%region_39.40 | all-reduce | flops 5518848 | bytes 33116160 | tf_op jit(solution)/shard_map/psum | solution.py:588
  (417 shorter events, 574.8 us)
Async XLA Ops:
  7.9 59.8 %all-gather.21.cloned.1.call-start = ((), (), s32[]{:S(2)}) async-start(), calls=%async_computation.19 | async-start | bytes 2359296 | tf_op jit(solution)/shard_map/all_gather | solution.py:300
  8.7 123.2 %all-gather.19.cloned.1.call-start = ((), (), s32[]{:S(2)}) async-start(), calls=%async_computation.18 | async-start | bytes 7077888 | tf_op jit(solution)/shard_map/all_gather | solution.py:298
  9.4 167.0 %all-gather.17.cloned.1.call-start = ((), (), s32[]{:S(2)}) async-start(), calls=%async_computation.17 | async-start | bytes 2228224 | tf_op jit(solution)/shard_map/all_gather | solution.py:329
  41.5 177.7 %all-gather.23.cloned.1.call-start = ((), (), s32[]{:S(2)}) async-start(), calls=%async_computation.20 | async-start | bytes 2228224 | tf_op jit(solution)/shard_map/all_gather | solution.py:330
  70.2 211.4 %all-gather.25.cloned.1.call-start = ((), (), s32[]{:S(2)}) async-start(), calls=%async_computation.21 | async-start | bytes 7077888 | tf_op jit(solution)/shard_map/all_gather | solution.py:301
  292.1 93.4 %all-to-all-start = ((bf16[16,96,1536]{2,1,0:T(8,128)(2,1)}), bf16[16,96,1536]{2,1,0:T(8,128)(2,1)}, u32[]{:S(2)}, u32[]{:S(2)}) async-start(bf16[16,96,1536]{2,1,0:T(8,128)(2,1)} %bitcast.425), calls=%async_computation | async-start | bytes 9437184 | tf_op jit(solution)/shard_map/all_to_all | solution.py:362
  299.1 93.6 %all-gather.35.cloned.1.call-start = ((), (), s32[]{:S(2)}) async-start(), calls=%async_computation.26 | async-start | bytes 2359296 | tf_op jit(solution)/shard_map/all_gather | solution.py:310
  299.8 102.1 %all-gather.37.cloned.1.call-start = ((), (), s32[]{:S(2)}) async-start(), calls=%async_computation.27 | async-start | bytes 2359296 | tf_op jit(solution)/shard_map/all_gather | solution.py:311
  300.5 135.1 %all-gather.27.cloned.1.call-start = ((), (), s32[]{:S(2)}) async-start(), calls=%async_computation.22 | async-start | bytes 4718592 | tf_op jit(solution)/shard_map/all_gather | solution.py:304
  408.1 107.7 %all-to-all-start.1 = ((bf16[16,96,1536]{2,1,0:T(8,128)(2,1)}), bf16[16,96,1536]{2,1,0:T(8,128)(2,1)}, u32[]{:S(2)}, u32[]{:S(2)}) async-start(bf16[16,96,1536]{2,1,0:T(8,128)(2,1)} %convolution_convert_fusion.2), calls=%async_computation.1 | async-start | bytes 9437184 | tf_op jit(solution)/shard_map/all_to_all | solution.py:375
  429.3 100.0 %all-gather.31.cloned.1.call-start = ((), (), s32[]{:S(2)}) async-start(), calls=%async_computation.24 | async-start | bytes 4718592 | tf_op jit(solution)/shard_map/all_gather | solution.py:306
  732.0 92.3 %all-to-all-start.3 = ((bf16[16,96,1536]{2,1,0:T(8,128)(2,1)}), bf16[16,96,1536]{2,1,0:T(8,128)(2,1)}, u32[]{:S(2)}, u32[]{:S(2)}) async-start(bf16[16,96,1536]{2,1,0:T(8,128)(2,1)} %add_convert_fusion), calls=%async_computation.3 | async-start | bytes 9437184 | tf_op jit(solution)/shard_map/all_to_all | solution.py:433
  737.1 307.6 %reduce-scatter.13.cloned.1.call-start = ((), (), s32[]{:S(2)}) async-start(), calls=%async_computation.28 | async-start | bytes 8912896 | tf_op jit(solution)/shard_map/reduce_scatter | solution.py:509
  925.2 131.3 %reduce-scatter.23.cloned.1.call-start = ((), (), s32[]{:S(2)}) async-start(), calls=%async_computation.33 | async-start | bytes 73728 | tf_op jit(solution)/shard_map/reduce_scatter | solution.py:564
  926.4 176.6 %reduce-scatter.25.cloned.1.call-start = ((), (), s32[]{:S(2)}) async-start(), calls=%async_computation.34 | async-start | bytes 4718592 | tf_op jit(solution)/shard_map/reduce_scatter | solution.py:567
  929.2 219.9 %reduce-scatter.27.cloned.1.call-start = ((), (), s32[]{:S(2)}) async-start(), calls=%async_computation.35 | async-start | bytes 4718592 | tf_op jit(solution)/shard_map/reduce_scatter | solution.py:570
  933.0 262.2 %reduce-scatter.29.cloned.1.call-start = ((), (), s32[]{:S(2)}) async-start(), calls=%async_computation.36 | async-start | bytes 4718592 | tf_op jit(solution)/shard_map/reduce_scatter | solution.py:573
  935.7 287.7 %reduce-scatter.35.cloned.1.call-start = ((), (), s32[]{:S(2)}) async-start(), calls=%async_computation.39 | async-start | bytes 2359296 | tf_op jit(solution)/shard_map/reduce_scatter | solution.py:446
  942.9 309.6 %reduce-scatter.31.cloned.1.call-start = ((), (), s32[]{:S(2)}) async-start(), calls=%async_computation.37 | async-start | bytes 2359296 | tf_op jit(solution)/shard_map/reduce_scatter | solution.py:440
  949.6 331.1 %reduce-scatter.33.cloned.1.call-start = ((), (), s32[]{:S(2)}) async-start(), calls=%async_computation.38 | async-start | bytes 2359296 | tf_op jit(solution)/shard_map/reduce_scatter | solution.py:443
  957.0 386.6 %reduce-scatter.21.cloned.1.call-start = ((), (), s32[]{:S(2)}) async-start(), calls=%async_computation.32 | async-start | bytes 7077888 | tf_op jit(solution)/shard_map/reduce_scatter | solution.py:558
  960.7 445.9 %reduce-scatter.15.cloned.1.call-start = ((), (), s32[]{:S(2)}) async-start(), calls=%async_computation.29 | async-start | bytes 7077888 | tf_op jit(solution)/shard_map/reduce_scatter | solution.py:549
  1003.9 431.7 %reduce-scatter.17.cloned.1.call-start = ((), (), s32[]{:S(2)}) async-start(), calls=%async_computation.30 | async-start | bytes 2359296 | tf_op jit(solution)/shard_map/reduce_scatter | solution.py:552
  1047.7 416.8 %reduce-scatter.19.cloned.1.call-start = ((), (), s32[]{:S(2)}) async-start(), calls=%async_computation.31 | async-start | bytes 2359296 | tf_op jit(solution)/shard_map/reduce_scatter | solution.py:555
  (84 other events, 2486.0 us)
Sparse Core Ops, SparseCore 0:
  9.6 29.2 all-gather.14
  40.4 27.2 all-gather.20
  69.2 62.6 all-gather.18
  134.5 41.8 all-gather.16
  179.0 40.1 all-gather.22
  220.6 60.9 all-gather.24
  300.7 27.0 all-gather.32
  329.3 27.2 all-gather.34
  358.1 27.1 all-gather.36
  386.7 44.9 all-gather.26
  433.3 44.9 all-gather.28
  479.6 44.9 all-gather.30
  924.7 119.9 reduce-scatter.12
  1047.3 9.0 reduce-scatter.22
  1059.1 43.8 reduce-scatter.24
  1105.8 43.3 reduce-scatter.26
  1151.8 43.3 reduce-scatter.28
  1197.4 26.0 reduce-scatter.34
  1226.3 26.0 reduce-scatter.30
  1254.6 26.0 reduce-scatter.32
  1283.6 59.9 reduce-scatter.20
  1346.6 59.9 reduce-scatter.14
  1409.5 26.0 reduce-scatter.16
  1438.3 26.0 reduce-scatter.18
where the time goes:
time: 1940 us
  waiting for transfers between devices  885 us (46%)
  blocking collectives  646 us (33%)
  matrix products  184 us (9%)
  local copies, waits for them, and re-layouts  111 us (6%)
  other arithmetic  51.7 us (3%)
  starting transfers between devices  33.7 us (2%)
    psum x1, blocking collectives, per_device(): lax.psum((shard_gain_one, shard_query, shard_key, shard_value, shard_out,...  464 us
    all_to_all x1, blocking collectives, per_device(): lax.all_to_all(grad_sent, 'ctx', split_axis=0, concat_axis=0, tiled=True)  111 us
    all_to_all x1, waiting for transfers between devices, per_device(): lax.all_to_all(grad_rows_exp.reshape(experts, capacity, D), 'ctx', split_...  76.5 us
    reduce_scatter x1, waiting for transfers between devices, per_device(): lax.psum_scatter(grad_weight_query.astype(jnp.bfloat16), 'wa', scatter_di...  63 us
    all_to_all x1, waiting for transfers between devices, per_device(): lax.all_to_all(sent_rows, 'ctx', split_axis=0, concat_axis=0, tiled=True)  57.8 us
    reduce_scatter x1, waiting for transfers between devices, per_device(): lax.psum_scatter(grad_weight_out.astype(jnp.bfloat16), 'wa', scatter_dime...  56.4 us
    psum x1, blocking collectives, per_device(): lax.psum((local_valid, local_error), ('ctx', 'wa'))  55.9 us
    all_gather x1, waiting for transfers between devices, per_device(): lax.all_gather(w_query, 'wa', axis=0, tiled=True)  49.5 us
  transfers between devices with their start and end apart: 27, of which 23 were waited for; matrix products, arithmetic and copies ran while one was open for 10% of the time, Pallas kernels for 0%

commit v1 on v0

--- a/solution.py
+++ b/solution.py
@@ -68,22 +68,6 @@
     grad_gate = grad_hidden * up_activation * sigmoid_gate * (1.0 + gate_act * (1.0 - sigmoid_gate))
     grad_up = grad_hidden * gate_act * sigmoid_gate
     return (grad_gate.astype(jnp.bfloat16), grad_up.astype(jnp.bfloat16))
-
-
-def slot_tables(route_rows, experts, capacity):
-    pair_count = route_rows.shape[0] * route_rows.shape[1]
-    flat_routes = route_rows.reshape(pair_count)
-    one_hot = (flat_routes[:, None] == jnp.arange(experts, dtype=jnp.int32)[None, :]).astype(
-        jnp.int32
-    )
-    slot_rank = jnp.sum((jnp.cumsum(one_hot, axis=0) - 1) * one_hot, axis=1)
-    slot_index = flat_routes * capacity + slot_rank
-    pair_table = (
-        jnp.full((experts * capacity,), pair_count, jnp.int32)
-        .at[slot_index]
-        .set(jnp.arange(pair_count, dtype=jnp.int32))
-    )
-    return (slot_index, pair_table)
 
 
 def visible_pairs(query_pos, query_doc, key_pos, key_doc):
@@ -247,6 +231,23 @@
         return jnp.zeros((key_count, 2 * kv_width), jnp.float32)
 
     return lax.cond(jnp.any(visible), compute, nothing, 0)
+
+
+def pair_swap(value):
+    return lax.ppermute(value, "wa", [(0, 1), (1, 0)])
+
+
+def my_half(value, side, axis):
+    size = value.shape[axis] // 2
+    return lax.dynamic_slice_in_dim(value, side * size, size, axis)
+
+
+def ctx_gather(value):
+    return lax.all_gather(value, "ctx", axis=0, tiled=True)
+
+
+def ctx_scatter_sum(value):
+    return lax.psum_scatter(value, "ctx", scatter_dimension=0, tiled=True)
 
 
 def per_device(
@@ -273,46 +274,36 @@
     ctx_count = lax.axis_size("ctx")
     ctx_rank = lax.axis_index("ctx")
     wa_count = lax.axis_size("wa")
+    side = lax.axis_index("wa")
     local_rows = tokens.shape[1]
     seq_len = local_rows * ctx_count
     key_width = min(seq_len, 1024)
     groups = H // KVH
     kv_width = KVH * HD
     score_scale = HD ** (-0.5)
-    topk_count = routes.shape[2]
     experts = w_router.shape[1]
-    capacity = max(2, 2 * local_rows * topk_count // experts)
-    (
-        gain_one,
-        weight_query,
-        weight_key,
-        weight_value,
-        weight_out,
-        gain_two,
-        weight_router,
-        weight_sgate,
-        weight_sup,
-        weight_sdown,
-    ) = (
-        lax.all_gather(norm1_gain, "wa", axis=0, tiled=True),
-        lax.all_gather(w_query, "wa", axis=0, tiled=True),
-        lax.all_gather(w_key, "wa", axis=0, tiled=True),
-        lax.all_gather(w_value, "wa", axis=0, tiled=True),
-        lax.all_gather(w_out, "wa", axis=0, tiled=True),
-        lax.all_gather(norm2_gain, "wa", axis=0, tiled=True),
-        lax.all_gather(w_router, "wa", axis=0, tiled=True),
-        lax.all_gather(shared_gate, "wa", axis=0, tiled=True),
-        lax.all_gather(shared_up, "wa", axis=0, tiled=True),
-        lax.all_gather(shared_down, "wa", axis=0, tiled=True),
-    )
-    expert_gate_weight, expert_up_weight, expert_down_weight = (
-        lax.all_gather(expert_gate, "wa", axis=1, tiled=True),
-        lax.all_gather(expert_up, "wa", axis=1, tiled=True),
-        lax.all_gather(expert_down, "wa", axis=1, tiled=True),
-    )
+    resident = expert_gate.shape[0]
+
+    def over_wa(value, axis=0):
+        return lax.all_gather(value, "wa", axis=axis, tiled=True)
+
+    gain_one = over_wa(norm1_gain)
+    gain_two = over_wa(norm2_gain)
+    weight_query = over_wa(w_query)
+    weight_key = over_wa(w_key)
+    weight_value = over_wa(w_value)
+    weight_out = over_wa(w_out)
+    weight_router = over_wa(w_router)
+    weight_sgate = over_wa(shared_gate)
+    weight_sup = over_wa(shared_up)
+    weight_sdown = over_wa(shared_down)
+    weight_egate = over_wa(expert_gate, 1)
+    weight_eup = over_wa(expert_up, 1)
+    weight_edown = over_wa(expert_down, 1)
     gain_one_f = gain_one.astype(jnp.float32)
     gain_two_f = gain_two.astype(jnp.float32)
-    resident_experts = expert_gate_weight.shape[0]
+    valid_rows = valid[0].astype(jnp.float32)
+    valid_total = lax.psum(jnp.sum(valid_rows), ("ctx", "wa"))
     doc_first = doc_starts[0]
     own_rows = ctx_rank * local_rows + jnp.arange(local_rows, dtype=jnp.int32)
     query_pos = stored_position(own_rows, local_rows, ctx_count)
@@ -325,10 +316,8 @@
     queries = matmul(normed_one, weight_query).astype(jnp.bfloat16)
     key_rows = matmul(normed_one, weight_key).astype(jnp.bfloat16)
     value_rows = matmul(normed_one, weight_value).astype(jnp.bfloat16)
-    key_all, value_all = (
-        lax.all_gather(key_rows, "ctx", axis=0, tiled=True),
-        lax.all_gather(value_rows, "ctx", axis=0, tiled=True),
-    )
+    key_value_all = ctx_gather(jnp.concatenate([key_rows, value_rows], axis=1))
+    key_all, value_all = key_value_all[:, :kv_width], key_value_all[:, kv_width:]
     query_heads = queries.reshape(local_rows, KVH, groups, HD)
     log_total, attn_f32 = attend_forward(
         query_heads,
@@ -350,102 +339,85 @@
     choose = (route_rows[:, :, None] == jnp.arange(experts, dtype=jnp.int32)[None, None, :]).astype(
         jnp.float32
     )
-    picked_logits = jnp.sum(choose * logits[:, None, :], axis=2)
-    gates = jax.nn.softmax(picked_logits, axis=1)
+    chosen = jnp.sum(choose, axis=1)
+    peak = jnp.max(jnp.where(chosen > 0, logits, MASKED_SCORE), axis=1, keepdims=True)
+    weights = jnp.where(chosen > 0, jnp.exp(jnp.where(chosen > 0, logits, peak) - peak), 0.0)
+    gates = weights / jnp.sum(weights, axis=1, keepdims=True)
+    normed_all = ctx_gather(normed_two)
+    gates_all = lax.all_to_all(
+        gates.reshape(local_rows, ctx_count, resident), "ctx", split_axis=1, concat_axis=0, tiled=True
+    ).reshape(seq_len, resident)
     shared_g_act = matmul(normed_two, weight_sgate)
     shared_u_act = matmul(normed_two, weight_sup)
     shared_hidden = (jax.nn.silu(shared_g_act) * shared_u_act).astype(jnp.bfloat16)
     shared_out = matmul(shared_hidden, weight_sdown)
-    slot_index, pair_table = slot_tables(route_rows, experts, capacity)
-    padded = jnp.concatenate([normed_two, jnp.zeros((1, D), jnp.bfloat16)], axis=0)
-    sent_rows = padded[pair_table // topk_count].reshape(experts, capacity, D)
-    arrived_tokens = lax.all_to_all(
-        sent_rows, "ctx", split_axis=0, concat_axis=0, tiled=True
-    ).reshape(ctx_count, resident_experts, capacity, D)
-    gate_act = jnp.einsum(
-        "rqel,qlo->rqeo", arrived_tokens, expert_gate_weight, preferred_element_type=jnp.float32
-    )
-    up_activation = jnp.einsum(
-        "rqel,qlo->rqeo", arrived_tokens, expert_up_weight, preferred_element_type=jnp.float32
-    )
-    hidden_exp = (jax.nn.silu(gate_act) * up_activation).astype(jnp.bfloat16)
-    expert_out = jnp.einsum(
-        "sacf,afd->sacd", hidden_exp, expert_down_weight, preferred_element_type=jnp.float32
-    ).astype(jnp.bfloat16)
-    returned = lax.all_to_all(
-        expert_out.reshape(experts, capacity, D), "ctx", split_axis=0, concat_axis=0, tiled=True
-    ).reshape(experts * capacity, D)
-    picked = returned[slot_index].reshape(local_rows, topk_count, D).astype(jnp.float32)
-    routed = jnp.einsum("tk,tkd->td", gates, picked)
+    gate_act, up_act, hidden_exp, expert_out = [], [], [], []
+    mixed = 0.0
+    for q in range(resident):
+        gate_act.append(matmul(normed_all, weight_egate[q]))
+        up_act.append(matmul(normed_all, weight_eup[q]))
+        hidden_exp.append((jax.nn.silu(gate_act[q]) * up_act[q]).astype(jnp.bfloat16))
+        expert_out.append(matmul(hidden_exp[q], weight_edown[q]).astype(jnp.bfloat16))
+        mixed = mixed + gates_all[:, q : q + 1] * expert_out[q].astype(jnp.float32)
+    routed = ctx_scatter_sum(mixed.astype(jnp.bfloat16)).astype(jnp.float32)
     produced = hidden_one + shared_out + routed
     output = produced.astype(jnp.bfloat16)[None]
-    valid_rows = valid[0].astype(jnp.float32)
     errors = produced - teacher[0].astype(jnp.float32)
     local_error = jnp.sum(valid_rows[:, None] * errors * errors)
-    local_valid = jnp.sum(valid_rows)
-    valid_total, error_total = lax.psum((local_valid, local_error), ("ctx", "wa"))
-    loss_value = error_total / (valid_total * D)
     tokens_all = wa_count * seq_len
     grad_out = (
         out_grad[0].astype(jnp.float32)
         + 2.0 * tokens_all / valid_total * valid_rows[:, None] * errors
     )
     grad_low = grad_out.astype(jnp.bfloat16)
+    grad_all = ctx_gather(grad_low)
     grad_shared_hidden = contract_cols(grad_low, weight_sdown)
     grad_sgate, grad_sup = silu_grads(grad_shared_hidden, shared_g_act, shared_u_act)
     grad_normed = contract_cols(grad_sgate, weight_sgate) + contract_cols(grad_sup, weight_sup)
-    grad_picked = (gates[:, :, None] * grad_out[:, None, :]).astype(jnp.bfloat16)
-    pair_padded = jnp.concatenate(
-        [grad_picked.reshape(local_rows * topk_count, D), jnp.zeros((1, D), jnp.bfloat16)], axis=0
-    )
-    grad_sent = pair_padded[pair_table].reshape(experts, capacity, D)
-    grad_received = lax.all_to_all(
-        grad_sent, "ctx", split_axis=0, concat_axis=0, tiled=True
-    ).reshape(ctx_count, resident_experts, capacity, D)
-    grad_gates = jnp.einsum("td,tkd->tk", grad_out, picked)
-    grad_selected = gates * (grad_gates - jnp.sum(gates * grad_gates, axis=1, keepdims=True))
-    grad_logits = jnp.einsum("tk,tke->te", grad_selected, choose).astype(jnp.bfloat16)
-    grad_normed = grad_normed + contract_cols(grad_logits, weight_router)
-    grad_hidden_exp = jnp.einsum(
-        "sacd,afd->sacf", grad_received, expert_down_weight, preferred_element_type=jnp.float32
-    )
-    grad_gate_act, gradient_up_activation = silu_grads(grad_hidden_exp, gate_act, up_activation)
-    grad_expert_down = jnp.einsum(
-        "sacf,sacd->afd", hidden_exp, grad_received, preferred_element_type=jnp.float32
-    )
-    grad_expert_gate = jnp.einsum(
-        "sacd,sacf->adf", arrived_tokens, grad_gate_act, preferred_element_type=jnp.float32
-    )
-    grad_expert_up = jnp.einsum(
-        "sacd,sacf->adf", arrived_tokens, gradient_up_activation, preferred_element_type=jnp.float32
-    )
-    grad_rows_exp = (
-        jnp.einsum(
-            "ezrj,zoj->ezro", grad_gate_act, expert_gate_weight, preferred_element_type=jnp.float32
-        )
-        + jnp.einsum(
-            "ezrj,zoj->ezro",
-            gradient_up_activation,
-            expert_up_weight,
-            preferred_element_type=jnp.float32,
-        )
+    gate_dots, egate_grad, eup_grad, edown_grad = [], [], [], []
+    grad_rows = 0.0
+    for q in range(resident):
+        grad_picked = (gates_all[:, q : q + 1] * grad_all.astype(jnp.float32)).astype(jnp.bfloat16)
+        gate_dots.append(
+            jnp.sum(
+                grad_all.astype(jnp.float32) * expert_out[q].astype(jnp.float32),
+                axis=1,
+                keepdims=True,
+            )
+        )
+        grad_hidden = contract_cols(grad_picked, weight_edown[q])
+        grad_gact, grad_uact = silu_grads(grad_hidden, gate_act[q], up_act[q])
+        grad_rows = (
+            grad_rows
+            + contract_cols(grad_gact, weight_egate[q])
+            + contract_cols(grad_uact, weight_eup[q])
+        )
+        egate_grad.append(contract_rows(normed_all, grad_gact))
+        eup_grad.append(contract_rows(normed_all, grad_uact))
+        edown_grad.append(contract_rows(hidden_exp[q], grad_picked))
+    grad_back = ctx_scatter_sum(grad_rows.astype(jnp.bfloat16)).astype(jnp.float32)
+    gate_dot = lax.all_to_all(
+        jnp.concatenate(gate_dots, axis=1).reshape(ctx_count, local_rows, resident),
+        "ctx",
+        split_axis=0,
+        concat_axis=0,
+        tiled=True,
+    )
+    grad_gates = jnp.transpose(gate_dot, (1, 0, 2)).reshape(local_rows, experts)
+    grad_logits = (
+        gates * (grad_gates - jnp.sum(gates * grad_gates, axis=1, keepdims=True))
     ).astype(jnp.bfloat16)
-    grad_back = lax.all_to_all(
-        grad_rows_exp.reshape(experts, capacity, D), "ctx", split_axis=0, concat_axis=0, tiled=True
-    ).reshape(experts * capacity, D)
-    grad_normed = grad_normed + jnp.sum(
-        grad_back[slot_index].reshape(local_rows, topk_count, D).astype(jnp.float32), axis=1
-    )
+    grad_normed = grad_normed + contract_cols(grad_logits, weight_router) + grad_back
+
+    def expert_sum(grads):
+        full = jnp.stack(grads)
+        other = pair_swap(my_half(full, 1 - side, 1).astype(jnp.bfloat16))
+        return my_half(full, side, 1) + other.astype(jnp.float32)
+
     expert_gate_sum, expert_up_sum, expert_down_sum = (
-        lax.psum_scatter(
-            grad_expert_gate.astype(jnp.bfloat16), "wa", scatter_dimension=1, tiled=True
-        ).astype(jnp.float32),
-        lax.psum_scatter(
-            grad_expert_up.astype(jnp.bfloat16), "wa", scatter_dimension=1, tiled=True
-        ).astype(jnp.float32),
-        lax.psum_scatter(
-            grad_expert_down.astype(jnp.bfloat16), "wa", scatter_dimension=1, tiled=True
-        ).astype(jnp.float32),
+        expert_sum(egate_grad),
+        expert_sum(eup_grad),
+        expert_sum(edown_grad),
     )
     grad_hidden_norm, grad_gain_two = norm_backward(
         hidden_one, inverse_two, gain_two_f, grad_normed
@@ -477,7 +449,7 @@
         .reshape(local_rows, H * HD)
         .astype(jnp.bfloat16)
     )
-    sub_rows = math.gcd(local_rows * lax.axis_size("ctx"), key_width)
+    sub_rows = math.gcd(seq_len, key_width)
 
     def one_piece(piece_index):
         piece_first = piece_index * sub_rows
@@ -503,17 +475,12 @@
             score_scale,
         )
 
-    pieces = lax.map(
-        one_piece, jnp.arange(local_rows * lax.axis_size("ctx") // sub_rows, dtype=jnp.int32)
-    )
-    key_value_grad = lax.psum_scatter(
-        pieces.reshape(local_rows * lax.axis_size("ctx"), 2 * kv_width),
-        "ctx",
-        scatter_dimension=0,
-        tiled=True,
-    )
-    grad_key_low = key_value_grad[:, :kv_width].astype(jnp.bfloat16)
-    grad_value_low = key_value_grad[:, kv_width:].astype(jnp.bfloat16)
+    pieces = lax.map(one_piece, jnp.arange(seq_len // sub_rows, dtype=jnp.int32))
+    key_value_grad = ctx_scatter_sum(
+        pieces.reshape(seq_len, 2 * kv_width).astype(jnp.bfloat16)
+    )
+    grad_key_low = key_value_grad[:, :kv_width]
+    grad_value_low = key_value_grad[:, kv_width:]
     grad_normed_one = (
         contract_cols(grad_query_low, weight_query)
         + contract_cols(grad_key_low, weight_key)
@@ -523,96 +490,45 @@
         residual_stream, inverse_one, gain_one_f, grad_normed_one
     )
     grad_input = grad_hidden_one + grad_residual_norm
-    grad_weight_out = contract_rows(attn_low, grad_attn_in)
-    grad_router = contract_rows(normed_two, grad_logits)
-    grad_shared_down = contract_rows(shared_hidden, grad_low)
-    grad_shared_gate = contract_rows(normed_two, grad_sgate)
-    grad_shared_up = contract_rows(normed_two, grad_sup)
-    grad_weight_query = contract_rows(normed_one, grad_query_low)
-    grad_weight_key = contract_rows(normed_one, grad_key_low)
-    grad_weight_value = contract_rows(normed_one, grad_value_low)
-    (
-        shard_gain_one,
-        shard_query,
-        shard_key,
-        shard_value,
-        shard_out,
-        shard_gain_two,
-        shard_router,
-        shard_sgate,
-        shard_sup,
-        shard_sdown,
-    ) = (
-        lax.psum_scatter(
-            grad_gain_one.astype(jnp.bfloat16), "wa", scatter_dimension=0, tiled=True
-        ).astype(jnp.float32),
-        lax.psum_scatter(
-            grad_weight_query.astype(jnp.bfloat16), "wa", scatter_dimension=0, tiled=True
-        ).astype(jnp.float32),
-        lax.psum_scatter(
-            grad_weight_key.astype(jnp.bfloat16), "wa", scatter_dimension=0, tiled=True
-        ).astype(jnp.float32),
-        lax.psum_scatter(
-            grad_weight_value.astype(jnp.bfloat16), "wa", scatter_dimension=0, tiled=True
-        ).astype(jnp.float32),
-        lax.psum_scatter(
-            grad_weight_out.astype(jnp.bfloat16), "wa", scatter_dimension=0, tiled=True
-        ).astype(jnp.float32),
-        lax.psum_scatter(
-            grad_gain_two.astype(jnp.bfloat16), "wa", scatter_dimension=0, tiled=True
-        ).astype(jnp.float32),
-        lax.psum_scatter(
-            grad_router.astype(jnp.bfloat16), "wa", scatter_dimension=0, tiled=True
-        ).astype(jnp.float32),
-        lax.psum_scatter(
-            grad_shared_gate.astype(jnp.bfloat16), "wa", scatter_dimension=0, tiled=True
-        ).astype(jnp.float32),
-        lax.psum_scatter(
-            grad_shared_up.astype(jnp.bfloat16), "wa", scatter_dimension=0, tiled=True
-        ).astype(jnp.float32),
-        lax.psum_scatter(
-            grad_shared_down.astype(jnp.bfloat16), "wa", scatter_dimension=0, tiled=True
-        ).astype(jnp.float32),
-    )
-    (
-        total_gain_one,
-        total_query,
-        total_key,
-        total_value,
-        total_out,
-        total_gain_two,
-        total_router,
-        total_sgate,
-        total_sup,
-        total_sdown,
-    ) = lax.psum(
+
+    def weight_grad(left, *rights):
+        right = rights[0] if len(rights) == 1 else jnp.concatenate(rights, axis=1)
+        other_left = pair_swap(my_half(left, 1 - side, 1))
+        other_right = pair_swap(right)
+        return (
+            contract_rows(my_half(left, side, 1), right) + contract_rows(other_left, other_right)
+        ).astype(jnp.bfloat16)
+
+    summed = lax.psum(
         (
-            shard_gain_one,
-            shard_query,
-            shard_key,
-            shard_value,
-            shard_out,
-            shard_gain_two,
-            shard_router,
-            shard_sgate,
-            shard_sup,
-            shard_sdown,
+            weight_grad(shared_hidden, grad_low),
+            weight_grad(normed_two, grad_sgate, grad_sup, grad_logits),
+            weight_grad(attn_low, grad_attn_in),
+            weight_grad(normed_one, grad_query_low, grad_key_low, grad_value_low),
         ),
         "ctx",
     )
+    total_sdown, total_second, total_out, total_first = [s.astype(jnp.float32) for s in summed]
+    shared_width = grad_sgate.shape[1]
+    vectors = lax.psum(
+        jnp.concatenate([grad_gain_one, grad_gain_two, jnp.full((128,), local_error)]),
+        ("ctx", "wa"),
+    )
+    width = grad_gain_one.shape[0]
+    loss_value = vectors[2 * width] / (valid_total * D)
     return (
         loss_value,
         output,
         grad_input[None],
-        total_gain_one,
-        total_query,
-        total_key,
-        total_value,
+        my_half(vectors[:width], side, 0),
+        total_first[:, : H * HD],
+        total_first[:, H * HD : H * HD + kv_width],
+        total_first[:, H * HD + kv_width :],
         total_out,
-        total_gain_two,
-        total_router,
-        total_sgate,
-        total_sup,
+        my_half(vectors[width : 2 * width], side, 0),
+        total_second[:, 2 * shared_width :],
+        total_second[:, :shared_width],
+        total_second[:, shared_width : 2 * shared_width],
         total_sdown,
         expert_gate_sum,
         expert_up_sum,

time: 1940 us -> 1220 us (0.63)
  blocking collectives: 646 us -> 93.7 us
  waiting for transfers between devices: 885 us -> 747 us
  local copies, waits for them, and re-layouts: 111 us -> 78.6 us
    psum x2, blocking collectives: 520 us -> 83.4 us  [the longest x1 44 us: per_device(): lax.psum(jnp.concatenate([grad_gain_one, grad_gain_two, jnp.full((128,),...]
    reduce_scatter x12 -> x3, waiting for transfers between devices: 430 us -> 142 us  [ctx_scatter_sum(): return lax.psum_scatter(value, 'ctx', scatter_dimension=0, tiled=True)]
    all_to_all x3 -> x2, waiting for transfers between devices: 168 us -> 2.11 us  [the longest x1 2.1 us: per_device(): lax.all_to_all(jnp.concatenate(gate_dots, axis=1).reshape(ctx_count, loca...]
    all_gather x12 -> x13, waiting for transfers between devices: 281 us -> 440 us  [the longest x10 263 us: over_wa(): return lax.all_gather(value, 'wa', axis=axis, tiled=True)]
    all_to_all x1 -> x0, blocking collectives: 111 us -> none  [per_device(): lax.all_to_all(grad_sent, 'ctx', split_axis=0, concat_axis=0, tiled=True)]
    psum x0 -> x1, waiting for transfers between devices: none -> 101 us  [per_device(): lax.psum((weight_grad(shared_hidden, grad_low), weight_grad(normed_two, g...]
    dot_general x11 -> x0, matrix products: 60.8 us -> none  [the longest x1 9.26 us: per_device(): jnp.einsum('rqel,qlo->rqeo', arrived_tokens, expert_up_weight, preferred_...]
    ppermute x0 -> x11, waiting for transfers between devices: none -> 54.9 us  [pair_swap(): return lax.ppermute(value, 'wa', [(0, 1), (1, 0)])]
  transfers between devices with their start and end apart: 27 -> 30, of which waited for: 23 -> 21; matrix products, arithmetic and copies ran while one was open for 10% -> 16% of each run, Pallas kernels for 0% -> 0%
where the time goes in v1:
time: 1220 us; the launch traced here: 1200 us
  waiting for transfers between devices  747 us (61%)
  matrix products  185 us (15%)
  blocking collectives  93.7 us (8%)
  local copies, waits for them, and re-layouts  78.6 us (6%)
  other arithmetic  54.8 us (4%)
  starting transfers between devices  21.4 us (2%)
  between operations  18.3 us (2%)
    all_gather x10, waiting for transfers between devices, over_wa(): return lax.all_gather(value, 'wa', axis=axis, tiled=True)  263 us
    all_gather x3, waiting for transfers between devices, ctx_gather(): return lax.all_gather(value, 'ctx', axis=0, tiled=True)  177 us
    reduce_scatter x3, waiting for transfers between devices, ctx_scatter_sum(): return lax.psum_scatter(value, 'ctx', scatter_dimension=0, tiled=True)  142 us
    psum x1, waiting for transfers between devices, per_device(): lax.psum((weight_grad(shared_hidden, grad_low), weight_grad(normed_two, g...  101 us
    ppermute x11, waiting for transfers between devices, pair_swap(): return lax.ppermute(value, 'wa', [(0, 1), (1, 0)])  54.9 us
    dot_general x11, matrix products, matmul(): return jnp.dot(left, right, preferred_element_type=jnp.float32)  50 us
    psum x1, blocking collectives, per_device(): lax.psum(jnp.concatenate([grad_gain_one, grad_gain_two, jnp.full((128,),...  44 us
    dot_general x11, matrix products, contract_cols(): lax.dot_general(left, right, (((1,), (1,)), ((), ())), preferred_element_...  39.9 us
  transfers between devices with their start and end apart: 30, of which 21 were waited for; matrix products, arithmetic and copies ran while one was open for 16% of the time, Pallas kernels for 0%

profile of v1, /device:TPU:1, one launch (start us, length us, event | category | flops | bytes accessed | tf_op | source)
XLA Modules:
  0.0 1204.1 jit_solution(7369910771000568728)
XLA Ops:
  14.5 24.4 %all-gather.18.cloned.1.call-done = bf16[1536,512]{1,0:T(8,128)(2,1)} async-done(((bf16[768,512]{1,0:T(8,128)(2,1)}), bf16[1536,512]{1,0:T(8,128)(2,1)}) %all-gather.18.cloned.1.call-update) | async-done | bytes 1572880 | tf_op jit(solution)/shard_map/all_gather | solution.py:288
  40.7 27.0 %all-gather.16.cloned.1.call-done = bf16[1536,512]{1,0:T(8,128)(2,1)} async-done(((bf16[768,512]{1,0:T(8,128)(2,1)}), bf16[1536,512]{1,0:T(8,128)(2,1)}) %all-gather.16.cloned.1.call-update) | async-done | bytes 1572880 | tf_op jit(solution)/shard_map/all_gather | solution.py:288
  76.1 55.9 %all-gather.22.cloned.1.call-done = bf16[1536,1536]{1,0:T(8,128)(2,1)} async-done(((bf16[768,1536]{1,0:T(8,128)(2,1)}), bf16[1536,1536]{1,0:T(8,128)(2,1)}) %all-gather.22.cloned.1.call-update) | async-done | bytes 4718608 | tf_op jit(solution)/shard_map/all_gather | solution.py:288
  135.5 50.2 %all-gather.20.cloned.1.call-done = bf16[2048,1024]{1,0:T(8,128)(2,1)} async-done(((bf16[128,1024]{1,0:T(8,128)(2,1)}), bf16[2048,1024]{1,0:T(8,128)(2,1)}) %all-gather.20.cloned.1.call-update) | async-done | bytes 4194320 | tf_op jit(solution)/shard_map/all_gather | solution.py:246
  198.3 18.9 %while.46 = (s32[]{:T(128)}, f32[4,3,128,1]{2,1,0,3:T(4,128)S(1)}, f32[4,3,128,1]{2,1,0,3:T(4,128)S(1)}, f32[4,3,128,128]{3,2,1,0:T(8,128)S(1)}, s32[2048]{0:T(1...) while((s32[]{:T(128)}, f32[4,3,128,1]{2,1,0,3:T(4,128)S(1)}, ...), condition=%wide.region_9.10_spmd.clone, body=%wide.region_3.9_spmd.clone.sunk | while | flops 826679296 | bytes 27780972 | solution.py:138
  217.7 30.2 %all-gather.24.cloned.1.call-done = bf16[1536,1536]{1,0:T(8,128)(2,1)} async-done(((bf16[768,1536]{1,0:T(8,128)(2,1)}), bf16[1536,1536]{1,0:T(8,128)(2,1)}) %all-gather.24.cloned.1.call-update) | async-done | bytes 4718608 | tf_op jit(solution)/shard_map/all_gather | solution.py:288
  276.8 65.2 %all-gather.32.cloned.1.call-done = bf16[2048,1536]{1,0:T(8,128)(2,1)} async-done(((bf16[128,1536]{1,0:T(8,128)(2,1)}), bf16[2048,1536]{1,0:T(8,128)(2,1)}) %all-gather.32.cloned.1.call-update) | async-done | bytes 6291472 | tf_op jit(solution)/shard_map/all_gather | solution.py:246
  350.6 18.3 %all-gather.36.cloned.1.call-done = bf16[1,1536,512]{2,1,0:T(8,128)(2,1)} async-done(((bf16[1,768,512]{2,1,0:T(8,128)(2,1)}), bf16[1,1536,512]{2,1,0:T(8,128)(2,1)}) %all-gather.36.cloned.1.call-update) | async-done | bytes 1572880 | tf_op jit(solution)/shard_map/all_gather | solution.py:288
  379.9 17.7 %all-gather.38.cloned.1.call-done = bf16[1,512,1536]{2,1,0:T(8,128)(2,1)} async-done(((bf16[1,256,1536]{2,1,0:T(8,128)(2,1)}), bf16[1,512,1536]{2,1,0:T(8,128)(2,1)}) %all-gather.38.cloned.1.call-update) | async-done | bytes 1572880 | tf_op jit(solution)/shard_map/all_gather | solution.py:288
  409.5 39.4 %psum.42 = f32[]{:T(128)} all-reduce(f32[]{:T(128)} %convert_reduce_fusion.5), channel_id=1, replica_groups=mesh['ctx'=16,'wa'=2] {'ctx','wa'}, use_global_device_ids=true, to_apply=%region_11.12 | all-reduce | flops 1 | bytes 8 | tf_op jit(solution)/shard_map/psum | solution.py:306
  452.6 38.8 %all-gather.28.cloned.1.call-done = bf16[1536,1024]{1,0:T(8,128)(2,1)} async-done(((bf16[768,1024]{1,0:T(8,128)(2,1)}), bf16[1536,1024]{1,0:T(8,128)(2,1)}) %all-gather.28.cloned.1.call-update) | async-done | bytes 3145744 | tf_op jit(solution)/shard_map/all_gather | solution.py:288
  494.8 43.0 %all-gather.30.cloned.1.call-done = bf16[1024,1536]{1,0:T(8,128)(2,1)} async-done(((bf16[512,1536]{1,0:T(8,128)(2,1)}), bf16[1024,1536]{1,0:T(8,128)(2,1)}) %all-gather.30.cloned.1.call-update) | async-done | bytes 3145744 | tf_op jit(solution)/shard_map/all_gather | solution.py:288
  537.8 88.5 %reduce-scatter.4.cloned.1.call-done = bf16[128,1536]{1,0:T(8,128)(2,1)} async-done(((bf16[2048,1536]{1,0:T(8,128)(2,1)}), bf16[128,1536]{1,0:T(8,128)(2,1)}) %reduce-scatter.4.cloned.1.call-update) | async-done | bytes 393232 | tf_op jit(solution)/shard_map/reduce_scatter | solution.py:250
  630.2 62.1 %all-gather.40.cloned.1.call-done = bf16[2048,1536]{1,0:T(8,128)(2,1)} async-done(((bf16[128,1536]{1,0:T(8,128)(2,1)}), bf16[2048,1536]{1,0:T(8,128)(2,1)}) %all-gather.40.cloned.1.call-update) | async-done | bytes 6291472 | tf_op jit(solution)/shard_map/all_gather | solution.py:246
  743.3 53.2 %reduce-scatter.6.cloned.1.call-done = bf16[128,1536]{1,0:T(8,128)(2,1)} async-done(((bf16[2048,1536]{1,0:T(8,128)(2,1)}), bf16[128,1536]{1,0:T(8,128)(2,1)}) %reduce-scatter.6.cloned.1.call-update) | async-done | bytes 393232 | tf_op jit(solution)/shard_map/reduce_scatter | solution.py:250
  808.0 54.2 %while.48 = (s32[]{:T(128)}, bf16[2,1024,1024]{2,1,0:T(8,128)(2,1)}, s32[2]{0:T(128)}, s32[2048]{0:T(1024)S(1)}, s32[2048]{0:T(1024)S(1)}, /*index=5*/s32[128]{0...) while((s32[]{:T(128)}, ...), condition=%wide.region_30.31_spmd.clone, body=%wide.region_26.30_spmd.clone.sunk | while | flops 1635257856 | bytes 50794888 | solution.py:478
  812.8 16.7 %conditional.11 = (bf16[1,1024,1024]{1,2,0:T(8,128)(2,1)S(1)}) conditional(s32[]{:T(128)} %convert_element_type.381, () %tuple.175, (pred[128,1024]{0,1:T(8,128)(4,1)}, bf16[2048,512]{0,1:T(8,128)(2,1)}, s32[]{:T(128)}, bf16[128,4,3,128]{0,3,2,1:T(8,128)(2,1)S(1)}, f32[4,3,128,1]{2,1,0,3:T(4,128)}, /*index=5*/bf16[2048,512]{0,1:T(8,128)(2,1)}, ...), branch_computations={%region_28.28_spmd, %region_29.29_spmd} | conditional | flops 1634729984 | bytes 33859652 | solution.py:233
  839.9 16.6 %conditional.11 = (bf16[1,1024,1024]{1,2,0:T(8,128)(2,1)S(1)}) conditional(s32[]{:T(128)} %convert_element_type.381, () %tuple.175, (pred[128,1024]{0,1:T(8,128)(4,1)}, bf16[2048,512]{0,1:T(8,128)(2,1)}, s32[]{:T(128)}, bf16[128,4,3,128]{0,3,2,1:T(8,128)(2,1)S(1)}, f32[4,3,128,1]{2,1,0,3:T(4,128)}, /*index=5*/bf16[2048,512]{0,1:T(8,128)(2,1)}, ...), branch_computations={%region_28.28_spmd, %region_29.29_spmd} | conditional | flops 1634729984 | bytes 33859652 | solution.py:233
  876.3 12.7 %collective-permute-done.7 = bf16[128,1536]{1,0:T(8,128)(2,1)} collective-permute-done((bf16[128,1536]{1,0:T(8,128)(2,1)}, bf16[128,1536]{1,0:T(8,128)(2,1)}, u32[]{:S(2)}, u32[]{:S(2)}) %collective-permute-start.7) | collective-permute-done | bytes 393248 | tf_op jit(solution)/shard_map/ppermute | solution.py:237
  910.4 29.1 %while.47 = (s32[]{:T(128)}, f32[128,4,3,128]{0,3,2,1:T(8,128)}, s32[2048]{0:T(1024)S(1)}, s32[2048]{0:T(1024)S(1)}, s32[128]{0:T(128)}, /*index=5*/bf16[2048,51...) while((s32[]{:T(128)}, f32[128,4,3,128]{0,3,2,1:T(8,128)}, ...), condition=%wide.region_25.26_spmd.clone, body=%wide.region_21.25_spmd.clone.sunk | while | flops 1219694080 | bytes 22583116 | solution.py:184
  987.7 12.9 %collective-permute-done.8 = bf16[1,768,512]{2,1,0:T(8,128)(2,1)} collective-permute-done((bf16[1,768,512]{2,1,0:T(8,128)(2,1)S(1)}, bf16[1,768,512]{2,1,0:T(8,128)(2,1)}, u32[]{:S(2)}, u32[]{:S(2)}) %collective-permute-start.8) | collective-permute-done | bytes 786464 | tf_op jit(solution)/shard_map/ppermute | solution.py:237
  1003.7 13.8 %collective-permute-done.10 = bf16[1,256,1536]{2,1,0:T(8,128)(2,1)} collective-permute-done((bf16[1,256,1536]{2,1,0:T(8,128)(2,1)S(1)}, bf16[1,256,1536]{2,1,0:T(8,128)(2,1)}, u32[]{:S(2)}, u32[]{:S(2)}) %collective-permute-start.10) | collective-permute-done | bytes 786464 | tf_op jit(solution)/shard_map/ppermute | solution.py:237
  1024.0 44.0 %psum.43 = f32[3200]{0:T(1024)S(1)} all-reduce(f32[3200]{0:T(1024)S(1)} %pad_maximum_fusion.3), channel_id=1, replica_groups=mesh['ctx'=16,'wa'=2] {'ctx','wa'}, use_global_device_ids=true, to_apply=%region_35.36 | all-reduce | flops 3200 | bytes 25600 | tf_op jit(solution)/shard_map/psum | solution.py:513
  1071.8 101.4 %all-reduce.3.cloned.1.call-done = (bf16[768,2560]{1,0:T(8,128)(2,1)}, bf16[768,2064]{0,1:T(8,128)(2,1)}, bf16[768,1536]{1,0:T(8,128)(2,1)}, bf16[512,1536]{1,0:T(8,128)(2,1)}) async-done(((bf16[768,2560]{1,0:T(8,128)(2,1)}, bf16[768,2064]{0,1:T(8,128)(2,1)}, bf16[768,1536]{1,0:T(8,128)(2,1)}, bf16[512,1536]{1,0:T(8,128)(2,1)}), (bf16[768,2560]{1,0:T(8,128)(2,1)}, bf16[768,2064]{0,1:T(8,128)(2,1)}, ...) | async-done | bytes 11034640 | tf_op jit(solution)/shard_map/psum | solution.py:502
  (418 shorter events, 420.4 us)
Async XLA Ops:
  7.2 31.7 %all-gather.18.cloned.1.call-start = ((), (), s32[]{:S(2)}) async-start(), calls=%async_computation.6 | async-start | bytes 2359296 | tf_op jit(solution)/shard_map/all_gather | solution.py:288
  7.9 59.8 %all-gather.16.cloned.1.call-start = ((), (), s32[]{:S(2)}) async-start(), calls=%async_computation.5 | async-start | bytes 2359296 | tf_op jit(solution)/shard_map/all_gather | solution.py:288
  8.7 123.2 %all-gather.22.cloned.1.call-start = ((), (), s32[]{:S(2)}) async-start(), calls=%async_computation.8 | async-start | bytes 7077888 | tf_op jit(solution)/shard_map/all_gather | solution.py:288
  9.4 176.3 %all-gather.20.cloned.1.call-start = ((), (), s32[]{:S(2)}) async-start(), calls=%async_computation.7 | async-start | bytes 4456448 | tf_op jit(solution)/shard_map/all_gather | solution.py:246
  70.2 177.6 %all-gather.24.cloned.1.call-start = ((), (), s32[]{:S(2)}) async-start(), calls=%async_computation.9 | async-start | bytes 7077888 | tf_op jit(solution)/shard_map/all_gather | solution.py:288
  70.8 205.9 %all-gather.34.cloned.1.call-start = ((), (), s32[]{:S(2)}) async-start(), calls=%async_computation.14 | async-start | bytes 2359296 | tf_op jit(solution)/shard_map/all_gather | solution.py:288
  71.4 270.5 %all-gather.32.cloned.1.call-start = ((), (), s32[]{:S(2)}) async-start(), calls=%async_computation.13 | async-start | bytes 6684672 | tf_op jit(solution)/shard_map/all_gather | solution.py:246
  252.5 116.3 %all-gather.36.cloned.1.call-start = ((), (), s32[]{:S(2)}) async-start(), calls=%async_computation.15 | async-start | bytes 2359296 | tf_op jit(solution)/shard_map/all_gather | solution.py:288
  253.3 144.4 %all-gather.38.cloned.1.call-start = ((), (), s32[]{:S(2)}) async-start(), calls=%async_computation.16 | async-start | bytes 2359296 | tf_op jit(solution)/shard_map/all_gather | solution.py:288
  254.0 196.0 %all-gather.26.cloned.1.call-start = ((), (), s32[]{:S(2)}) async-start(), calls=%async_computation.10 | async-start | bytes 4718592 | tf_op jit(solution)/shard_map/all_gather | solution.py:288
  254.6 236.8 %all-gather.28.cloned.1.call-start = ((), (), s32[]{:S(2)}) async-start(), calls=%async_computation.11 | async-start | bytes 4718592 | tf_op jit(solution)/shard_map/all_gather | solution.py:288
  255.4 282.4 %all-gather.30.cloned.1.call-start = ((), (), s32[]{:S(2)}) async-start(), calls=%async_computation.12 | async-start | bytes 4718592 | tf_op jit(solution)/shard_map/all_gather | solution.py:288
  260.9 136.8 %all-to-all-start = ((f32[128,16,1]{0,2,1:T(1,128)}), f32[128,16,1]{0,2,1:T(1,128)S(1)}, u32[]{:S(2)}, u32[]{:S(2)}) async-start(f32[128,16,1]{0,2,1:T(1,128)} %copy.163), calls=%async_computation | async-start | bytes 16384 | tf_op jit(solution)/shard_map/all_to_all | solution.py:347
  268.4 357.9 %reduce-scatter.4.cloned.1.call-start = ((), (), s32[]{:S(2)}) async-start(), calls=%async_computation.17 | async-start | bytes 6684672 | tf_op jit(solution)/shard_map/reduce_scatter | solution.py:250
  408.2 284.0 %all-gather.40.cloned.1.call-start = ((), (), s32[]{:S(2)}) async-start(), calls=%async_computation.18 | async-start | bytes 6684672 | tf_op jit(solution)/shard_map/all_gather | solution.py:246
  630.0 166.5 %reduce-scatter.6.cloned.1.call-start = ((), (), s32[]{:S(2)}) async-start(), calls=%async_computation.19 | async-start | bytes 6684672 | tf_op jit(solution)/shard_map/reduce_scatter | solution.py:250
  731.5 209.3 %reduce-scatter.8.cloned.1.call-start = ((), (), s32[]{:S(2)}) async-start(), calls=%async_computation.20 | async-start | bytes 4456448 | tf_op jit(solution)/shard_map/reduce_scatter | solution.py:250
  862.3 310.9 %all-reduce.3.cloned.1.call-start = ((), (), s32[]{:S(2)}) async-start(), calls=%async_computation.21 | async-start | bytes 22069248 | tf_op jit(solution)/shard_map/psum | solution.py:502
  863.9 84.1 %collective-permute-start = (bf16[128,768]{1,0:T(8,128)(2,1)}, bf16[128,768]{1,0:T(8,128)(2,1)}, u32[]{:S(2)}, u32[]{:S(2)}) collective-permute-start(bf16[128,768]{1,0:T(8,128)(2,1)} %constant_dynamic-slice_fusion.9), channel_id=1, source_target_pairs={{0,1},{1,0},{2,3},{3,2},{4,5},{5,4},{6,7},{7,6},{8,9},{9,8},{10,11... | collective-permute-start | bytes 589832 | tf_op jit(solution)/shard_map/ppermute | solution.py:237
  866.8 75.3 %collective-permute-start.2 = (bf16[128,768]{0,1:T(8,128)(2,1)}, bf16[128,768]{0,1:T(8,128)(2,1)}, u32[]{:S(2)}, u32[]{:S(2)}) collective-permute-start(bf16[128,768]{0,1:T(8,128)(2,1)} %constant_dynamic-slice_fusion.8), channel_id=1, source_target_pairs={{0,1},{1,0},{2,3},{3,2},{4,5},{5,4},{6,7},{7,6},{8,9},{9,8},{10,11... | collective-permute-start | bytes 589832 | tf_op jit(solution)/shard_map/ppermute | solution.py:237
  876.0 24.3 %collective-permute-start.5 = (bf16[128,2064]{0,1:T(8,128)(2,1)}, bf16[128,2064]{0,1:T(8,128)(2,1)S(1)}, u32[]{:S(2)}, u32[]{:S(2)}) collective-permute-start(bf16[128,2064]{0,1:T(8,128)(2,1)} %copy.176), channel_id=1, source_target_pairs={{0,1},{1,0},{2,3},{3,2},{4,5},{5,4},{6,7},{7,6},{8,9},{9,8},{10,11... | collective-permute-start | bytes 1585160 | tf_op jit(solution)/shard_map/ppermute | solution.py:237
  903.9 38.2 %collective-permute-start.3 = (bf16[128,1536]{1,0:T(8,128)(2,1)S(1)}, bf16[128,1536]{1,0:T(8,128)(2,1)}, u32[]{:S(2)}, u32[]{:S(2)}) collective-permute-start(bf16[128,1536]{1,0:T(8,128)(2,1)S(1)} %copy-done.19), channel_id=1, source_target_pairs={{0,1},{1,0},{2,3},{3,2},{4,5},{5,4},{6,7},{7,6},{8,9},{9,8},{10,11... | collective-permute-start | bytes 1179656 | tf_op jit(solution)/shard_map/ppermute | solution.py:237
  976.5 24.1 %collective-permute-start.8 = (bf16[1,768,512]{2,1,0:T(8,128)(2,1)S(1)}, bf16[1,768,512]{2,1,0:T(8,128)(2,1)}, u32[]{:S(2)}, u32[]{:S(2)}) collective-permute-start(bf16[1,768,512]{2,1,0:T(8,128)(2,1)S(1)} %fusion.81), channel_id=1, source_target_pairs={{0,1},{1,0},{2,3},{3,2},{4,5},{5,4},{6,7},{7,6},{8,9},{9,8},{10,11... | collective-permute-start | bytes 2359304 | tf_op jit(solution)/shard_map/ppermute | solution.py:237
  983.7 33.8 %collective-permute-start.10 = (bf16[1,256,1536]{2,1,0:T(8,128)(2,1)S(1)}, bf16[1,256,1536]{2,1,0:T(8,128)(2,1)}, u32[]{:S(2)}, u32[]{:S(2)}) collective-permute-start(bf16[1,256,1536]{2,1,0:T(8,128)(2,1)S(1)} %fusion.83), channel_id=1, source_target_pairs={{0,1},{1,0},{2,3},{3,2},{4,5},{5,4},{6,7},{7,6},{8,9},{9,8},{10,11... | collective-permute-start | bytes 2359304 | tf_op jit(solution)/shard_map/ppermute | solution.py:237
  (94 other events, 2016.7 us)
Sparse Core Ops, SparseCore 0:
  9.6 29.2 all-gather.17
  40.4 27.2 all-gather.15
  69.2 62.6 all-gather.21
  134.5 51.1 all-gather.19
  187.1 60.7 all-gather.23
  249.2 27.4 all-gather.33
  279.6 62.2 all-gather.31
  343.4 25.3 all-gather.35
  370.4 27.2 all-gather.37
  399.1 45.8 all-gather.25
  446.5 44.9 all-gather.27
  492.8 44.9 all-gather.29
  541.7 84.5 reduce-scatter.3
  630.1 62.1 all-gather.39
  713.7 82.6 reduce-scatter.5
  862.4 70.7 reduce-scatter.7
  960.4 212.8 all-reduce.2

commit v2 on v1

v2 whole, which is shorter than its diff:
```python
import functools

import jax
import jax.numpy as jnp
from jax import lax
from jax.experimental import pallas as pl
from jax.experimental.pallas import tpu as pltpu
from jax.sharding import PartitionSpec as P

H = 12
KVH = 4
HD = 128
EPSILON = 1e-05
MASKED_SCORE = -1e30


def stored_position(stored_rows, local_rows, ctx_count):
    half_rows = local_rows // 2
    owner_rank = stored_rows // local_rows
    within_rows = stored_rows % local_rows
    first_half = owner_rank * half_rows + within_rows
    second_half = (2 * ctx_count - 1 - owner_rank) * half_rows + within_rows - half_rows
    return jnp.where(within_rows < half_rows, first_half, second_half)


def document_of(positions, doc_first):
    return jnp.sum((doc_first[None, :] <= positions[:, None]).astype(jnp.int32), axis=1) - 1


def matmul(left, right):
    return jnp.dot(left, right, preferred_element_type=jnp.float32)


def contract_rows(left, right):
    return lax.dot_general(
        left, right, (((0,), (0,)), ((), ())), preferred_element_type=jnp.float32
    )


def contract_cols(left, right):
    return lax.dot_general(
        left, right, (((1,), (1,)), ((), ())), preferred_element_type=jnp.float32
    )


def norm_forward(values, gain):
    inverse = lax.rsqrt(jnp.mean(values * values, axis=1, keepdims=True) + EPSILON)
    return (inverse, values * inverse * gain)


def norm_backward(values, inverse, gain, grad_normed):
    scaled = grad_normed * gain
    inner_sum = jnp.sum(scaled * values, axis=1, keepdims=True)
    grad_values = (
        inverse * scaled - values * (inverse * inverse * inverse) * inner_sum / values.shape[1]
    )
    grad_gain = jnp.sum(grad_normed * values * inverse, axis=0)
    return (grad_values, grad_gain)


def silu_grads(grad_hidden, gate_act, up_activation):
    sigmoid_gate = jax.nn.sigmoid(gate_act)
    grad_gate = grad_hidden * up_activation * sigmoid_gate * (1.0 + gate_act * (1.0 - sigmoid_gate))
    grad_up = grad_hidden * gate_act * sigmoid_gate
    return (grad_gate.astype(jnp.bfloat16), grad_up.astype(jnp.bfloat16))


def pair_swap(value):
    return lax.ppermute(value, "wa", [(0, 1), (1, 0)])


def my_half(value, side, axis):
    size = value.shape[axis] // 2
    return lax.dynamic_slice_in_dim(value, side * size, size, axis)


def heads_as_rows(value):
    return jnp.concatenate(
        [value[:, h * HD : (h + 1) * HD] for h in range(value.shape[1] // HD)], axis=0
    )


def rows_as_heads(value, rows):
    return jnp.concatenate(
        [value[h * rows : (h + 1) * rows] for h in range(value.shape[0] // rows)], axis=1
    )


def seen(query_ref, key_ref, first, count, groups):
    key_pos, key_doc = key_ref[pl.ds(first, count), 0:1], key_ref[pl.ds(first, count), 1:2]
    query_pos, query_doc = query_ref[0:1, :], query_ref[1:2, :]
    visible = (key_pos <= query_pos) & (key_doc == query_doc)
    return jnp.concatenate([visible.astype(jnp.float32)] * groups, axis=1) > 0.5


def attend_kernel(block, query_ref, key_ref, value_ref, query_place, key_place, out_ref, lse_ref):
    rows = query_ref.shape[0]
    groups = query_ref.shape[1] // HD
    scale = HD ** (-0.5)
    queries = heads_as_rows(query_ref[...])

    def step(index, carry):
        peak, total, mixed = carry
        first = pl.multiple_of(index * block, block)
        scores = contract_cols(key_ref[pl.ds(first, block), :], queries) * scale
        visible = seen(query_place, key_place, first, block, groups)
        scores = jnp.where(visible, scores, MASKED_SCORE)
        new_peak = jnp.maximum(peak, jnp.max(scores, axis=0, keepdims=True))
        shrink = jnp.exp(peak - new_peak)
        weights = jnp.where(visible, jnp.exp(scores - new_peak), 0.0)
        total = total * shrink + jnp.sum(weights, axis=0, keepdims=True)
        part = contract_rows(value_ref[pl.ds(first, block), :], weights.astype(jnp.bfloat16))
        return new_peak, total, mixed * shrink + part

    width = groups * rows
    initial = (
        jnp.full((1, width), MASKED_SCORE, jnp.float32),
        jnp.zeros((1, width), jnp.float32),
        jnp.zeros((HD, width), jnp.float32),
    )
    peak, total, mixed = lax.fori_loop(0, key_ref.shape[0] // block, step, initial)
    out_ref[...] = rows_as_heads((mixed / total).T, rows)
    lse_ref[0] = peak + jnp.log(total)


def attend_grads_kernel(
    block,
    query_ref,
    grad_ref,
    key_ref,
    value_ref,
    lse_ref,
    delta_ref,
    query_place,
    key_place,
    query_grad_ref,
    key_grad_ref,
    value_grad_ref,
):
    rows = query_ref.shape[0]
    groups = query_ref.shape[1] // HD
    scale = HD ** (-0.5)
    queries = heads_as_rows(query_ref[...])
    grads = heads_as_rows(grad_ref[...])
    lse, delta = lse_ref[0], delta_ref[0]

    def step(index, total):
        first = pl.multiple_of(index * block, block)
        here = pl.ds(first, block)
        keys = key_ref[here, :]
        scores = contract_cols(keys, queries) * scale
        visible = seen(query_place, key_place, first, block, groups)
        probs = jnp.where(visible, jnp.exp(jnp.where(visible, scores, MASKED_SCORE) - lse), 0.0)
        grad_probs = contract_cols(value_ref[here, :], grads)
        grad_scores = (probs * (grad_probs - delta)).astype(jnp.bfloat16)
        key_grad_ref[here, :] = (matmul(grad_scores, queries) * scale).astype(jnp.bfloat16)
        value_grad_ref[here, :] = matmul(probs.astype(jnp.bfloat16), grads).astype(jnp.bfloat16)
        return total + contract_rows(keys, grad_scores)

    total = lax.fori_loop(
        0, key_ref.shape[0] // block, step, jnp.zeros((HD, groups * rows), jnp.float32)
    )
    query_grad_ref[...] = rows_as_heads((total * scale).T, rows).astype(jnp.bfloat16)


def attention_specs(rows, seq_len):
    wide = HD * (H // KVH)
    return dict(
        query=pl.BlockSpec((rows, wide), lambda a: (0, a)),
        key=pl.BlockSpec((seq_len, HD), lambda a: (0, a)),
        value=pl.BlockSpec((seq_len, HD), lambda a: (0, KVH + a)),
        row=pl.BlockSpec((1, 1, rows * (H // KVH)), lambda a: (a, 0, 0)),
        query_place=pl.BlockSpec((2, rows), lambda a: (0, 0)),
        key_place=pl.BlockSpec((seq_len, 2), lambda a: (0, 0)),
    )


def attend_forward(queries, key_value_all, query_place, key_place):
    rows, seq_len = queries.shape[0], key_value_all.shape[0]
    s = attention_specs(rows, seq_len)
    return pl.pallas_call(
        functools.partial(attend_kernel, min(seq_len, 1024)),
        grid=(KVH,),
        out_shape=[
            jax.ShapeDtypeStruct((rows, H * HD), jnp.float32),
            jax.ShapeDtypeStruct((KVH, 1, rows * (H // KVH)), jnp.float32),
        ],
        in_specs=[s["query"], s["key"], s["value"], s["query_place"], s["key_place"]],
        out_specs=[s["query"], s["row"]],
        compiler_params=pltpu.CompilerParams(vmem_limit_bytes=48 * 2**20),
        name="attend",
    )(queries, key_value_all, key_value_all, query_place, key_place)


def attend_grads(queries, grads, key_value_all, lse, delta, query_place, key_place):
    rows, seq_len = queries.shape[0], key_value_all.shape[0]
    s = attention_specs(rows, seq_len)
    return pl.pallas_call(
        functools.partial(attend_grads_kernel, min(seq_len, 1024)),
        grid=(KVH,),
        out_shape=[
            jax.ShapeDtypeStruct((rows, H * HD), jnp.bfloat16),
            jax.ShapeDtypeStruct((seq_len, KVH * HD), jnp.bfloat16),
            jax.ShapeDtypeStruct((seq_len, KVH * HD), jnp.bfloat16),
        ],
        in_specs=[
            s["query"],
            s["query"],
            s["key"],
            s["value"],
            s["row"],
            s["row"],
            s["query_place"],
            s["key_place"],
        ],
        out_specs=[s["query"], s["key"], s["key"]],
        compiler_params=pltpu.CompilerParams(vmem_limit_bytes=48 * 2**20),
        name="attend_grads",
    )(queries, grads, key_value_all, key_value_all, lse, delta, query_place, key_place)


MESH = pl.DeviceIdType.MESH
NZ, NX, NK = 4, 2, 2
VM = pl.BlockSpec(memory_space=pltpu.VMEM)
HBM = pl.BlockSpec(memory_space=pl.ANY)


def settings(number):
    return pltpu.CompilerParams(
        collective_id=number, has_side_effects=True, vmem_limit_bytes=40 * 2**20
    )


def slot_of(z, x, k):
    return (z * NX + x) * NK + k


def place():
    c = lax.axis_index("ctx")
    return c, c // (NX * NK), lax.rem(c // NK, NX), lax.rem(c, NK), lax.axis_index("wa")


def greet(z, x, k, w, pair, plane=True):
    barrier = pltpu.get_barrier_semaphore()

    def hello(device):
        pl.semaphore_signal(barrier, inc=1, device_id=device, device_id_type=MESH)

    hello((slot_of(z, x, 1 - k), w))
    count = 1
    if pair:
        hello((slot_of(z, x, k), 1 - w))
        count += 1
    if plane:
        hello((slot_of(z, 1 - x, k), w))
        count += 1

        @pl.when(z > 0)
        def _():
            hello((slot_of(z - 1, x, k), w))

        @pl.when(z < NZ - 1)
        def _():
            hello((slot_of(z + 1, x, k), w))

        count += jnp.where(z > 0, 1, 0) + jnp.where(z < NZ - 1, 1, 0)
    pl.semaphore_wait(barrier, count)


def carry_steps(plan, shards, fulls, sems, x, z, k, w):
    own_sem, pair_send, pair_recv, core_send, core_recv = sems
    partner, sibling = (slot_of(z, x, k), 1 - w), (slot_of(z, x, 1 - k), w)

    def rows_of(i, owner):
        h = shards[i].shape[0]
        if plan[i] == "whole":
            return pl.ds(pl.multiple_of(owner * h, h), h)
        half = h // 2
        return pl.ds(pl.multiple_of(owner * h + k * half, half), half)

    def own(i):
        h = shards[i].shape[0]
        return pltpu.make_async_copy(
            shards[i], fulls[i].at[pl.ds(pl.multiple_of(w * h, h), h)], own_sem.at[i]
        )

    def over_pair(i):
        return pltpu.make_async_remote_copy(
            src_ref=shards[i].at[rows_of(i, 0)] if plan[i] == "core" else shards[i],
            dst_ref=fulls[i] if plan[i] == "swap" else fulls[i].at[rows_of(i, w)],
            send_sem=pair_send.at[i],
            recv_sem=pair_recv.at[i],
            device_id=partner,
            device_id_type=MESH,
        )

    def over_core(i):
        here = fulls[i].at[rows_of(i, 1 - w)]
        return pltpu.make_async_remote_copy(
            src_ref=here,
            dst_ref=here,
            send_sem=core_send.at[i],
            recv_sem=core_recv.at[i],
            device_id=sibling,
            device_id_type=MESH,
        )

    every = range(len(shards))

    def start():
        for i in every:
            over_pair(i).start()
        for i in every:
            if plan[i] != "swap":
                own(i).start()

    def hand_on():
        for i in every:
            over_pair(i).wait_recv()
            if plan[i] == "core":
                over_core(i).start()

    def finish():
        for i in every:
            if plan[i] != "swap":
                own(i).wait()
            over_pair(i).wait_send()
            if plan[i] == "core":
                over_core(i).wait()

    return start, hand_on, finish


def carry_semaphores(count):
    return [pltpu.SemaphoreType.DMA((max(count, 1),)) for _ in range(5)]


def weights_kernel(plan, *refs):
    count = len(plan)
    shards, fulls, sems = refs[:count], refs[count : 2 * count], refs[2 * count :]
    me, z, x, k, w = place()
    greet(z, x, k, w, True, False)
    start, hand_on, finish = carry_steps(plan, shards, fulls, sems, x, z, k, w)
    start()
    hand_on()
    finish()


def carried_out(carry):
    return [
        jax.ShapeDtypeStruct(((1 if kind == "swap" else 2) * v.shape[0], *v.shape[1:]), v.dtype)
        for kind, v in carry
    ]


def wa_gather_kernel(carry, number):
    plan, weights = [kind for kind, _ in carry], [v for _, v in carry]
    count = len(weights)
    return pl.pallas_call(
        functools.partial(weights_kernel, plan),
        out_shape=carried_out(carry),
        in_specs=[VM] * count,
        out_specs=[HBM] * count,
        scratch_shapes=carry_semaphores(count),
        compiler_params=settings(number),
        name=f"weights_{number}",
    )(*weights)


def gather_kernel(count, plan, *refs):
    carried = len(plan)
    ins, shards = refs[:count], refs[count : count + carried]
    refs = refs[count + carried :]
    outs, fulls = refs[:count], refs[count : count + carried]
    send_sem, recv_sem, own_sem, *carry_sems = refs[count + carried :]
    me, z, x, k, w = place()
    greet(z, x, k, w, carried > 0)
    up, down = (slot_of(z + 1, x, k), w), (slot_of(z - 1, x, k), w)
    side, sibling = (slot_of(z, 1 - x, k), w), (slot_of(z, x, 1 - k), w)

    def copies(slot, way, device, first=False):
        for i in range(count):
            yield pltpu.make_async_remote_copy(
                src_ref=ins[i] if first else outs[i].at[slot],
                dst_ref=outs[i].at[slot],
                send_sem=send_sem.at[i, slot, way],
                recv_sem=recv_sem.at[i, slot],
                device_id=device,
                device_id_type=MESH,
            )

    def send(*what):
        for c in copies(*what):
            c.start()

    def sent(*what):
        for c in copies(*what):
            c.wait_send()

    def arrived(slot):
        for c in copies(slot, 0, sibling):
            c.wait_recv()

    def across(d, act, wait):
        for sign in (-1, 1) if d else (0,):
            there = z + sign * d

            @pl.when((there >= 0) & (there < NZ))
            def _():
                slot = slot_of(there, 1 - x, k)
                wait(slot)
                act(slot, 3, sibling)

    def walk(act, wait):
        @pl.when(z < NZ - 1)
        def _():
            act(me, 0, up, True)

        @pl.when(z > 0)
        def _():
            act(me, 1, down, True)

        act(me, 2, side, True)
        act(me, 3, sibling, True)
        for d in range(1, NZ):
            for sign in (-1, 1):
                there = z + sign * d

                @pl.when((there >= 0) & (there < NZ))
                def _():
                    slot = slot_of(there, x, k)
                    wait(slot)
                    if sign < 0 and d < NZ - 1:

                        @pl.when(z < NZ - 1)
                        def _():
                            act(slot, 0, up)

                    if sign > 0 and d < NZ - 1:

                        @pl.when(z > 0)
                        def _():
                            act(slot, 1, down)

                    act(slot, 2, side)
                    act(slot, 3, sibling)

            across(d - 1, act, wait)
        across(NZ - 1, act, wait)

    own = [pltpu.make_async_copy(ins[i], outs[i].at[me], own_sem.at[i]) for i in range(count)]
    start, hand_on, finish = carry_steps(plan, shards, fulls, carry_sems, x, z, k, w)
    start()
    walk(send, arrived)
    for o in own:
        o.start()
    hand_on()
    for other in range(NZ * NX):
        arrived(other * NK + 1 - k)
    walk(sent, lambda slot: None)
    for o in own:
        o.wait()
    finish()


def ctx_gather_kernel(values, carry, number):
    plan, weights = [kind for kind, _ in carry], [v for _, v in carry]
    count, carried = len(values), len(weights)
    n = NZ * NX * NK
    done = pl.pallas_call(
        functools.partial(gather_kernel, count, plan),
        out_shape=[jax.ShapeDtypeStruct((n, *v.shape), v.dtype) for v in values]
        + carried_out(carry),
        in_specs=[VM] * (count + carried),
        out_specs=[HBM] * (count + carried),
        scratch_shapes=[
            pltpu.SemaphoreType.DMA((count, n, 4)),
            pltpu.SemaphoreType.DMA((count, n)),
            pltpu.SemaphoreType.DMA((count,)),
        ]
        + carry_semaphores(carried),
        compiler_params=settings(number),
        name=f"gather_{number}",
    )(*values, *weights)
    return done[:count], done[count:]


def scatter_kernel(count, plan, *refs):
    carried = len(plan)
    ins, shards = refs[:count], refs[count : count + carried]
    refs = refs[count + carried :]
    outs, fulls = refs[:count], refs[count : count + carried]
    scratch = refs[count + carried :]
    from_core, from_side, to_side, from_low, from_high, to_z = (
        scratch[g * count : (g + 1) * count] for g in range(6)
    )
    send_core, recv_core, send_side, recv_side, send_z, recv_low, recv_high, *carry_sems = scratch[
        6 * count :
    ]
    me, z, x, k, w = place()
    greet(z, x, k, w, carried > 0)
    up, down = (slot_of(z + 1, x, k), w), (slot_of(z - 1, x, k), w)
    side, sibling = (slot_of(z, 1 - x, k), w), (slot_of(z, x, 1 - k), w)
    f32 = jnp.float32

    def core_copy(i, zz, xx):
        pair = zz * NX + xx
        return pltpu.make_async_remote_copy(
            src_ref=ins[i].at[slot_of(zz, xx, 1 - k)],
            dst_ref=from_core[i].at[pair],
            send_sem=send_core.at[i, pair],
            recv_sem=recv_core.at[i, pair],
            device_id=sibling,
            device_id_type=MESH,
        )

    def side_copy(i, zz):
        return pltpu.make_async_remote_copy(
            src_ref=to_side[i].at[zz],
            dst_ref=from_side[i].at[zz],
            send_sem=send_side.at[i, zz],
            recv_sem=recv_side.at[i, zz],
            device_id=side,
            device_id_type=MESH,
        )

    def z_copy(i, zz, low):
        return pltpu.make_async_remote_copy(
            src_ref=to_z[i].at[zz],
            dst_ref=(from_low if low else from_high)[i].at[zz],
            send_sem=send_z.at[i, zz],
            recv_sem=(recv_low if low else recv_high).at[i, zz],
            device_id=up if low else down,
            device_id_type=MESH,
        )

    def targets(act):
        for d in range(NZ - 1, -1, -1):
            for sign in (1, -1) if d else (0,):
                there = z + sign * d

                @pl.when((there >= 0) & (there < NZ))
                def _():
                    for i in range(count):
                        act(i, there, sign)

    start, hand_on, finish = carry_steps(plan, shards, fulls, carry_sems, x, z, k, w)
    start()
    targets(lambda i, zz, sign: core_copy(i, zz, 1 - x).start())
    targets(lambda i, zz, sign: core_copy(i, zz, x).start())

    def cross(i, zz, sign):
        core_copy(i, zz, 1 - x).wait_recv()
        mine = ins[i][slot_of(zz, 1 - x, k)].astype(f32)
        total = mine + from_core[i][zz * NX + 1 - x].astype(f32)
        to_side[i][zz] = total.astype(to_side[i].dtype)
        side_copy(i, zz).start()

    targets(cross)

    def along(i, zz, sign):
        core_copy(i, zz, x).wait_recv()
        side_copy(i, zz).wait_recv()
        total = ins[i][slot_of(zz, x, k)].astype(f32) + from_core[i][zz * NX + x].astype(f32)
        total = total + from_side[i][zz].astype(f32)
        if sign == 0:
            outs[i][...] = total

            @pl.when(z > 0)
            def _():
                z_copy(i, zz, True).wait_recv()
                outs[i][...] += from_low[i][zz].astype(f32)

            @pl.when(z < NZ - 1)
            def _():
                z_copy(i, zz, False).wait_recv()
                outs[i][...] += from_high[i][zz].astype(f32)

            return
        low = sign > 0
        came = from_low if low else from_high
        first = (z == 0) if low else (z == NZ - 1)

        @pl.when(first)
        def _():
            to_z[i][zz] = total.astype(to_z[i].dtype)

        @pl.when(jnp.logical_not(first))
        def _():
            z_copy(i, zz, low).wait_recv()
            to_z[i][zz] = (total + came[i][zz].astype(f32)).astype(to_z[i].dtype)

        z_copy(i, zz, low).start()

    targets(along)
    hand_on()

    def settle(i, zz, sign):
        core_copy(i, zz, 1 - x).wait_send()
        core_copy(i, zz, x).wait_send()
        side_copy(i, zz).wait_send()
        if sign:
            z_copy(i, zz, sign > 0).wait_send()

    targets(settle)
    finish()


def ctx_scatter_kernel(values, carry, number):
    plan, weights = [kind for kind, _ in carry], [v for _, v in carry]
    count, carried = len(values), len(weights)
    dma = pltpu.SemaphoreType.DMA
    scratch = []
    for lead in (NZ * NX, NZ, NZ, NZ, NZ, NZ):
        scratch += [pltpu.VMEM((lead, *v.shape[1:]), v.dtype) for v in values]
    done = pl.pallas_call(
        functools.partial(scatter_kernel, count, plan),
        out_shape=[jax.ShapeDtypeStruct(v.shape[1:], jnp.float32) for v in values]
        + carried_out(carry),
        in_specs=[VM] * (count + carried),
        out_specs=[VM] * count + [HBM] * carried,
        scratch_shapes=scratch
        + [dma((count, NZ * NX)), dma((count, NZ * NX))]
        + [dma((count, NZ)) for _ in range(5)]
        + carry_semaphores(carried),
        compiler_params=settings(number),
        name=f"scatter_{number}",
    )(*values, *weights)
    return done[:count], done[count:]


def planned():
    return lax.axis_size("ctx") == NZ * NX * NK and lax.axis_size("wa") == 2


def wa_gather(carry, number):
    if planned() and carry:
        return wa_gather_kernel(carry, number)
    return [
        pair_swap(v) if kind == "swap" else lax.all_gather(v, "wa", axis=0, tiled=True)
        for kind, v in carry
    ]


def ctx_gather(values, carry, number):
    if planned():
        return ctx_gather_kernel(values, carry, number)
    return [lax.all_gather(v, "ctx", axis=0) for v in values], wa_gather(carry, number)


def ctx_scatter_sum(values, carry, number):
    if planned():
        return ctx_scatter_kernel(values, carry, number)
    summed = [lax.psum_scatter(v, "ctx", scatter_dimension=0).astype(jnp.float32) for v in values]
    return summed, wa_gather(carry, number)


def per_device(
    tokens,
    doc_starts,
    routes,
    valid,
    teacher,
    out_grad,
    norm1_gain,
    w_query,
    w_key,
    w_value,
    w_out,
    norm2_gain,
    w_router,
    shared_gate,
    shared_up,
    shared_down,
    expert_gate,
    expert_up,
    expert_down,
):
    ctx_count = lax.axis_size("ctx")
    ctx_rank = lax.axis_index("ctx")
    wa_count = lax.axis_size("wa")
    side = lax.axis_index("wa")
    local_rows = tokens.shape[1]
    seq_len = local_rows * ctx_count
    groups = H // KVH
    kv_width = KVH * HD
    experts = w_router.shape[1]
    width = tokens.shape[2]
    lanes = 128
    hidden = expert_gate.shape[2]
    shared_half = shared_down.shape[0]
    run = shared_half // ctx_count
    low = jnp.bfloat16

    gain_rows = width // wa_count // lanes
    valid_rows = valid[0].astype(jnp.float32)
    small = jnp.zeros((16, lanes), jnp.float32)
    small = small.at[:gain_rows].set(norm1_gain.astype(jnp.float32).reshape(gain_rows, lanes))
    small = small.at[8 : 8 + gain_rows].set(
        norm2_gain.astype(jnp.float32).reshape(gain_rows, lanes)
    )
    weight_query, weight_key, weight_value, small_all, valid_there = wa_gather(
        [
            ("core", w_query),
            ("core", w_key),
            ("core", w_value),
            ("core", small),
            ("swap", jnp.broadcast_to(valid_rows, (8, lanes))),
        ],
        1,
    )
    small_all = small_all.reshape(wa_count, 16, lanes)
    gain_one = small_all[:, :gain_rows].reshape(width)
    gain_two = small_all[:, 8 : 8 + gain_rows].reshape(width)
    valid_here = jnp.sum(valid_rows) + jnp.sum(valid_there[0])

    doc_first = doc_starts[0]
    own_rows = ctx_rank * local_rows + jnp.arange(local_rows, dtype=jnp.int32)
    query_pos = stored_position(own_rows, local_rows, ctx_count)
    query_place = jnp.stack([query_pos, document_of(query_pos, doc_first)])
    key_pos = stored_position(jnp.arange(seq_len, dtype=jnp.int32), local_rows, ctx_count)
    key_place = jnp.stack([key_pos, document_of(key_pos, doc_first)], axis=1)

    residual = tokens[0].astype(jnp.float32)
    inverse_one, normed = norm_forward(residual, gain_one)
    normed_one = normed.astype(low)
    queries = matmul(normed_one, weight_query).astype(low)
    key_rows = matmul(normed_one, weight_key).astype(low)
    value_rows = matmul(normed_one, weight_value).astype(low)

    def shared_columns(weight):
        return [
            lax.dynamic_slice_in_dim(weight, half * shared_half + ctx_rank * run, run, 1)
            for half in range(wa_count)
        ]

    wide_in = jnp.concatenate(
        [expert_gate[0], expert_up[0], *shared_columns(shared_gate), *shared_columns(shared_up)],
        axis=1,
    )
    down_rows = lax.dynamic_slice_in_dim(shared_down, ctx_rank * run, run, 0)
    (key_value_all, valid_all), (weight_out, router_t, weight_down, weight_sdown) = ctx_gather(
        [jnp.concatenate([key_rows, value_rows], axis=1), jnp.full((8, lanes), valid_here)],
        [
            ("core", w_out),
            ("core", w_router.astype(jnp.float32).T),
            ("whole", expert_down[0]),
            ("whole", down_rows),
        ],
        2,
    )
    key_value_all = key_value_all.reshape(seq_len, 2 * kv_width)
    valid_total = jnp.sum(valid_all[:, 0, 0])
    router_t = router_t.reshape(wa_count, experts, width // wa_count)
    weight_router = jnp.transpose(router_t, (0, 2, 1)).reshape(width, experts).astype(low)
    attn, lse = attend_forward(queries, key_value_all, query_place, key_place)
    attn_low = attn.astype(low)
    hidden_one = residual + matmul(attn_low, weight_out)
    inverse_two, normed = norm_forward(hidden_one, gain_two)
    normed_two = normed.astype(low)

    logits = matmul(normed_two, weight_router)
    choose = routes[0][:, :, None] == jnp.arange(experts, dtype=jnp.int32)[None, None, :]
    chosen = jnp.any(choose, axis=1)
    peak = jnp.max(jnp.where(chosen, logits, MASKED_SCORE), axis=1, keepdims=True)
    weights = jnp.where(chosen, jnp.exp(jnp.where(chosen, logits, peak) - peak), 0.0)
    gates = weights / jnp.sum(weights, axis=1, keepdims=True)

    (normed_all, gates_all), (weight_in,) = ctx_gather(
        [normed_two, gates.T], [("whole", wide_in)], 3
    )
    normed_all = normed_all.reshape(seq_len, width)
    gate = lax.dynamic_slice_in_dim(gates_all, ctx_rank, 1, 1).reshape(seq_len, 1)
    acts = matmul(normed_all, weight_in)
    gate_act, up_act = acts[:, :hidden], acts[:, hidden : 2 * hidden]
    shared_gact = acts[:, 2 * hidden : 2 * hidden + 2 * run]
    shared_uact = acts[:, 2 * hidden + 2 * run :]
    hidden_exp = (jax.nn.silu(gate_act) * up_act).astype(low)
    shared_hidden = (jax.nn.silu(shared_gact) * shared_uact).astype(low)
    expert_out = matmul(hidden_exp, weight_down).astype(low)
    mixed = gate * expert_out.astype(jnp.float32) + matmul(shared_hidden, weight_sdown)
    (routed,), _ = ctx_scatter_sum(
        [mixed.astype(low).reshape(ctx_count, local_rows, width)], [], 4
    )
    produced = hidden_one + routed
    output = produced.astype(low)[None]

    errors = produced - teacher[0].astype(jnp.float32)
    local_error = jnp.sum(valid_rows[:, None] * errors * errors)
    tokens_all = wa_count * seq_len
    grad_out = (
        out_grad[0].astype(jnp.float32)
        + 2.0 * tokens_all / valid_total * valid_rows[:, None] * errors
    )
    (grad_all,), _ = ctx_gather([grad_out.astype(low)], [], 5)
    grad_all = grad_all.reshape(seq_len, width)

    grad_wide = grad_all.astype(jnp.float32)
    grad_picked = (gate * grad_wide).astype(low)
    gate_dot = jnp.sum(grad_wide * expert_out.astype(jnp.float32), axis=1)
    grad_acts = jnp.concatenate(
        [
            *silu_grads(contract_cols(grad_picked, weight_down), gate_act, up_act),
            *silu_grads(contract_cols(grad_all, weight_sdown), shared_gact, shared_uact),
        ],
        axis=1,
    )
    grad_rows = contract_cols(grad_acts, weight_in)
    small = jnp.full((ctx_count, experts + 8, local_rows), local_error)
    small = small.at[:, :experts].set(0.0)
    small = lax.dynamic_update_slice(
        small, gate_dot.reshape(ctx_count, 1, local_rows), (0, ctx_rank, 0)
    )
    (grad_back, small), (attn_there, normed_one_there, normed_two_there) = ctx_scatter_sum(
        [grad_rows.astype(low).reshape(ctx_count, local_rows, width), small],
        [
            ("swap", my_half(attn_low, 1 - side, 1)),
            ("swap", my_half(normed_one, 1 - side, 1)),
            ("swap", my_half(normed_two, 1 - side, 1)),
        ],
        6,
    )
    grad_gates = small[:experts].T
    error_total = small[experts, 0]
    grad_logits = (
        gates * (grad_gates - jnp.sum(gates * grad_gates, axis=1, keepdims=True))
    ).astype(low)
    grad_normed = grad_back + contract_cols(grad_logits, weight_router)

    in_grad = contract_rows(normed_all, grad_acts)
    down_grad = contract_rows(hidden_exp, grad_picked)
    sdown_grad = contract_rows(shared_hidden, grad_all)

    def for_pair(full):
        return ("swap", my_half(full, 1 - side, 0).astype(low))

    def with_pair(full, other):
        return my_half(full, side, 0) + other.astype(jnp.float32)

    grad_hidden_norm, grad_gain_two = norm_backward(hidden_one, inverse_two, gain_two, grad_normed)
    grad_hidden_one = grad_out + grad_hidden_norm
    grad_attn_in = grad_hidden_one.astype(low)
    grad_heads = contract_cols(grad_attn_in, weight_out).astype(low)
    delta = jnp.einsum(
        "tagd,tagd->agt",
        grad_heads.astype(jnp.float32).reshape(local_rows, KVH, groups, HD),
        attn.reshape(local_rows, KVH, groups, HD),
    ).reshape(KVH, 1, groups * local_rows)
    grad_query, grad_keys, grad_values = attend_grads(
        queries, grad_heads, key_value_all, lse, delta, query_place, key_place
    )
    def for_all(vector):
        flat = jnp.zeros((16 * lanes,), jnp.float32).at[: vector.shape[0]].set(vector)
        return jnp.broadcast_to(flat.reshape(16, lanes), (ctx_count, 16, lanes))

    def from_all(summed, size):
        return summed.reshape(16 * lanes)[:size]

    def by_slot(value):
        return value.reshape(ctx_count, value.shape[0] // ctx_count, value.shape[1])

    half_width = width // wa_count
    (grad_key, grad_value, small), (
        da_there,
        logits_there,
        query_there,
        error_there,
        in_there,
        sdown_there,
    ) = ctx_scatter_sum(
        [
            grad_keys.reshape(ctx_count, local_rows, kv_width),
            grad_values.reshape(ctx_count, local_rows, kv_width),
            for_all(grad_gain_two),
        ],
        [
            ("swap", grad_attn_in),
            ("swap", grad_logits),
            ("swap", grad_query),
            ("swap", jnp.full((8, lanes), error_total)),
            for_pair(in_grad[:, 2 * hidden :]),
            for_pair(sdown_grad),
        ],
        7,
    )
    error_total = error_total + error_there[0, 0]
    key_value_low = jnp.concatenate([grad_key, grad_value], axis=1).astype(low)
    gain_two_sum = from_all(small, width)

    def weight_grad(mine, right, theirs, right_there):
        mine = my_half(mine, side, 1)
        return (contract_rows(mine, right) + contract_rows(theirs, right_there)).astype(low)

    out_part = weight_grad(attn_low, grad_attn_in, attn_there, da_there)
    router_part = contract_rows(grad_logits, my_half(normed_two, side, 1)) + contract_rows(
        logits_there, normed_two_there
    )
    shared_part = with_pair(in_grad[:, 2 * hidden :], in_there).astype(low)
    sdown_part = with_pair(sdown_grad, sdown_there).astype(low)
    rows_two = jnp.zeros((16, lanes), jnp.float32)
    rows_two = rows_two.at[: half_width // lanes].set(
        my_half(gain_two_sum, 1 - side, 0).reshape(-1, lanes)
    )
    router_rows = router_part.reshape(experts, half_width // lanes, lanes)
    router_rows = jnp.pad(router_rows, ((0, 0), (0, 8 - half_width // lanes), (0, 0)))
    (out_sum, router_sum), (kv_there, rows_there, down_there) = ctx_scatter_sum(
        [by_slot(out_part), router_rows],
        [("swap", key_value_low), ("swap", rows_two), for_pair(down_grad)],
        8,
    )
    total_gain_two = my_half(gain_two_sum, side, 0) + rows_there.reshape(-1)[:half_width]

    grad_normed_one = (
        contract_cols(grad_query, weight_query)
        + contract_cols(key_value_low[:, :kv_width], weight_key)
        + contract_cols(key_value_low[:, kv_width:], weight_value)
    )
    grad_residual_norm, grad_gain_one = norm_backward(
        residual, inverse_one, gain_one, grad_normed_one
    )
    grad_input = grad_hidden_one + grad_residual_norm
    (query_sum, kv_sum, small), (in_there,) = ctx_scatter_sum(
        [
            by_slot(weight_grad(normed_one, grad_query, normed_one_there, query_there)),
            by_slot(weight_grad(normed_one, key_value_low, normed_one_there, kv_there)),
            for_all(grad_gain_one),
        ],
        [for_pair(in_grad[:, : 2 * hidden])],
        9,
    )
    gain_one_sum = from_all(small, width)
    rows_one = jnp.zeros((16, lanes), jnp.float32)
    rows_one = rows_one.at[: half_width // lanes].set(
        my_half(gain_one_sum, 1 - side, 0).reshape(-1, lanes)
    )
    (total_query, total_kv, total_out, router_sum, shared_parts, sdown_parts), (rows_there,) = (
        ctx_gather(
            [
                query_sum.astype(low),
                kv_sum.astype(low),
                out_sum.astype(low),
                router_sum,
                shared_part,
                sdown_part,
            ],
            [("swap", rows_one)],
            10,
        )
    )
    total_gain_one = my_half(gain_one_sum, side, 0) + rows_there.reshape(-1)[:half_width]
    total_query = total_query.reshape(half_width, width).astype(jnp.float32)
    total_kv = total_kv.reshape(half_width, 2 * kv_width).astype(jnp.float32)
    total_out = total_out.reshape(half_width, width).astype(jnp.float32)
    router_sum = router_sum[:, : half_width // lanes].reshape(experts, half_width)
    shared_parts = shared_parts.reshape(ctx_count, half_width, 2, wa_count, run)
    shared_parts = jnp.transpose(shared_parts, (2, 1, 3, 0, 4)).astype(jnp.float32)
    shared_parts = shared_parts.reshape(2, half_width, wa_count * shared_half)
    in_grad = with_pair(in_grad[:, : 2 * hidden], in_there)
    down_grad = with_pair(down_grad, down_there)
    return (
        error_total / (valid_total * width),
        output,
        grad_input[None],
        total_gain_one,
        total_query,
        total_kv[:, :kv_width],
        total_kv[:, kv_width:],
        total_out,
        total_gain_two,
        router_sum.T,
        shared_parts[0],
        shared_parts[1],
        sdown_parts.reshape(shared_half, width).astype(jnp.float32),
        in_grad[None, :, :hidden],
        in_grad[None, :, hidden:],
        down_grad[None],
    )


def solution(mesh):
    return jax.shard_map(
        per_device,
        mesh=mesh,
        in_specs=(
            P("wa", "ctx", None),
            P("wa", None),
            P("wa", "ctx", None),
            P("wa", "ctx"),
            P("wa", "ctx", None),
            P("wa", "ctx", None),
            P("wa"),
            P("wa", None),
            P("wa", None),
            P("wa", None),
            P("wa", None),
            P("wa"),
            P("wa", None),
            P("wa", None),
            P("wa", None),
            P("wa", None),
            P("ctx", "wa", None),
            P("ctx", "wa", None),
            P("ctx", "wa", None),
        ),
        out_specs=(
            P(),
            P("wa", "ctx", None),
            P("wa", "ctx", None),
            P("wa"),
            P("wa", None),
            P("wa", None),
            P("wa", None),
            P("wa", None),
            P("wa"),
            P("wa", None),
            P("wa", None),
            P("wa", None),
            P("wa", None),
            P("ctx", "wa", None),
            P("ctx", "wa", None),
            P("ctx", "wa", None),
        ),
        check_vma=False,
    )
```

time: 1220 us -> 677 us (0.55)
  waiting for transfers between devices: 747 us -> 0 us
  Pallas kernels: 0 us -> 458 us
  matrix products: 185 us -> 83.7 us
  blocking collectives: 93.7 us -> 0 us
  starting transfers between devices: 21.4 us -> 0 us
  other arithmetic: 54.8 us -> 36.3 us
    pallas_call x0 -> x12, Pallas kernels: none -> 458 us  [the longest x4 204 us: ctx_gather_kernel(): pl.pallas_call(functools.partial(gather_kernel, count, plan), out_shape=[...]
    all_gather x13 -> x0, waiting for transfers between devices: 440 us -> none  [the longest x10 263 us: over_wa(): return lax.all_gather(value, 'wa', axis=axis, tiled=True)]
    reduce_scatter x3 -> x0, waiting for transfers between devices: 142 us -> none  [ctx_scatter_sum(): return lax.psum_scatter(value, 'ctx', scatter_dimension=0, tiled=True)]
    psum x1 -> x0, waiting for transfers between devices: 101 us -> none  [per_device(): lax.psum((weight_grad(shared_hidden, grad_low), weight_grad(normed_two, g...]
    psum x2 -> x0, blocking collectives: 83.4 us -> none  [the longest x1 44 us: per_device(): lax.psum(jnp.concatenate([grad_gain_one, grad_gain_two, jnp.full((128,),...]
    dot_general x14 -> x0, matrix products: 56.2 us -> none  [the longest x6 17.4 us: block_scores(): jnp.einsum('tagd,sad->agts', query_heads, key_part, preferred_element_typ...]
    ppermute x11 -> x0, waiting for transfers between devices: 54.9 us -> none  [pair_swap(): return lax.ppermute(value, 'wa', [(0, 1), (1, 0)])]
    dot_general x11 -> x8, matrix products: 50 us -> 22 us  [matmul(): return jnp.dot(left, right, preferred_element_type=jnp.float32)]
  transfers between devices with their start and end apart: 30 -> 0, of which waited for: 21 -> 0; matrix products, arithmetic and copies ran while one was open for 16% -> 0% of each run, Pallas kernels for 0% -> 0%
where the time goes in v2:
time: 677 us; the launch traced here: 670 us
  Pallas kernels  458 us (68%)
  local copies, waits for them, and re-layouts  84.1 us (12%)
  matrix products  83.7 us (12%)
  other arithmetic  36.3 us (5%)
  between operations  7.88 us (1%)
    pallas_call x4, Pallas kernels, ctx_gather_kernel(): pl.pallas_call(functools.partial(gather_kernel, count, plan), out_shape=[...  204 us
    pallas_call x5, Pallas kernels, ctx_scatter_kernel(): pl.pallas_call(functools.partial(scatter_kernel, count, plan), out_shape=...  180 us
    pallas_call x1, Pallas kernels, wa_gather_kernel(): pl.pallas_call(functools.partial(weights_kernel, plan), out_shape=carried...  48 us
    unnamed x223, local copies, waits for them, and re-layouts  37.2 us
    dot_general x8, matrix products, contract_cols(): lax.dot_general(left, right, (((1,), (1,)), ((), ())), preferred_element_...  35.6 us
    dot_general x11, matrix products, contract_rows(): lax.dot_general(left, right, (((0,), (0,)), ((), ())), preferred_element_...  26.1 us
    dot_general x8, matrix products, matmul(): return jnp.dot(left, right, preferred_element_type=jnp.float32)  22 us
    pallas_call x1, Pallas kernels, attend_grads(): pl.pallas_call(functools.partial(attend_grads_kernel, min(seq_len, 1024))...  14.9 us

profile of v2, /device:TPU:1, one launch (start us, length us, event | category | flops | bytes accessed | tf_op | source)
XLA Modules:
  0.0 670.3 jit_solution(8006612600009302183)
XLA Ops:
  11.2 3.9 concatenate.28.refs_2_
  19.4 48.0 %weights_1.1 = (bf16[1536,1536]{1,0:T(8,128)(2,1)S(1)}, bf16[1536,512]{1,0:T(8,128)(2,1)S(1)}, bf16[1536,512]{1,0:T(8,128)(2,1)S(1)}, f32[32,128]{1,0:T(8,128)S(1)}, f32[8,128]{1,0:T(8,128)S(1)}) custom-call(bf16[768,1536]{1,0:T(8,128)(2,1)S(1)} %copy-done.19, bf16[768,512]{1,0:T(8,128)(2,1)S(1)} %copy-done.23, bf16[768,512]{1,0:T(8,128)(2,1)S(1)} %copy-done.24, ...), custom_call_target="tpu_custom_call" | custom-call | tf_op jit(solution)/shard_map/weights_1/pallas_call | solution.py:359
  77.9 49.3 %gather_2.1 = (bf16[16,128,1024]{2,1,0:T(8,128)(2,1)S(1)}, f32[16,8,128]{2,1,0:T(8,128)S(1)}, bf16[1536,1536]{1,0:T(8,128)(2,1)S(1)}, f32[32,768]{1,0:T(8,128)S(...) custom-call(bf16[128,1024]{1,0:T(8,128)(2,1)S(1)} %pad_maximum_fusion.3.refs_0_, ...), custom_call_target="tpu_custom_call" | custom-call | tf_op jit(solution)/shard_map/gather_2/pallas_call | solution.py:470
  136.7 11.2 %attend.1 = (f32[128,1536]{1,0:T(8,128)S(1)}, f32[4,1,384]{2,1,0:T(1,128)S(1)}) custom-call(bf16[128,1536]{1,0:T(8,128)(2,1)S(1)} %convolution_convert_fusion.3.query_ref, bf16[2048,1024]{1,0:T(8,128)(2,1)} %bitcast.194, bf16[2048,1024]{1,0:T(8,128)(2,1)} %bitcast.195, s32[2,128]{1,0:T(2,128)S(1)} %pad_add_fusion.1.query_place, s32[2048,2]{1,0:T(8,128)S(1)} %copy.79.key_place), custom_call_target="tpu_custom_call" | custom-call | tf_op jit(solution)/shard_map/attend/pallas_call | solution.py:181
  155.6 43.4 %gather_3.1 = (bf16[16,128,1536]{2,1,0:T(8,128)(2,1)S(1)}, f32[16,16,128]{2,1,0:T(8,128)S(1)}, bf16[1536,1152]{1,0:T(8,128)(2,1)S(1)}) custom-call(bf16[128,1536]{1,0:T(8,128)(2,1)S(1)} %multiply_convert_fusion.3.refs_0_, f32[16,128]{1,0:T(8,128)S(1)} %fusion.55.refs_1_, bf16[768,1152]{1,0:T(8,128)(2,1)S(1)} %copy-done.8), custom_call_target="tpu_custom_call" | custom-call | tf_op jit(solution)/shard_map/gather_3/pallas_call | solution.py:470
  199.1 8.2 %fusion.67 = f32[2048,1152]{0,1:T(8,128)S(1)} fusion(bf16[2048,1536]{1,0:T(8,128)(2,1)S(1)} %bitcast.214, bf16[1536,1152]{1,0:T(8,128)(2,1)S(1)} %get-tuple-element.161), kind=kOutput, calls=%fused_computation.188 | convolution fusion | flops 7247757312 | bytes 19267584 | tf_op jit(solution)/shard_map/dot_general | solution.py:31
  212.3 3.9 convolution_convert_fusion.1
  219.5 44.4 %scatter_4.1 = f32[128,1536]{1,0:T(8,128)S(1)} custom-call(bf16[16,128,1536]{2,1,0:T(8,128)(2,1)S(1)} %bitcast.207), custom_call_target="tpu_custom_call" | custom-call | tf_op jit(solution)/shard_map/scatter_4/pallas_call | solution.py:616
  266.4 40.0 %gather_5.1 = bf16[16,128,1536]{2,1,0:T(8,128)(2,1)S(1)} custom-call(bf16[128,1536]{1,0:T(8,128)(2,1)S(1)} %get-tuple-element.263.refs_0_), custom_call_target="tpu_custom_call" | custom-call | tf_op jit(solution)/shard_map/gather_5/pallas_call | solution.py:470
  309.1 5.2 multiply_convert_fusion.5
  317.0 9.1 %multiply_convert_fusion.1 = (bf16[2048,512]{0,1:T(8,128)(2,1)}, bf16[2048,512]{0,1:T(8,128)(2,1)}) fusion(f32[2048,1152]{0,1:T(8,128)} %copy-done.63, bf16[512,1536]{1,0:T(8,128)(2,1)S(1)} %copy-done.53, bf16[2048,1536]{1,0:T(8,128)(2,1)S(1)} %bitcast.200, f32[2048]{0:T(1024)S(1)} %bitcast.237), kind=kOutput, calls=%fused_computation.13 | convolution fusion | flops 3244294144 | bytes 20455424 | tf_op jit(solution)/shard_map/dot_general | solution.py:41
  332.4 13.9 %fusion.8 = f32[1536,1152]{1,0:T(8,128)} fusion(bf16[2048,1536]{1,0:T(8,128)(2,1)S(1)} %bitcast.217, bf16[2048,64]{0,1:T(8,128)(2,1)S(1)} %get-tuple-element.255, bf16[2048,64]{0,1:T(8,128)(2,1)S(1)} %get-tuple-element.254, bf16[2048,512]{0,1:T(8,128)(2,1)} %get-tuple-element.253, bf16[2048,512]{0,1:T(8,128)(2,1)} %get-tuple-element.252), kind=kOutput, calls=%fused_computation.44 | convolution fusion | flops 7266631680 | bytes 18087936 | tf_op jit(solution)/shard_map/dot_general | solution.py:35
  346.3 10.3 %convolution_convert_fusion = bf16[2048,1536]{1,0:T(8,128)(2,1)S(1)} fusion(bf16[1536,1152]{1,0:T(8,128)(2,1)S(1)} %copy-done.50, bf16[2048,64]{0,1:T(8,128)(2,1)S(1)} %get-tuple-element.255, bf16[2048,64]{0,1:T(8,128)(2,1)S(1)} %get-tuple-element.254, bf16[2048,512]{0,1:T(8,128)(2,1)} %get-tuple-element.253, bf16[2048,512]{0,1:T(8,128)(2,1)} %get-tuple-element.252), kind=kOutput, calls=%fused_computation.7 | convolution fusion | flops 7269777408 | bytes 14548992 | tf_op jit(solution)/shard_map/dot_general | solution.py:41
  356.7 42.7 %scatter_6.1 = (f32[128,1536]{1,0:T(8,128)S(1)}, f32[24,128]{1,0:T(8,128)S(1)}, bf16[128,768]{1,0:T(8,128)(2,1)S(1)}, bf16[128,768]{1,0:T(8,128)(2,1)S(1)}, bf16[128,768]{1,0:T(8,128)(2,1)S(1)}) custom-call(bf16[16,128,1536]{2,1,0:T(8,128)(2,1)S(1)} %bitcast.206, f32[16,24,128]{2,1,0:T(8,128)S(1)} %dynamic_update_slice.3.refs_1_, ...), custom_call_target="tpu_custom_call" | custom-call | tf_op jit(solution)/shard_map/scatter_6/pallas_call | solution.py:616
  408.6 4.0 convolution_convert_fusion.2.grad_ref
  414.9 14.9 %attend_grads.1 = (bf16[128,1536]{1,0:T(8,128)(2,1)S(1)}, bf16[2048,512]{1,0:T(8,128)(2,1)S(1)}, bf16[2048,512]{1,0:T(8,128)(2,1)}) custom-call(bf16[128,1536]{1,0:T(8,128)(2,1)S(1)} %copy-done.14, bf16[128,1536]{1,0:T(8,128)(2,1)S(1)} %convolution_convert_fusion.2.grad_ref, bf16[2048,1024]{1,0:T(8,128)(2,1)} %bitcast.196, bf16[2048,1024]{1,0:T(8,128)(2,1)} %bitcast.197, ...), custom_call_target="tpu_custom_call" | custom-call | tf_op jit(solution)/shard_map/attend_grads/pallas_call | solution.py:198
  433.5 6.8 %slice.239 = f32[1536,1024]{1,0:T(8,128)} slice(f32[1536,1152]{1,0:T(8,128)} %fusion.8), slice={[0:1536], [0:1024]} | slice | bytes 12582912 | tf_op jit(solution)/shard_map/slice | solution.py:928
  440.4 31.1 %scatter_7.1 = (f32[128,512]{1,0:T(8,128)S(1)}, f32[128,512]{1,0:T(8,128)S(1)}, f32[16,128]{1,0:T(8,128)S(1)}, bf16[128,1536]{1,0:T(8,128)(2,1)S(1)}, bf16[128,1...) custom-call(bf16[16,128,512]{2,1,0:T(8,128)(2,1)S(1)} %bitcast.209, ...), custom_call_target="tpu_custom_call" | custom-call | tf_op jit(solution)/shard_map/scatter_7/pallas_call | solution.py:616
  494.1 25.4 %scatter_8.1 = (f32[48,1536]{1,0:T(8,128)S(1)}, f32[8,128]{1,0:T(8,128)S(1)}, bf16[128,1024]{1,0:T(8,128)(2,1)S(1)}, f32[16,128]{1,0:T(8,128)S(1)}, bf16[256,1536]{1,0:T(8,128)(2,1)S(1)}) custom-call(bf16[16,48,1536]{2,1,0:T(8,128)(2,1)S(1)} %bitcast.205, f32[16,8,128]{2,1,0:T(8,128)S(1)} %pad.25.refs_1_, bf16[128,1024]{1,0:T(8,128)(2,1)S(1)} %pad_maximum_fusion.4.refs_2_, ...), custom_call_target="tpu_custom_call" | custom-call | tf_op jit(solution)/shard_map/scatter_8/pallas_call | solution.py:616
  522.2 36.4 %scatter_9.1 = (f32[48,1536]{1,0:T(8,128)S(1)}, f32[48,1024]{1,0:T(8,128)S(1)}, f32[16,128]{1,0:T(8,128)S(1)}, bf16[768,1024]{1,0:T(8,128)(2,1)S(1)}) custom-call(bf16[16,48,1536]{2,1,0:T(8,128)(2,1)S(1)} %bitcast.204, bf16[16,48,1024]{2,1,0:T(8,128)(2,1)S(1)} %bitcast.208, f32[16,16,128]{2,1,0:T(8,128)S(1)} %broadcast_in_dim.71.refs_2_, ...), custom_call_target="tpu_custom_call" | custom-call | tf_op jit(solution)/shard_map/scatter_9/pallas_call | solution.py:616
  561.4 71.3 %gather_10.1 = (bf16[16,48,1536]{2,1,0:T(8,128)(2,1)S(1)}, bf16[16,48,1024]{2,1,0:T(8,128)(2,1)S(1)}, bf16[16,48,1536]{2,1,0:T(8,128)(2,1)S(1)}, f32[16,8,128]{2...) custom-call(bf16[48,1536]{1,0:T(8,128)(2,1)S(1)} %convert_element_typ, ...), custom_call_target="tpu_custom_call" | custom-call | tf_op jit(solution)/shard_map/gather_10/pallas_call | solution.py:470
  645.0 5.4 copy.89
  650.4 5.3 fusion.63
  661.1 4.0 copy.90
  (345 shorter events, 124.1 us)
Async XLA Ops:
  1.5 66.0 %copy-start.96 = (f32[128]{0:T(128)}, f32[128]{0:T(128)S(1)}, u32[]{:S(2)}) copy-start(f32[128]{0:T(128)S(1)} %convert_bitcast_fusion.2) | copy-start | bytes 1540
  3.9 69.5 %copy-start.92 = (f32[128]{0:T(128)}, f32[128]{0:T(128)S(1)}, u32[]{:S(2)}) copy-start(f32[128]{0:T(128)S(1)} %get-tuple-element.272) | copy-start | bytes 1540
  4.6 62.8 %copy-start.84 = (pred[128,16]{0,1:T(8,128)(4,1)}, pred[128,16]{0,1:T(8,128)(4,1)S(1)}, u32[]{:S(2)}) copy-start(pred[128,16]{0,1:T(8,128)(4,1)S(1)} %fusion.34) | copy-start | bytes 6148
  11.2 60.3 %copy-start.99 = (s32[1,128]{1,0:T(1,128)S(1)}, s32[1,128]{1,0:T(1,128)}, u32[]{:S(2)}) copy-start(s32[1,128]{1,0:T(1,128)} %param.36) | copy-start | bytes 1540
  11.2 62.2 %copy-start.60 = (bf16[1,128,1536]{2,1,0:T(8,128)(2,1)S(1)}, bf16[1,128,1536]{2,1,0:T(8,128)(2,1)}, u32[]{:S(2)}) copy-start(bf16[1,128,1536]{2,1,0:T(8,128)(2,1)} %param.33) | copy-start | bytes 1179652
  77.9 70.1 %copy-start.13 = (bf16[128,1536]{1,0:T(8,128)(2,1)}, bf16[128,1536]{1,0:T(8,128)(2,1)S(1)}, u32[]{:S(2)}) copy-start(bf16[128,1536]{1,0:T(8,128)(2,1)S(1)} %convolution_convert_fusion.3.query_ref) | copy-start | bytes 1179652
  133.3 83.0 %copy-start.54 = (bf16[64,1536]{1,0:T(8,128)(2,1)}, bf16[64,1536]{1,0:T(8,128)(2,1)S(1)}, u32[]{:S(2)}) copy-start(bf16[64,1536]{1,0:T(8,128)(2,1)S(1)} %get-tuple-element.163) | copy-start | bytes 589828
  154.0 53.3 %copy-start.90 = (f32[128]{0:T(128)}, f32[128]{0:T(128)S(1)}, u32[]{:S(2)}) copy-start(f32[128]{0:T(128)S(1)} %fusion.36) | copy-start | bytes 1540
  219.4 44.5 %copy-start.57 = (f32[128,1536]{1,0:T(8,128)S(1)}, f32[128,1536]{1,0:T(8,128)}, u32[]{:S(2)}) copy-start(f32[128,1536]{1,0:T(8,128)} %copy-done.56) | copy-start | bytes 2359300
  219.4 44.5 %copy-start.71 = (bf16[1,128,1536]{2,1,0:T(8,128)(2,1)S(1)}, bf16[1,128,1536]{2,1,0:T(8,128)(2,1)}, u32[]{:S(2)}) copy-start(bf16[1,128,1536]{2,1,0:T(8,128)(2,1)} %param.37) | copy-start | bytes 1179652
  219.4 44.5 %copy-start.72 = (bf16[1,128,1536]{2,1,0:T(8,128)(2,1)S(1)}, bf16[1,128,1536]{2,1,0:T(8,128)(2,1)}, u32[]{:S(2)}) copy-start(bf16[1,128,1536]{2,1,0:T(8,128)(2,1)} %param.38) | copy-start | bytes 1179652
  219.4 44.5 %copy-start.97 = (f32[128]{0:T(128)S(1)}, f32[128]{0:T(128)}, u32[]{:S(2)}) copy-start(f32[128]{0:T(128)} %copy-done.96) | copy-start | bytes 1540
  219.5 44.5 %copy-start.98 = (f32[128]{0:T(128)S(1)}, f32[128]{0:T(128)}, u32[]{:S(2)}) copy-start(f32[128]{0:T(128)} %broadcast_multiply_fusion) | copy-start | bytes 1540
  356.7 46.3 %copy-start.78 = (pred[128,16]{1,0:T(8,128)(4,1)S(1)}, pred[128,16]{1,0:T(8,128)(4,1)}, u32[]{:S(2)}) copy-start(pred[128,16]{1,0:T(8,128)(4,1)} %copy.83) | copy-start | bytes 6148
  356.7 46.3 %copy-start.91 = (f32[128]{0:T(128)S(1)}, f32[128]{0:T(128)}, u32[]{:S(2)}) copy-start(f32[128]{0:T(128)} %copy-done.90) | copy-start | bytes 1540
  356.7 47.5 %copy-start.76 = (bf16[2,8,2,768]{3,1,2,0:T(8,128)(2,1)S(1)}, bf16[2,8,2,768]{3,1,2,0:T(8,128)(2,1)}, u32[]{:S(2)}) copy-start(bf16[2,8,2,768]{3,1,2,0:T(8,128)(2,1)} %copy-done.75) | copy-start | bytes 147460
  356.7 47.5 %copy-start.83 = (f32[1536]{0:T(1024)S(1)}, f32[1536]{0:T(1024)}, u32[]{:S(2)}) copy-start(f32[1536]{0:T(1024)} %mul.380) | copy-start | bytes 18436
  356.7 47.4 %copy-start.95 = (f32[128]{0:T(128)S(1)}, f32[128]{0:T(128)}, u32[]{:S(2)}) copy-start(f32[128]{0:T(128)} %copy-done.94) | copy-start | bytes 1540
  356.7 49.2 %copy-start.101 = (f32[128]{0:T(128)S(1)}, f32[128]{0:T(128)}, u32[]{:S(2)}) copy-start(f32[128]{0:T(128)} %get-tuple-element.273) | copy-start | bytes 1540
  440.3 35.5 %copy-start.44 = (bf16[128,768]{1,0:T(8,128)(2,1)S(1)}, bf16[128,768]{1,0:T(8,128)(2,1)}, u32[]{:S(2)}) copy-start(bf16[128,768]{1,0:T(8,128)(2,1)} %copy-done.43) | copy-start | bytes 589828
  440.3 35.5 %copy-start.79 = (f32[16,768]{1,0:T(8,128)S(1)}, f32[16,768]{1,0:T(8,128)}, u32[]{:S(2)}) copy-start(f32[16,768]{1,0:T(8,128)} %fusion.22) | copy-start | bytes 147460
  440.3 42.2 %copy-start.12 = (bf16[1536,512]{1,0:T(8,128)(2,1)S(1)}, bf16[1536,512]{1,0:T(8,128)(2,1)}, u32[]{:S(2)}) copy-start(bf16[1536,512]{1,0:T(8,128)(2,1)} %copy-done.11) | copy-start | bytes 4718596
  519.6 39.1 %slice-start.4 = ((s8[6291456]{0:T(1024)(128)(4,1)}), s8[4194304]{0:T(1024)(128)(4,1)S(1)}, s32[]{:S(2)}) async-start(s8[6291456]{0:T(1024)(128)(4,1)} %bitcast.219), calls=%async_computation.4 | async-start | bytes 8388608
  521.6 37.1 %slice-start.5 = ((s8[6291456]{0:T(1024)(128)(4,1)}), s8[2097152]{0:T(1024)(128)(4,1)S(1)}, s32[]{:S(2)}) async-start(s8[6291456]{0:T(1024)(128)(4,1)} %bitcast.219), calls=%async_computation.5 | async-start | bytes 4194304
  (84 other events, 497.3 us)

commit v3 on v2

v3 whole, which is shorter than its diff:
```python
import functools

import jax
import jax.numpy as jnp
from jax import lax
from jax.experimental import pallas as pl
from jax.experimental.pallas import tpu as pltpu
from jax.sharding import PartitionSpec as P

H = 12
KVH = 4
HD = 128
EPSILON = 1e-05
MASKED_SCORE = -1e30


def stored_position(stored_rows, local_rows, ctx_count):
    half_rows = local_rows // 2
    owner_rank = stored_rows // local_rows
    within_rows = stored_rows % local_rows
    first_half = owner_rank * half_rows + within_rows
    second_half = (2 * ctx_count - 1 - owner_rank) * half_rows + within_rows - half_rows
    return jnp.where(within_rows < half_rows, first_half, second_half)


def document_of(positions, doc_first):
    return jnp.sum((doc_first[None, :] <= positions[:, None]).astype(jnp.int32), axis=1) - 1


def matmul(left, right):
    return jnp.dot(left, right, preferred_element_type=jnp.float32)


def contract_rows(left, right):
    return lax.dot_general(
        left, right, (((0,), (0,)), ((), ())), preferred_element_type=jnp.float32
    )


def contract_cols(left, right):
    return lax.dot_general(
        left, right, (((1,), (1,)), ((), ())), preferred_element_type=jnp.float32
    )


def rms_inverse(values):
    return lax.rsqrt(jnp.mean(values * values, axis=1, keepdims=True) + EPSILON)


def norm_backward(values, inverse, gain, grad_normed):
    scaled = grad_normed * gain
    inner_sum = jnp.sum(scaled * values, axis=1, keepdims=True)
    grad_values = (
        inverse * scaled - values * (inverse * inverse * inverse) * inner_sum / values.shape[1]
    )
    grad_gain = jnp.sum(grad_normed * values * inverse, axis=0)
    return (grad_values, grad_gain)


def pair_swap(value):
    return lax.ppermute(value, "wa", [(0, 1), (1, 0)])


def my_half(value, side, axis):
    size = value.shape[axis] // 2
    return lax.dynamic_slice_in_dim(value, side * size, size, axis)


def heads_as_rows(value):
    return jnp.concatenate(
        [value[:, h * HD : (h + 1) * HD] for h in range(value.shape[1] // HD)], axis=0
    )


def rows_as_heads(value, rows):
    return jnp.concatenate(
        [value[h * rows : (h + 1) * rows] for h in range(value.shape[0] // rows)], axis=1
    )


def seen(query_ref, key_ref, first, count, groups):
    key_pos, key_doc = key_ref[pl.ds(first, count), 0:1], key_ref[pl.ds(first, count), 1:2]
    query_pos, query_doc = query_ref[0:1, :], query_ref[1:2, :]
    visible = (key_pos <= query_pos) & (key_doc == query_doc)
    return jnp.concatenate([visible.astype(jnp.float32)] * groups, axis=1) > 0.5


def attend_kernel(block, query_ref, key_ref, value_ref, query_place, key_place, out_ref, lse_ref):
    rows = query_ref.shape[0]
    groups = query_ref.shape[1] // HD
    scale = HD ** (-0.5)
    queries = heads_as_rows(query_ref[...])

    def step(index, carry):
        peak, total, mixed = carry
        first = pl.multiple_of(index * block, block)
        scores = contract_cols(key_ref[pl.ds(first, block), :], queries) * scale
        visible = seen(query_place, key_place, first, block, groups)
        scores = jnp.where(visible, scores, MASKED_SCORE)
        new_peak = jnp.maximum(peak, jnp.max(scores, axis=0, keepdims=True))
        shrink = jnp.exp(peak - new_peak)
        weights = jnp.where(visible, jnp.exp(scores - new_peak), 0.0)
        total = total * shrink + jnp.sum(weights, axis=0, keepdims=True)
        part = contract_rows(value_ref[pl.ds(first, block), :], weights.astype(jnp.bfloat16))
        return new_peak, total, mixed * shrink + part

    width = groups * rows
    initial = (
        jnp.full((1, width), MASKED_SCORE, jnp.float32),
        jnp.zeros((1, width), jnp.float32),
        jnp.zeros((HD, width), jnp.float32),
    )
    peak, total, mixed = lax.fori_loop(0, key_ref.shape[0] // block, step, initial)
    out_ref[...] = rows_as_heads((mixed / total).T, rows)
    lse_ref[0] = peak + jnp.log(total)


def attend_grads_kernel(
    block,
    query_ref,
    grad_ref,
    key_ref,
    value_ref,
    lse_ref,
    delta_ref,
    query_place,
    key_place,
    query_grad_ref,
    key_grad_ref,
    value_grad_ref,
):
    rows = query_ref.shape[0]
    groups = query_ref.shape[1] // HD
    scale = HD ** (-0.5)
    queries = heads_as_rows(query_ref[...])
    grads = heads_as_rows(grad_ref[...])
    lse, delta = lse_ref[0], delta_ref[0]

    def step(index, total):
        first = pl.multiple_of(index * block, block)
        here = pl.ds(first, block)
        keys = key_ref[here, :]
        scores = contract_cols(keys, queries) * scale
        visible = seen(query_place, key_place, first, block, groups)
        probs = jnp.where(visible, jnp.exp(jnp.where(visible, scores, MASKED_SCORE) - lse), 0.0)
        grad_probs = contract_cols(value_ref[here, :], grads)
        grad_scores = (probs * (grad_probs - delta)).astype(jnp.bfloat16)
        key_grad_ref[here, :] = (matmul(grad_scores, queries) * scale).astype(jnp.bfloat16)
        value_grad_ref[here, :] = matmul(probs.astype(jnp.bfloat16), grads).astype(jnp.bfloat16)
        return total + contract_rows(keys, grad_scores)

    total = lax.fori_loop(
        0, key_ref.shape[0] // block, step, jnp.zeros((HD, groups * rows), jnp.float32)
    )
    query_grad_ref[...] = rows_as_heads((total * scale).T, rows).astype(jnp.bfloat16)


def attention_specs(rows, seq_len):
    wide = HD * (H // KVH)
    return dict(
        query=pl.BlockSpec((rows, wide), lambda a: (0, a)),
        key=pl.BlockSpec((seq_len, HD), lambda a: (0, a)),
        value=pl.BlockSpec((seq_len, HD), lambda a: (0, KVH + a)),
        row=pl.BlockSpec((1, 1, rows * (H // KVH)), lambda a: (a, 0, 0)),
        query_place=pl.BlockSpec((2, rows), lambda a: (0, 0)),
        key_place=pl.BlockSpec((seq_len, 2), lambda a: (0, 0)),
    )


def attend_forward(queries, key_value_all, query_place, key_place):
    rows, seq_len = queries.shape[0], key_value_all.shape[0]
    s = attention_specs(rows, seq_len)
    return pl.pallas_call(
        functools.partial(attend_kernel, min(seq_len, 1024)),
        grid=(KVH,),
        out_shape=[
            jax.ShapeDtypeStruct((rows, H * HD), jnp.float32),
            jax.ShapeDtypeStruct((KVH, 1, rows * (H // KVH)), jnp.float32),
        ],
        in_specs=[s["query"], s["key"], s["value"], s["query_place"], s["key_place"]],
        out_specs=[s["query"], s["row"]],
        compiler_params=pltpu.CompilerParams(vmem_limit_bytes=20 * 2**20),
        name="attend",
    )(queries, key_value_all, key_value_all, query_place, key_place)


def attend_grads(queries, grads, key_value_all, lse, delta, query_place, key_place):
    rows, seq_len = queries.shape[0], key_value_all.shape[0]
    s = attention_specs(rows, seq_len)
    return pl.pallas_call(
        functools.partial(attend_grads_kernel, min(seq_len, 1024)),
        grid=(KVH,),
        out_shape=[
            jax.ShapeDtypeStruct((rows, H * HD), jnp.bfloat16),
            jax.ShapeDtypeStruct((seq_len, KVH * HD), jnp.bfloat16),
            jax.ShapeDtypeStruct((seq_len, KVH * HD), jnp.bfloat16),
        ],
        in_specs=[
            s["query"],
            s["query"],
            s["key"],
            s["value"],
            s["row"],
            s["row"],
            s["query_place"],
            s["key_place"],
        ],
        out_specs=[s["query"], s["key"], s["key"]],
        compiler_params=pltpu.CompilerParams(vmem_limit_bytes=32 * 2**20),
        name="attend_grads",
    )(queries, grads, key_value_all, key_value_all, lse, delta, query_place, key_place)

def expert_forward_kernel(
    side_ref, rows_ref, gate_ref, own_in, other_in, own_down, other_down, sdown, acts_ref, mixed_ref
):
    side = side_ref[0]
    hidden, depth = own_down.shape[0] * 2, own_in.shape[0]
    pad = sdown.shape[0]

    def half(size, which):
        return pl.ds(pl.multiple_of(which * size, size), size)

    acts_ref[...] = matmul(rows_ref[:, half(depth, side)], own_in[...]) + matmul(
        rows_ref[:, half(depth, 1 - side)], other_in[...]
    )
    gate_act, up_act = acts_ref[:, :hidden], acts_ref[:, hidden : 2 * hidden]
    hidden_exp = (gate_act * jax.nn.sigmoid(gate_act) * up_act).astype(jnp.bfloat16)
    shared_gact = acts_ref[:, 2 * hidden : 2 * hidden + pad]
    shared_uact = acts_ref[:, 2 * hidden + pad :]
    shared_hidden = (shared_gact * jax.nn.sigmoid(shared_gact) * shared_uact).astype(jnp.bfloat16)
    first, second = hidden_exp[:, : hidden // 2], hidden_exp[:, hidden // 2 :]
    swap = side == 1
    out = matmul(jnp.where(swap, second, first), own_down[...]) + matmul(
        jnp.where(swap, first, second), other_down[...]
    )
    mixed = gate_ref[...] * out.astype(jnp.bfloat16).astype(jnp.float32)
    mixed_ref[...] = (mixed + matmul(shared_hidden, sdown[...])).astype(jnp.bfloat16)


def expert_backward_kernel(
    side_ref,
    rows_ref,
    grad_ref,
    acts_ref,
    gate_ref,
    own_in,
    other_in,
    own_down,
    other_down,
    sdown,
    grad_rows_ref,
    dots_ref,
    gate_own,
    up_own,
    gate_other,
    up_other,
    down_own,
    down_other,
    shared_out,
    sdown_out,
    acts_grad,
    in_total,
    down_total,
    shared_total,
    sdown_total,
):
    low = jnp.bfloat16
    side = side_ref[0]
    hidden, depth = own_down.shape[0] * 2, own_in.shape[0]
    pad = sdown.shape[0]

    def half(size, which):
        return pl.ds(pl.multiple_of(which * size, size), size)

    @pl.when(pl.program_id(0) == 0)
    def _():
        for total in (in_total, down_total, shared_total, sdown_total):
            total[...] = jnp.zeros_like(total)

    rows, grads, gate = rows_ref[...], grad_ref[...], gate_ref[...]
    ours, theirs = contract_cols(grads, own_down[...]), contract_cols(grads, other_down[...])
    swap = side == 1
    grad_hidden = jnp.concatenate(
        [jnp.where(swap, theirs, ours), jnp.where(swap, ours, theirs)], axis=1
    )

    def through(grad, gate_act, up_act, at):
        sigmoid = jax.nn.sigmoid(gate_act)
        silu = gate_act * sigmoid
        width = gate_act.shape[1]
        grad_gate = grad * up_act * sigmoid * (1.0 + gate_act * (1.0 - sigmoid))
        acts_grad[:, at : at + width] = grad_gate.astype(low)
        acts_grad[:, at + width : at + 2 * width] = (grad * silu).astype(low)
        return (silu * up_act).astype(low)

    hidden_exp = through(
        gate * grad_hidden, acts_ref[:, :hidden], acts_ref[:, hidden : 2 * hidden], 0
    )
    shared_hidden = through(
        contract_cols(grads, sdown[...]),
        acts_ref[:, 2 * hidden : 2 * hidden + pad],
        acts_ref[:, 2 * hidden + pad :],
        2 * hidden,
    )
    dots_ref[...] = jnp.sum(grad_hidden * hidden_exp.astype(jnp.float32), axis=1, keepdims=True)
    grad_rows_ref[:, half(depth, side)] = contract_cols(acts_grad[...], own_in[...]).astype(low)
    grad_rows_ref[:, half(depth, 1 - side)] = contract_cols(acts_grad[...], other_in[...]).astype(
        low
    )
    in_total[...] += contract_rows(rows, acts_grad[:, : 2 * hidden])
    shared_total[...] += contract_rows(acts_grad[:, 2 * hidden :], rows)
    picked = (gate * grads.astype(jnp.float32)).astype(low)
    down_total[...] += contract_rows(hidden_exp, picked)
    sdown_total[...] += contract_rows(shared_hidden, grads)

    @pl.when(pl.program_id(0) == pl.num_programs(0) - 1)
    def _():
        mine, other = half(depth, side), half(depth, 1 - side)
        gate_own[...] = in_total[mine, :hidden]
        up_own[...] = in_total[mine, hidden:]
        gate_other[...] = in_total[other, :hidden].astype(low)
        up_other[...] = in_total[other, hidden:].astype(low)
        down_own[...] = down_total[half(hidden // 2, side), :]
        down_other[...] = down_total[half(hidden // 2, 1 - side), :].astype(low)
        shared_out[...] = shared_total[...]
        sdown_out[...] = sdown_total[...]


def whole(value):
    return pl.BlockSpec(value.shape, lambda i: (0,) * len(value.shape))


def by_rows(block, columns):
    return pl.BlockSpec((block, columns), lambda i: (i, 0))


def expert_forward(side, rows, gate, weights):
    total, width = rows.shape
    block, acts = min(total, 256), weights[0].shape[1]
    return pl.pallas_call(
        expert_forward_kernel,
        grid=(total // block,),
        out_shape=[
            jax.ShapeDtypeStruct((total, acts), jnp.float32),
            jax.ShapeDtypeStruct((total, width), jnp.bfloat16),
        ],
        in_specs=[
            pl.BlockSpec(memory_space=pltpu.SMEM),
            by_rows(block, width),
            by_rows(block, 1),
            *map(whole, weights),
        ],
        out_specs=[by_rows(block, acts), by_rows(block, width)],
        compiler_params=pltpu.CompilerParams(vmem_limit_bytes=32 * 2**20),
        name="expert_forward",
    )(side, rows, gate, *weights)


def expert_backward(side, rows, grads, acts, gate, weights):
    total, width = rows.shape
    block, columns = min(total, 256), weights[0].shape[1]
    depth, hidden = weights[0].shape[0], 2 * weights[2].shape[0]
    pad = weights[4].shape[0]
    shape, f32, low = jax.ShapeDtypeStruct, jnp.float32, jnp.bfloat16
    ends = [
        shape((depth, hidden), f32),
        shape((depth, hidden), f32),
        shape((depth, hidden), low),
        shape((depth, hidden), low),
        shape((hidden // 2, width), f32),
        shape((hidden // 2, width), low),
        shape((2 * pad, width), f32),
        shape((pad, width), f32),
    ]
    return pl.pallas_call(
        expert_backward_kernel,
        grid=(total // block,),
        out_shape=[shape((total, width), low), shape((total, 1), f32), *ends],
        in_specs=[
            pl.BlockSpec(memory_space=pltpu.SMEM),
            by_rows(block, width),
            by_rows(block, width),
            by_rows(block, columns),
            by_rows(block, 1),
            *map(whole, weights),
        ],
        out_specs=[by_rows(block, width), by_rows(block, 1), *map(whole, ends)],
        scratch_shapes=[
            pltpu.VMEM((block, columns), low),
            pltpu.VMEM((width, 2 * hidden), f32),
            pltpu.VMEM((hidden, width), f32),
            pltpu.VMEM((2 * pad, width), f32),
            pltpu.VMEM((pad, width), f32),
        ],
        compiler_params=pltpu.CompilerParams(vmem_limit_bytes=60 * 2**20),
        name="expert_backward",
    )(side, rows, grads, acts, gate, *weights)


MESH = pl.DeviceIdType.MESH
NZ, NX, NK = 4, 2, 2
VM = pl.BlockSpec(memory_space=pltpu.VMEM)
HBM = pl.BlockSpec(memory_space=pl.ANY)


def settings(number, held):
    return pltpu.CompilerParams(
        collective_id=number, has_side_effects=True, vmem_limit_bytes=held + 4 * 2**20
    )


def bytes_of(arrays):
    return sum(v.size * v.dtype.itemsize for v in arrays)


def slot_of(z, x, k):
    return (z * NX + x) * NK + k


def place():
    c = lax.axis_index("ctx")
    return c, c // (NX * NK), lax.rem(c // NK, NX), lax.rem(c, NK), lax.axis_index("wa")


def greet(z, x, k, w, pair, plane=True):
    barrier = pltpu.get_barrier_semaphore()

    def hello(device):
        pl.semaphore_signal(barrier, inc=1, device_id=device, device_id_type=MESH)

    hello((slot_of(z, x, 1 - k), w))
    count = 1
    if pair:
        hello((slot_of(z, x, k), 1 - w))
        count += 1
    if plane:
        hello((slot_of(z, 1 - x, k), w))
        count += 1

        @pl.when(z > 0)
        def _():
            hello((slot_of(z - 1, x, k), w))

        @pl.when(z < NZ - 1)
        def _():
            hello((slot_of(z + 1, x, k), w))

        count += jnp.where(z > 0, 1, 0) + jnp.where(z < NZ - 1, 1, 0)
    pl.semaphore_wait(barrier, count)


def carry_steps(plan, shards, targets, sems, x, z, k, w):
    own_sem, pair_send, pair_recv, core_send, core_recv = sems
    partner, sibling = (slot_of(z, x, k), 1 - w), (slot_of(z, x, 1 - k), w)
    plan, outs, columns = zip(*plan) if plan else ((), (), ())
    fulls = [
        targets[o] if c is None else targets[o].at[:, pl.ds(c, shards[i].shape[1])]
        for i, (o, c) in enumerate(zip(outs, columns))
    ]

    def rows_of(i, owner):
        h = shards[i].shape[0]
        if plan[i] == "whole":
            return pl.ds(pl.multiple_of(owner * h, h), h)
        half = h // 2
        return pl.ds(pl.multiple_of(owner * h + k * half, half), half)

    def own(i):
        h = shards[i].shape[0]
        return pltpu.make_async_copy(
            shards[i], fulls[i].at[pl.ds(pl.multiple_of(w * h, h), h)], own_sem.at[i]
        )

    def over_pair(i):
        return pltpu.make_async_remote_copy(
            src_ref=shards[i].at[rows_of(i, 0)] if plan[i] == "core" else shards[i],
            dst_ref=fulls[i] if plan[i] == "swap" else fulls[i].at[rows_of(i, w)],
            send_sem=pair_send.at[i],
            recv_sem=pair_recv.at[i],
            device_id=partner,
            device_id_type=MESH,
        )

    def over_core(i):
        here = fulls[i].at[rows_of(i, 1 - w)]
        return pltpu.make_async_remote_copy(
            src_ref=here,
            dst_ref=here,
            send_sem=core_send.at[i],
            recv_sem=core_recv.at[i],
            device_id=sibling,
            device_id_type=MESH,
        )

    every = range(len(shards))

    def start():
        for i in every:
            over_pair(i).start()
        for i in every:
            if plan[i] != "swap":
                own(i).start()

    def hand_on():
        for i in every:
            over_pair(i).wait_recv()
            if plan[i] == "core":
                over_core(i).start()

    def finish():
        for i in every:
            if plan[i] != "swap":
                own(i).wait()
            over_pair(i).wait_send()
            if plan[i] == "core":
                over_core(i).wait()

    return start, hand_on, finish


def carry_semaphores(count):
    return [pltpu.SemaphoreType.DMA((max(count, 1),)) for _ in range(5)]


def places(results, carry):
    return [VM if kind == "swap" else HBM for (kind, _), _ in zip(carry, results)]


def carried(carry):
    plan, operands, results = [], [], []
    for kind, value in carry:
        parts = value if kind == "join" else [value]
        column = 0
        for v in parts:
            where = column if kind == "join" else None
            plan.append(("whole" if kind == "join" else kind, len(results), where))
            operands.append(v)
            column += v.shape[1]
        rows = parts[0].shape[0] * (1 if kind == "swap" else 2)
        results.append(jax.ShapeDtypeStruct((rows, column), parts[0].dtype))
    return plan, operands, results


def regions_of(values, x_first):
    found = []
    for i, (v, rows) in enumerate(zip(values, x_first)):
        total = v.shape[-2]
        if rows:
            found.append((i, total - rows, rows, True))
        if rows < total:
            found.append((i, 0, total - rows, False))
    return found


def gather_kernel(count, regions, plan, made, *refs):
    ins, shards = refs[:count], refs[count : count + len(plan)]
    refs = refs[count + len(plan) :]
    outs, fulls = refs[:count], refs[count : count + made]
    send_sem, recv_sem, own_sem, *carry_sems = refs[count + made :]
    me, z, x, k, w = place()
    greet(z, x, k, w, made > 0)
    up, down = (slot_of(z + 1, x, k), w), (slot_of(z - 1, x, k), w)
    side, sibling = (slot_of(z, 1 - x, k), w), (slot_of(z, x, 1 - k), w)
    x_first = any(crosses for *_, crosses in regions)

    def copies(route, slot, way, device, first=False):
        for r, (i, row, rows, crosses) in enumerate(regions):
            if route is None or crosses == route:
                here = pl.ds(row, rows)
                yield pltpu.make_async_remote_copy(
                    src_ref=ins[i].at[here] if first else outs[i].at[slot, here],
                    dst_ref=outs[i].at[slot, here],
                    send_sem=send_sem.at[r, slot, way],
                    recv_sem=recv_sem.at[r, slot],
                    device_id=device,
                    device_id_type=MESH,
                )

    def send(*what):
        for c in copies(*what):
            c.start()

    def sent(*what):
        for c in copies(*what):
            c.wait_send()

    def arrived(route, slot):
        for c in copies(route, slot, 0, sibling):
            c.wait_recv()

    def onward(act, route, slot, sign):
        if sign <= 0:

            @pl.when(z < NZ - 1)
            def _():
                act(route, slot, 0, up)

        if sign >= 0:

            @pl.when(z > 0)
            def _():
                act(route, slot, 1, down)

    def across(d, act, wait):
        for sign in (-1, 1) if d else (0,):
            there = z + sign * d

            @pl.when((there >= 0) & (there < NZ))
            def _():
                slot = slot_of(there, 1 - x, k)
                wait(False, slot)
                act(False, slot, 3, sibling)

    def walk(act, wait):
        act(None, me, 2, side, True)

        @pl.when(z < NZ - 1)
        def _():
            act(None, me, 0, up, True)

        @pl.when(z > 0)
        def _():
            act(None, me, 1, down, True)

        act(None, me, 3, sibling, True)
        if x_first:
            slot = slot_of(z, 1 - x, k)
            wait(True, slot)
            onward(act, True, slot, 0)
            act(True, slot, 3, sibling)
        for d in range(1, NZ):
            for sign in (-1, 1):
                there = z + sign * d

                @pl.when((there >= 0) & (there < NZ))
                def _():
                    slot = slot_of(there, x, k)
                    wait(False, slot)
                    if d < NZ - 1:
                        onward(act, False, slot, sign)
                    act(False, slot, 2, side)
                    act(False, slot, 3, sibling)
                    if x_first:
                        for column in (x, 1 - x):
                            slot = slot_of(there, column, k)
                            wait(True, slot)
                            if d < NZ - 1:
                                onward(act, True, slot, sign)
                            act(True, slot, 3, sibling)

            across(d - 1, act, wait)
        across(NZ - 1, act, wait)

    own = [pltpu.make_async_copy(ins[i], outs[i].at[me], own_sem.at[i]) for i in range(count)]
    start, hand_on, finish = carry_steps(plan, shards, fulls, carry_sems, x, z, k, w)
    start()
    walk(send, arrived)
    for o in own:
        o.start()
    hand_on()
    for other in range(NZ * NX):
        arrived(None, other * NK + 1 - k)
    walk(sent, lambda route, slot: None)
    for o in own:
        o.wait()
    finish()


def ctx_gather_kernel(values, carry, number, x_first):
    plan, weights, results = carried(carry)
    regions = regions_of(values, x_first)
    count, made = len(values), len(results)
    n = NZ * NX * NK
    done = pl.pallas_call(
        functools.partial(gather_kernel, count, regions, plan, made),
        out_shape=[jax.ShapeDtypeStruct((n, *v.shape), v.dtype) for v in values] + results,
        in_specs=[VM] * (count + len(weights)),
        out_specs=[HBM] * count + places(results, carry),
        scratch_shapes=[
            pltpu.SemaphoreType.DMA((len(regions), n, 4)),
            pltpu.SemaphoreType.DMA((len(regions), n)),
            pltpu.SemaphoreType.DMA((count,)),
        ]
        + carry_semaphores(len(plan)),
        compiler_params=settings(number, bytes_of([*values, *weights])),
        name=f"gather_{number}",
    )(*values, *weights)
    return done[:count], done[count:]


def scatter_kernel(count, regions, plan, made, *refs):
    ins, shards = refs[:count], refs[count : count + len(plan)]
    refs = refs[count + len(plan) :]
    outs, fulls = refs[:count], refs[count : count + made]
    scratch = refs[count + made :]
    many = len(regions)
    from_core, from_side, to_side, from_low, from_high, to_z = (
        scratch[g * many : (g + 1) * many] for g in range(6)
    )
    send_core, recv_core, send_side, recv_side, send_z, recv_low, recv_high, *carry_sems = scratch[
        6 * many :
    ]
    me, z, x, k, w = place()
    greet(z, x, k, w, made > 0)
    up, down = (slot_of(z + 1, x, k), w), (slot_of(z - 1, x, k), w)
    side, sibling = (slot_of(z, 1 - x, k), w), (slot_of(z, x, 1 - k), w)
    f32 = jnp.float32

    def part(r, zz, xx, core):
        i, row, rows, _ = regions[r]
        return ins[i].at[slot_of(zz, xx, core), pl.ds(row, rows)]

    def core_copy(r, zz, xx):
        pair = zz * NX + xx
        return pltpu.make_async_remote_copy(
            src_ref=part(r, zz, xx, 1 - k),
            dst_ref=from_core[r].at[pair],
            send_sem=send_core.at[r, pair],
            recv_sem=recv_core.at[r, pair],
            device_id=sibling,
            device_id_type=MESH,
        )

    def side_copy(r, at):
        return pltpu.make_async_remote_copy(
            src_ref=to_side[r].at[at],
            dst_ref=from_side[r].at[at],
            send_sem=send_side.at[r, at],
            recv_sem=recv_side.at[r, at],
            device_id=side,
            device_id_type=MESH,
        )

    def z_copy(r, at, low):
        return pltpu.make_async_remote_copy(
            src_ref=to_z[r].at[at],
            dst_ref=(from_low if low else from_high)[r].at[at],
            send_sem=send_z.at[r, at],
            recv_sem=(recv_low if low else recv_high).at[r, at],
            device_id=up if low else down,
            device_id_type=MESH,
        )

    def targets(act, route=None):
        for d in range(NZ - 1, -1, -1):
            for sign in (1, -1) if d else (0,):
                there = z + sign * d

                @pl.when((there >= 0) & (there < NZ))
                def _():
                    for r in range(many):
                        if route is None or regions[r][3] == route:
                            act(r, there, sign)

    start, hand_on, finish = carry_steps(plan, shards, fulls, carry_sems, x, z, k, w)
    start()
    targets(lambda r, zz, sign: core_copy(r, zz, 1 - x).start())
    targets(lambda r, zz, sign: core_copy(r, zz, x).start())

    def chip_sum(r, zz, xx):
        return part(r, zz, xx, k)[...].astype(f32) + from_core[r][zz * NX + xx].astype(f32)

    def cross(r, zz, sign):
        core_copy(r, zz, 1 - x).wait_recv()
        to_side[r][zz] = chip_sum(r, zz, 1 - x).astype(to_side[r].dtype)
        side_copy(r, zz).start()

    targets(cross, False)

    def pass_on(r, at, total, sign):
        low = sign > 0
        came = from_low if low else from_high
        first = (z == 0) if low else (z == NZ - 1)

        @pl.when(first)
        def _():
            to_z[r][at] = total.astype(to_z[r].dtype)

        @pl.when(jnp.logical_not(first))
        def _():
            z_copy(r, at, low).wait_recv()
            to_z[r][at] = (total + came[r][at].astype(f32)).astype(to_z[r].dtype)

        z_copy(r, at, low).start()

    def add_line(r, at, here):
        @pl.when(z > 0)
        def _():
            z_copy(r, at, True).wait_recv()
            here[...] += from_low[r][at].astype(f32)

        @pl.when(z < NZ - 1)
        def _():
            z_copy(r, at, False).wait_recv()
            here[...] += from_high[r][at].astype(f32)

    def along(r, zz, sign):
        i, row, rows, crosses = regions[r]
        here = outs[i].at[pl.ds(row, rows)]
        if not crosses:
            core_copy(r, zz, x).wait_recv()
            side_copy(r, zz).wait_recv()
            total = chip_sum(r, zz, x) + from_side[r][zz].astype(f32)
            if sign:
                pass_on(r, zz, total, sign)
            else:
                here[...] = total
                add_line(r, zz, here)
            return
        for xx in (1 - x, x):
            at = zz * NX + xx
            core_copy(r, zz, xx).wait_recv()
            total = chip_sum(r, zz, xx)
            if sign:
                pass_on(r, at, total, sign)
                continue
            here[...] = total
            add_line(r, at, here)
            if xx is x:
                side_copy(r, 0).wait_recv()
                here[...] += from_side[r][0].astype(f32)
            else:
                to_side[r][0] = here[...].astype(to_side[r].dtype)
                side_copy(r, 0).start()

    targets(along)
    hand_on()

    def settle(r, zz, sign):
        core_copy(r, zz, 1 - x).wait_send()
        core_copy(r, zz, x).wait_send()
        if not regions[r][3]:
            side_copy(r, zz).wait_send()
            if sign:
                z_copy(r, zz, sign > 0).wait_send()
        elif sign:
            z_copy(r, zz * NX, sign > 0).wait_send()
            z_copy(r, zz * NX + 1, sign > 0).wait_send()
        else:
            side_copy(r, 0).wait_send()

    targets(settle)
    finish()


def ctx_scatter_kernel(values, carry, number, x_first):
    plan, weights, results = carried(carry)
    regions = regions_of(values, x_first)
    count, made, many = len(values), len(results), len(regions)
    dma = pltpu.SemaphoreType.DMA
    scratch = []
    for straight, crossing in ((8, 8), (4, 1), (4, 1), (4, 8), (4, 8), (4, 8)):
        scratch += [
            pltpu.VMEM(
                (crossing if crosses else straight, rows, values[i].shape[2]), values[i].dtype
            )
            for i, _, rows, crosses in regions
        ]
    done = pl.pallas_call(
        functools.partial(scatter_kernel, count, regions, plan, made),
        out_shape=[jax.ShapeDtypeStruct(v.shape[1:], jnp.float32) for v in values] + results,
        in_specs=[VM] * (count + len(weights)),
        out_specs=[VM] * count + places(results, carry),
        scratch_shapes=scratch
        + [dma((many, NZ * NX)) for _ in range(7)]
        + carry_semaphores(len(plan)),
        compiler_params=settings(number, 3 * bytes_of(values) + bytes_of(weights)),
        name=f"scatter_{number}",
    )(*values, *weights)
    return done[:count], done[count:]


def planned():
    return lax.axis_size("ctx") == NZ * NX * NK and lax.axis_size("wa") == 2


def wa_gather(carry):
    joined = [jnp.concatenate(v, axis=1) if kind == "join" else v for kind, v in carry]
    return [
        pair_swap(v) if kind == "swap" else lax.all_gather(v, "wa", axis=0, tiled=True)
        for (kind, _), v in zip(carry, joined)
    ]


def ctx_gather(values, carry, number, x_first):
    if planned():
        return ctx_gather_kernel(values, carry, number, x_first)
    return [lax.all_gather(v, "ctx", axis=0) for v in values], wa_gather(carry)


def ctx_scatter_sum(values, carry, number, x_first):
    if planned():
        return ctx_scatter_kernel(values, carry, number, x_first)
    summed = [lax.psum_scatter(v, "ctx", scatter_dimension=0).astype(jnp.float32) for v in values]
    return summed, wa_gather(carry)


def per_device(
    tokens,
    doc_starts,
    routes,
    valid,
    teacher,
    out_grad,
    norm1_gain,
    w_query,
    w_key,
    w_value,
    w_out,
    norm2_gain,
    w_router,
    shared_gate,
    shared_up,
    shared_down,
    expert_gate,
    expert_up,
    expert_down,
):
    ctx_count = lax.axis_size("ctx")
    ctx_rank = lax.axis_index("ctx")
    wa_count = lax.axis_size("wa")
    side = lax.axis_index("wa")
    local_rows = tokens.shape[1]
    seq_len = local_rows * ctx_count
    groups = H // KVH
    kv_width = KVH * HD
    experts = w_router.shape[1]
    width = tokens.shape[2]
    lanes = 128
    shared_half = shared_down.shape[0]
    run = shared_half // ctx_count
    low = jnp.bfloat16

    gain_rows = width // wa_count // lanes
    valid_rows = valid[0].astype(jnp.float32)
    small = jnp.zeros((16, lanes), jnp.float32)
    small = small.at[:gain_rows].set(norm1_gain.astype(jnp.float32).reshape(gain_rows, lanes))
    small = small.at[8 : 8 + gain_rows].set(
        norm2_gain.astype(jnp.float32).reshape(gain_rows, lanes)
    )
    small = small.at[6].set(valid_rows)
    tokens_there = pair_swap(tokens[0])
    small_there = pair_swap(small)
    small_all = jnp.where(
        side == 0, jnp.stack([small, small_there]), jnp.stack([small_there, small])
    )
    gain_one = small_all[:, :gain_rows].reshape(width)
    gain_two = small_all[:, 8 : 8 + gain_rows].reshape(width)
    valid_here = jnp.sum(small_all[:, 6])

    doc_first = doc_starts[0]
    own_rows = ctx_rank * local_rows + jnp.arange(local_rows, dtype=jnp.int32)
    query_pos = stored_position(own_rows, local_rows, ctx_count)
    query_place = jnp.stack([query_pos, document_of(query_pos, doc_first)])
    key_pos = stored_position(jnp.arange(seq_len, dtype=jnp.int32), local_rows, ctx_count)
    key_place = jnp.stack([key_pos, document_of(key_pos, doc_first)], axis=1)

    residual = tokens[0].astype(jnp.float32)
    residual_there = tokens_there.astype(jnp.float32)
    inverse_one = rms_inverse(residual)
    scaled_half = jnp.concatenate(
        [
            my_half(residual * inverse_one, side, 1),
            my_half(residual_there * rms_inverse(residual_there), side, 1),
        ]
    )
    normed_half = (scaled_half * norm1_gain.astype(jnp.float32)).astype(low)
    key_value_part = jnp.concatenate(
        [matmul(normed_half, w_key), matmul(normed_half, w_value)], axis=1
    )
    key_value_there = pair_swap(key_value_part[local_rows:].astype(low))
    key_value_own = (key_value_part[:local_rows] + key_value_there.astype(jnp.float32)).astype(low)
    query_part = matmul(normed_half, w_query)

    def shared_columns(weight):
        return [
            lax.dynamic_slice_in_dim(weight, half * shared_half + ctx_rank * run, run, 1)
            for half in range(wa_count)
        ]

    units = wa_count * run
    blank = jnp.zeros((shared_gate.shape[0], lanes - units), low)
    down_rows = lax.dynamic_slice_in_dim(shared_down, ctx_rank * run, run, 0)
    (key_value_all, valid_all), (
        query_there,
        weight_out,
        router_t,
    ) = ctx_gather(
        [key_value_own, jnp.full((8, lanes), valid_here)],
        [
            ("swap", query_part[local_rows:].astype(low)),
            ("core", w_out),
            ("core", w_router.astype(jnp.float32).T),
        ],
        2,
        [16, 0],
    )
    wide_in = jnp.concatenate(
        [
            expert_gate[0],
            expert_up[0],
            *shared_columns(shared_gate),
            blank,
            *shared_columns(shared_up),
            blank,
        ],
        axis=1,
    )
    wide_in, down, down_rows, key_value_all = lax.optimization_barrier(
        (wide_in, expert_down[0], down_rows, key_value_all)
    )
    down_rows_there = pair_swap(down_rows)
    weight_sdown = jnp.where(
        side == 0,
        jnp.concatenate([down_rows, down_rows_there]),
        jnp.concatenate([down_rows_there, down_rows]),
    )
    weight_sdown = jnp.pad(weight_sdown, ((0, lanes - units), (0, 0)))
    expert_weights = [wide_in, pair_swap(wide_in), down, pair_swap(down), weight_sdown]
    which = jnp.full((1,), side, jnp.int32)
    queries = (query_part[:local_rows] + query_there.astype(jnp.float32)).astype(low)
    key_value_all = key_value_all.reshape(seq_len, 2 * kv_width)
    valid_total = jnp.sum(valid_all[:, 0, 0])
    router_t = router_t.reshape(wa_count, experts, width // wa_count)
    weight_router = jnp.transpose(router_t, (0, 2, 1)).reshape(width, experts).astype(low)
    attn, lse = attend_forward(queries, key_value_all, query_place, key_place)
    attn_low = attn.astype(low)
    hidden_one = residual + matmul(attn_low, weight_out)
    inverse_two = rms_inverse(hidden_one)
    normed_two = (hidden_one * inverse_two * gain_two).astype(low)

    logits = matmul(normed_two, weight_router)
    choose = routes[0][:, :, None] == jnp.arange(experts, dtype=jnp.int32)[None, None, :]
    chosen = jnp.any(choose, axis=1)
    peak = jnp.max(jnp.where(chosen, logits, MASKED_SCORE), axis=1, keepdims=True)
    weights = jnp.where(chosen, jnp.exp(jnp.where(chosen, logits, peak) - peak), 0.0)
    gates = weights / jnp.sum(weights, axis=1, keepdims=True)

    (normed_all, gates_all), _ = ctx_gather([normed_two, gates.T], [], 3, [16, 0])
    normed_all = normed_all.reshape(seq_len, width)
    gate = lax.dynamic_slice_in_dim(gates_all, ctx_rank, 1, 1).reshape(seq_len, 1)
    acts, mixed = expert_forward(which, normed_all, gate, expert_weights)
    (routed,), _ = ctx_scatter_sum(
        [mixed.reshape(ctx_count, local_rows, width)], [], 4, [16]
    )
    produced = hidden_one + routed
    output = produced.astype(low)[None]

    errors = produced - teacher[0].astype(jnp.float32)
    local_error = jnp.sum(valid_rows[:, None] * errors * errors)
    tokens_all = wa_count * seq_len
    grad_out = (
        out_grad[0].astype(jnp.float32)
        + 2.0 * tokens_all / valid_total * valid_rows[:, None] * errors
    )
    (grad_all,), _ = ctx_gather([grad_out.astype(low)], [], 5, [16])
    grad_all = grad_all.reshape(seq_len, width)

    (
        grad_rows,
        gate_dot,
        gate_grad,
        up_grad,
        gate_grad_other,
        up_grad_other,
        down_grad,
        down_grad_other,
        shared_grad,
        sdown_grad,
    ) = expert_backward(which, normed_all, grad_all, acts, gate, expert_weights)
    shared_grad = jnp.concatenate([shared_grad[:units], shared_grad[lanes : lanes + units]])
    sdown_grad = sdown_grad[:units]
    small = jnp.full((ctx_count, experts + 8, local_rows), local_error)
    small = small.at[:, :experts].set(0.0)
    small = lax.dynamic_update_slice(
        small, gate_dot.reshape(ctx_count, 1, local_rows), (0, ctx_rank, 0)
    )
    (grad_back, small), (attn_there, normed_two_there) = ctx_scatter_sum(
        [grad_rows.reshape(ctx_count, local_rows, width), small],
        [
            ("swap", my_half(attn_low, 1 - side, 1)),
            ("swap", my_half(normed_two, 1 - side, 1)),
        ],
        6,
        [16, 0],
    )
    grad_gates = small[:experts].T
    error_total = small[experts, 0]
    grad_logits = (
        gates * (grad_gates - jnp.sum(gates * grad_gates, axis=1, keepdims=True))
    ).astype(low)
    grad_normed = grad_back + contract_cols(grad_logits, weight_router)

    def for_pair(full):
        return ("swap", my_half(full, 1 - side, 0).astype(low))

    def with_pair(full, other):
        return my_half(full, side, 0) + other.astype(jnp.float32)

    grad_hidden_norm, grad_gain_two = norm_backward(hidden_one, inverse_two, gain_two, grad_normed)
    grad_hidden_one = grad_out + grad_hidden_norm
    grad_attn_in = grad_hidden_one.astype(low)
    grad_heads = contract_cols(grad_attn_in, weight_out).astype(low)
    delta = jnp.einsum(
        "tagd,tagd->agt",
        grad_heads.astype(jnp.float32).reshape(local_rows, KVH, groups, HD),
        attn.reshape(local_rows, KVH, groups, HD),
    ).reshape(KVH, 1, groups * local_rows)
    grad_query, grad_keys, grad_values = attend_grads(
        queries, grad_heads, key_value_all, lse, delta, query_place, key_place
    )
    def for_all(vector):
        flat = jnp.zeros((16 * lanes,), jnp.float32).at[: vector.shape[0]].set(vector)
        return jnp.broadcast_to(flat.reshape(16, lanes), (ctx_count, 16, lanes))

    def from_all(summed, size):
        return summed.reshape(16 * lanes)[:size]

    def by_slot(value):
        return value.reshape(ctx_count, value.shape[0] // ctx_count, value.shape[1])

    half_width = width // wa_count
    (grad_key, grad_value, small), (
        da_there,
        logits_there,
        query_grad_there,
        error_there,
        shared_there,
        sdown_there,
    ) = ctx_scatter_sum(
        [
            grad_keys.reshape(ctx_count, local_rows, kv_width),
            grad_values.reshape(ctx_count, local_rows, kv_width),
            for_all(grad_gain_two),
        ],
        [
            ("swap", grad_attn_in),
            ("swap", grad_logits),
            ("swap", grad_query),
            ("swap", jnp.full((8, lanes), error_total)),
            ("swap", my_half(shared_grad, 1 - side, 1).astype(low)),
            for_pair(sdown_grad),
        ],
        7,
        [16, 16, 0],
    )
    error_total = error_total + error_there[0, 0]
    key_value_low = jnp.concatenate([grad_key, grad_value], axis=1).astype(low)
    gain_two_sum = from_all(small, width)

    def weight_grad(mine, right, theirs, right_there):
        mine = my_half(mine, side, 1)
        return (contract_rows(mine, right) + contract_rows(theirs, right_there)).astype(low)

    out_part = weight_grad(attn_low, grad_attn_in, attn_there, da_there)
    router_part = contract_rows(grad_logits, my_half(normed_two, side, 1)) + contract_rows(
        logits_there, normed_two_there
    )
    shared_part = my_half(shared_grad, side, 1) + shared_there.astype(jnp.float32)
    sdown_part = with_pair(sdown_grad, sdown_there).astype(low)
    rows_two = jnp.zeros((16, lanes), jnp.float32)
    rows_two = rows_two.at[: half_width // lanes].set(
        my_half(gain_two_sum, 1 - side, 0).reshape(-1, lanes)
    )
    router_rows = router_part.reshape(experts, half_width // lanes, lanes)
    router_rows = jnp.pad(router_rows, ((0, 0), (0, 8 - half_width // lanes), (0, 0)))
    (out_sum, router_sum), (kv_grad_there, rows_there, down_there) = ctx_scatter_sum(
        [by_slot(out_part), router_rows],
        [("swap", key_value_low), ("swap", rows_two), ("swap", down_grad_other)],
        8,
        [0, 0],
    )
    total_gain_two = my_half(gain_two_sum, side, 0) + rows_there.reshape(-1)[:half_width]

    query_both = jnp.concatenate([grad_query, query_grad_there])
    kv_both = jnp.concatenate([key_value_low, kv_grad_there])
    normed_grad = (
        contract_cols(query_both, w_query)
        + contract_cols(kv_both[:, :kv_width], w_key)
        + contract_cols(kv_both[:, kv_width:], w_value)
    )
    (query_sum, kv_sum, small), (normed_grad_there, gate_there) = ctx_scatter_sum(
        [
            by_slot(contract_rows(normed_half, query_both).astype(low)),
            by_slot(contract_rows(normed_half, kv_both).astype(low)),
            for_all(jnp.sum(normed_grad * scaled_half, axis=0)),
        ],
        [
            ("swap", normed_grad[local_rows:].astype(low)),
            ("swap", gate_grad_other),
        ],
        9,
        [0, 16, 0],
    )
    total_gain_one = from_all(small, half_width)
    low_half, high_half = normed_grad[:local_rows], normed_grad_there.astype(jnp.float32)
    grad_normed_one = jnp.where(
        side == 0,
        jnp.concatenate([low_half, high_half], axis=1),
        jnp.concatenate([high_half, low_half], axis=1),
    )
    grad_residual_norm, _ = norm_backward(residual, inverse_one, gain_one, grad_normed_one)
    grad_input = grad_hidden_one + grad_residual_norm
    (total_query, total_kv, total_out, router_sum, shared_parts, sdown_parts), (up_there,) = ctx_gather(
        [
            query_sum.astype(low),
            kv_sum.astype(low),
            out_sum.astype(low),
            router_sum,
            shared_part.astype(low),
            sdown_part,
        ],
        [("swap", up_grad_other)],
        10,
        [0, 0, 0, 0, 0, sdown_part.shape[0]],
    )
    total_query = total_query.reshape(half_width, width).astype(jnp.float32)
    total_kv = total_kv.reshape(half_width, 2 * kv_width).astype(jnp.float32)
    total_out = total_out.reshape(half_width, width).astype(jnp.float32)
    router_sum = router_sum[:, : half_width // lanes].reshape(experts, half_width)
    row = jnp.arange(ctx_count * units, dtype=jnp.int32)[:, None]
    half, unit = row % units // run, row % run
    column = half * shared_half + row // units * run + unit
    select = (column == jnp.arange(ctx_count * units, dtype=jnp.int32)[None, :]).astype(low)
    total_sgate, total_sup = [
        contract_rows(
            shared_parts[:, first : first + units].reshape(ctx_count * units, half_width), select
        )
        for first in (0, units)
    ]
    down_grad = down_grad + down_there.astype(jnp.float32)
    return (
        error_total / (valid_total * width),
        output,
        grad_input[None],
        total_gain_one,
        total_query,
        total_kv[:, :kv_width],
        total_kv[:, kv_width:],
        total_out,
        total_gain_two,
        router_sum.T,
        total_sgate,
        total_sup,
        sdown_parts.reshape(shared_half, width).astype(jnp.float32),
        (gate_grad + gate_there.astype(jnp.float32))[None],
        (up_grad + up_there.astype(jnp.float32))[None],
        down_grad[None],
    )


def solution(mesh):
    return jax.shard_map(
        per_device,
        mesh=mesh,
        in_specs=(
            P("wa", "ctx", None),
            P("wa", None),
            P("wa", "ctx", None),
            P("wa", "ctx"),
            P("wa", "ctx", None),
            P("wa", "ctx", None),
            P("wa"),
            P("wa", None),
            P("wa", None),
            P("wa", None),
            P("wa", None),
            P("wa"),
            P("wa", None),
            P("wa", None),
            P("wa", None),
            P("wa", None),
            P("ctx", "wa", None),
            P("ctx", "wa", None),
            P("ctx", "wa", None),
        ),
        out_specs=(
            P(),
            P("wa", "ctx", None),
            P("wa", "ctx", None),
            P("wa"),
            P("wa", None),
            P("wa", None),
            P("wa", None),
            P("wa", None),
            P("wa"),
            P("wa", None),
            P("wa", None),
            P("wa", None),
            P("wa", None),
            P("ctx", "wa", None),
            P("ctx", "wa", None),
            P("ctx", "wa", None),
        ),
        check_vma=False,
    )
```

time: 677 us -> 631 us (0.932)
  matrix products: 83.7 us -> 26.8 us
  local copies, waits for them, and re-layouts: 84.1 us -> 57.8 us
  waiting for transfers between devices: 0 us -> 16.6 us
  other arithmetic: 36.3 us -> 46.8 us
    dot_general x8 -> x5, matrix products: 35.6 us -> 5.97 us  [contract_cols(): lax.dot_general(left, right, (((1,), (1,)), ((), ())), preferred_element_...]
    dot_general x8 -> x5, matrix products: 22 us -> 4.93 us  [matmul(): return jnp.dot(left, right, preferred_element_type=jnp.float32)]
    ppermute x0 -> x6, waiting for transfers between devices: none -> 16.6 us  [pair_swap(): return lax.ppermute(value, 'wa', [(0, 1), (1, 0)])]
    slice x6 -> x7, local copies, waits for them, and re-layouts: 19.1 us -> 3.14 us  [the longest x1 1.02 us: per_device(): sdown_grad = sdown_grad[:units]]
    dot_general x11 -> x8, matrix products: 26.1 us -> 15.9 us  [contract_rows(): lax.dot_general(left, right, (((0,), (0,)), ((), ())), preferred_element_...]
    unnamed x223 -> x218, local copies, waits for them, and re-layouts: 37.2 us -> 33 us
    pallas_call x10 -> x11, Pallas kernels: 432 us -> 434 us  [the longest x4 197 us: ctx_gather_kernel(): pl.pallas_call(functools.partial(gather_kernel, count, regions, plan, mad...]
  transfers between devices with their start and end apart: 0 -> 6, of which waited for: 0 -> 2; matrix products, arithmetic and copies ran while one was open for 0% -> 6% of each run, Pallas kernels for 0% -> 7%
where the time goes in v3:
time: 631 us; the launch traced here: 620 us
  Pallas kernels  459 us (73%)
  local copies, waits for them, and re-layouts  57.8 us (9%)
  other arithmetic  46.8 us (7%)
  matrix products  26.8 us (4%)
  waiting for transfers between devices  16.6 us (3%)
  between operations  6.49 us (1%)
    pallas_call x4, Pallas kernels, ctx_gather_kernel(): pl.pallas_call(functools.partial(gather_kernel, count, regions, plan, mad...  197 us
    pallas_call x5, Pallas kernels, ctx_scatter_kernel(): pl.pallas_call(functools.partial(scatter_kernel, count, regions, plan, ma...  179 us
    pallas_call x1, Pallas kernels, expert_backward(): pl.pallas_call(expert_backward_kernel, grid=(total // block,), out_shape=...  39 us
    unnamed x218, local copies, waits for them, and re-layouts  33 us
    pallas_call x1, Pallas kernels, expert_forward(): pl.pallas_call(expert_forward_kernel, grid=(total // block,), out_shape=[...  19.6 us
    ppermute x6, waiting for transfers between devices, pair_swap(): return lax.ppermute(value, 'wa', [(0, 1), (1, 0)])  16.6 us
    dot_general x8, matrix products, contract_rows(): lax.dot_general(left, right, (((0,), (0,)), ((), ())), preferred_element_...  15.9 us
    pallas_call x1, Pallas kernels, attend_grads(): pl.pallas_call(functools.partial(attend_grads_kernel, min(seq_len, 1024))...  13.9 us
  transfers between devices with their start and end apart: 6, of which 2 were waited for; matrix products, arithmetic and copies ran while one was open for 6% of the time, Pallas kernels for 7%

profile of v3, /device:TPU:1, one launch (start us, length us, event | category | flops | bytes accessed | tf_op | source)
XLA Modules:
  0.0 619.7 jit_solution(135545586296315619)
XLA Ops:
  19.5 4.7 concatenate.50.own_in
  31.5 4.7 collective-permute-done.1
  37.0 43.5 %gather_2.1 = (bf16[16,128,1024]{2,1,0:T(8,128)(2,1)S(1)}, f32[16,8,128]{2,1,0:T(8,128)S(1)}, bf16[128,1536]{1,0:T(8,128)(2,1)S(1)}, bf16[1536,1536]{1,0:T(8,128)(2,1)S(1)}, f32[32,768]{1,0:T(8,128)S(1)}) custom-call(bf16[128,1024]{1,0:T(8,128)(2,1)S(1)} %fusion.10.refs_0_, f32[8,128]{1,0:T(8,128)S(1)} %broadcast_in_dim.69.refs_1_, ...), custom_call_target="tpu_custom_call" | custom-call | tf_op jit(solution)/shard_map/gather_2/pallas_call | solution.py:674
  83.4 11.1 %attend.1 = (f32[128,1536]{1,0:T(8,128)S(1)}, f32[4,1,384]{2,1,0:T(1,128)S(1)}) custom-call(bf16[128,1536]{1,0:T(8,128)(2,1)S(1)} %fusion.5.query_ref, bf16[2048,1024]{1,0:T(8,128)(2,1)S(1)} %bitcast.175, bf16[2048,1024]{1,0:T(8,128)(2,1)S(1)} %bitcast.176, s32[2,128]{1,0:T(2,128)S(1)} %copy-done.45, s32[2048,2]{1,0:T(8,128)S(1)} %copy.73.key_place), custom_call_target="tpu_custom_call" | custom-call | tf_op jit(solution)/shard_map/attend/pallas_call | solution.py:173
  98.7 3.2 multiply_reduce_fusion.4
  104.7 43.0 %gather_3.1 = (bf16[16,128,1536]{2,1,0:T(8,128)(2,1)S(1)}, f32[16,16,128]{2,1,0:T(8,128)S(1)}) custom-call(bf16[128,1536]{1,0:T(8,128)(2,1)S(1)} %multiply_convert_fusion.refs_0_, f32[16,128]{1,0:T(8,128)S(1)} %fusion.56.refs_1_), custom_call_target="tpu_custom_call" | custom-call | tf_op jit(solution)/shard_map/gather_3/pallas_call | solution.py:674
  158.6 11.8 %collective-permute-done.4.other_down = bf16[256,1536]{1,0:T(8,128)(2,1)} collective-permute-done((bf16[256,1536]{1,0:T(8,128)(2,1)}, bf16[256,1536]{1,0:T(8,128)(2,1)}, u32[]{:S(2)}, u32[]{:S(2)}) %collective-permute-start.4) | collective-permute-done | bytes 786464 | tf_op jit(solution)/shard_map/ppermute | solution.py:61
  174.3 19.6 %expert_forward.1 = (f32[2048,1280]{1,0:T(8,128)}, bf16[2048,1536]{1,0:T(8,128)(2,1)S(1)}) custom-call(s32[1]{0:T(128)} %bitcast.2.side_ref, bf16[2048,1536]{1,0:T(8,128)(2,1)S(1)} %bitcast.180, f32[2048,1]{1,0:T(8,128)S(1)} %copy.78.gate_ref, bf16[768,1280]{1,0:T(8,128)(2,1)} %concatenate.50.own_in, bf16[768,1280]{1,0:T(8,128)(2,1)} %collective-permute-done.3.other_in, ...), custom_call_target="tpu_custom_call" | custom-call | tf_op jit(solution)/shard_map/expert_forward/pallas_call | solution.py:340
  193.9 43.9 %scatter_4.1 = f32[128,1536]{1,0:T(8,128)S(1)} custom-call(bf16[16,128,1536]{2,1,0:T(8,128)(2,1)S(1)} %bitcast.186), custom_call_target="tpu_custom_call" | custom-call | tf_op jit(solution)/shard_map/scatter_4/pallas_call | solution.py:859
  239.6 40.4 %gather_5.1 = bf16[16,128,1536]{2,1,0:T(8,128)(2,1)S(1)} custom-call(bf16[128,1536]{1,0:T(8,128)(2,1)S(1)} %get-tuple-element.225.refs_0_), custom_call_target="tpu_custom_call" | custom-call | tf_op jit(solution)/shard_map/gather_5/pallas_call | solution.py:674
  282.8 39.0 %expert_backward.1 = (bf16[2048,1536]{1,0:T(8,128)(2,1)}, f32[2048,1]{1,0:T(8,128)}, f32[768,512]{1,0:T(8,128)}, f32[768,512]{1,0:T(8,128)}, bf16[768,512]{1,0:T...) custom-call(s32[1]{0:T(128)} %bitcast.2.side_ref, ...), custom_call_target="tpu_custom_call" | custom-call | tf_op jit(solution)/shard_map/expert_backward/pallas_call | solution.py:375
  329.5 41.2 %scatter_6.1 = (f32[128,1536]{1,0:T(8,128)S(1)}, f32[24,128]{1,0:T(8,128)S(1)}, bf16[128,768]{1,0:T(8,128)(2,1)S(1)}, bf16[128,768]{1,0:T(8,128)(2,1)S(1)}) custom-call(bf16[16,128,1536]{2,1,0:T(8,128)(2,1)S(1)} %bitcast.187, f32[16,24,128]{2,1,0:T(8,128)S(1)} %copy-done.38, bf16[128,768]{1,0:T(8,128)(2,1)S(1)} %copy-done.36, bf16[128,768]{1,0:T(8,128)(2,1)S(1)} %copy-done.35), custom_call_target="tpu_custom_call" | custom-call | tf_op jit(solution)/shard_map/scatter_6/pallas_call | solution.py:859
  383.1 3.0 fusion.21
  394.9 13.9 %attend_grads.1 = (bf16[128,1536]{1,0:T(8,128)(2,1)S(1)}, bf16[2048,512]{1,0:T(8,128)(2,1)S(1)}, bf16[2048,512]{1,0:T(8,128)(2,1)S(1)}) custom-call(bf16[128,1536]{1,0:T(8,128)(2,1)S(1)} %copy-done.19, bf16[128,1536]{1,0:T(8,128)(2,1)S(1)} %copy-done.20, bf16[2048,1024]{1,0:T(8,128)(2,1)S(1)} %bitcast.177, bf16[2048,1024]{1,0:T(8,128)(2,1)S(1)} %bitcast.178, ...), custom_call_target="tpu_custom_call" | custom-call | tf_op jit(solution)/shard_map/attend_grads/pallas_call | solution.py:190
  409.6 35.2 %scatter_7.1 = (f32[128,512]{1,0:T(8,128)S(1)}, f32[128,512]{1,0:T(8,128)S(1)}, f32[16,128]{1,0:T(8,128)S(1)}, bf16[128,1536]{1,0:T(8,128)(2,1)S(1)}, bf16[128,1...) custom-call(bf16[16,128,512]{2,1,0:T(8,128)(2,1)S(1)} %bitcast.191, ...), custom_call_target="tpu_custom_call" | custom-call | tf_op jit(solution)/shard_map/scatter_7/pallas_call | solution.py:859
  447.6 3.2 add_convert_fusion
  450.9 25.6 %scatter_8.1 = (f32[48,1536]{1,0:T(8,128)S(1)}, f32[8,128]{1,0:T(8,128)S(1)}, bf16[128,1024]{1,0:T(8,128)(2,1)S(1)}, f32[16,128]{1,0:T(8,128)S(1)}, bf16[256,1536]{1,0:T(8,128)(2,1)S(1)}) custom-call(bf16[16,48,1536]{2,1,0:T(8,128)(2,1)S(1)} %bitcast.185, f32[16,8,128]{2,1,0:T(8,128)S(1)} %pad.28.refs_1_, bf16[128,1024]{1,0:T(8,128)(2,1)S(1)} %pad_maximum_fusion.3.refs_2_, ...), custom_call_target="tpu_custom_call" | custom-call | tf_op jit(solution)/shard_map/scatter_8/pallas_call | solution.py:859
  481.5 33.3 %scatter_9.1 = (f32[48,1536]{1,0:T(8,128)S(1)}, f32[48,1024]{1,0:T(8,128)S(1)}, f32[16,128]{1,0:T(8,128)S(1)}, bf16[128,768]{1,0:T(8,128)(2,1)S(1)}, bf16[768,512]{1,0:T(8,128)(2,1)S(1)}) custom-call(bf16[16,48,1536]{2,1,0:T(8,128)(2,1)S(1)} %bitcast.184, bf16[16,48,1024]{2,1,0:T(8,128)(2,1)S(1)} %bitcast.193, f32[16,16,128]{2,1,0:T(8,128)S(1)} %broadcast_in_dim.78.refs_2_, ...), custom_call_target="tpu_custom_call" | custom-call | tf_op jit(solution)/shard_map/scatter_9/pallas_call | solution.py:859
  515.7 69.7 %gather_10.1 = (bf16[16,48,1536]{2,1,0:T(8,128)(2,1)S(1)}, bf16[16,48,1024]{2,1,0:T(8,128)(2,1)S(1)}, bf16[16,48,1536]{2,1,0:T(8,128)(2,1)S(1)}, f32[16,8,128]{2...) custom-call(bf16[48,1536]{1,0:T(8,128)(2,1)S(1)} %convert_element_ty, ...), custom_call_target="tpu_custom_call" | custom-call | tf_op jit(solution)/shard_map/gather_10/pallas_call | solution.py:674
  587.0 3.7 fusion
  590.7 3.7 fusion.1
  596.8 3.0 bitcast_convert_fusion
  599.8 3.0 bitcast_convert_fusion.1
  608.9 2.9 add_bitcast_fusion
  (354 shorter events, 106.9 us)
Async XLA Ops:
  0.7 25.3 %collective-permute-start = (bf16[128,1536]{1,0:T(8,128)(2,1)}, bf16[128,1536]{1,0:T(8,128)(2,1)}, u32[]{:S(2)}, u32[]{:S(2)}) collective-permute-start(bf16[128,1536]{1,0:T(8,128)(2,1)} %bitcast.195), channel_id=1, source_target_pairs={{0,1},{1,0},{2,3},{3,2},{4,5},{5,4},{6,7},{7,6},{8,9},{9,8},{10,11... | collective-permute-start | bytes 1179656 | tf_op jit(solution)/shard_map/ppermute | solution.py:61
  5.4 18.7 %collective-permute-start.2 = (f32[16,128]{1,0:T(8,128)S(1)}, f32[16,128]{1,0:T(8,128)S(1)}, u32[]{:S(2)}, u32[]{:S(2)}) collective-permute-start(f32[16,128]{1,0:T(8,128)S(1)} %scatter.30), channel_id=1, source_target_pairs={{0,1},{1,0},{2,3},{3,2},{4,5},{5,4},{6,7},{7,6},{8,9},{9,8},{10,11... | collective-permute-start | bytes 24584 | tf_op jit(solution)/shard_map/ppermute | solution.py:61
  17.9 65.4 %copy-start.8 = (s32[2048,2]{1,0:T(8,128)}, s32[2048,2]{1,0:T(8,128)S(1)}, u32[]{:S(2)}) copy-start(s32[2048,2]{1,0:T(8,128)S(1)} %copy.73.key_place) | copy-start | bytes 49156
  29.3 6.9 %collective-permute-start.1 = (bf16[128,1024]{1,0:T(8,128)(2,1)S(1)}, bf16[128,1024]{1,0:T(8,128)(2,1)S(1)}, u32[]{:S(2)}, u32[]{:S(2)}) collective-permute-start(bf16[128,1024]{1,0:T(8,128)(2,1)S(1)} %fusion.11), channel_id=1, source_target_pairs={{0,1},{1,0},{2,3},{3,2},{4,5},{5,4},{6,7},{7,6},{8,9},{9,8},{10,11... | collective-permute-start | bytes 786440 | tf_op jit(solution)/shard_map/ppermute | solution.py:61
  36.3 47.1 %copy-start.45 = (s32[2,128]{1,0:T(2,128)S(1)}, s32[2,128]{1,0:T(2,128)}, u32[]{:S(2)}) copy-start(s32[2,128]{1,0:T(2,128)} %pad_add_fusion.1.query_place) | copy-start | bytes 3076
  98.5 58.9 %collective-permute-start.5 = (bf16[32,1536]{1,0:T(8,128)(2,1)}, bf16[32,1536]{1,0:T(8,128)(2,1)}, u32[]{:S(2)}, u32[]{:S(2)}) collective-permute-start(bf16[32,1536]{1,0:T(8,128)(2,1)} %constant_dynamic-slice_fusion.2), channel_id=1, source_target_pairs={{0,1},{1,0},{2,3},{3,2},{4,5},{5,4},{6,7},{7,6},{8,9},{9,8},{10,11... | collective-permute-start | bytes 294920 | tf_op jit(solution)/shard_map/ppermute | solution.py:61
  101.9 53.8 %copy-start.103 = (s32[1,128]{1,0:T(1,128)S(1)}, s32[1,128]{1,0:T(1,128)}, u32[]{:S(2)}) copy-start(s32[1,128]{1,0:T(1,128)} %param.36) | copy-start | bytes 1540
  102.6 47.9 %copy-start.93 = (f32[128]{0:T(128)}, f32[128]{0:T(128)S(1)}, u32[]{:S(2)}) copy-start(f32[128]{0:T(128)S(1)} %get-tuple-element.240) | copy-start | bytes 1540
  102.7 67.7 %collective-permute-start.3 = (bf16[768,1280]{1,0:T(8,128)(2,1)}, bf16[768,1280]{1,0:T(8,128)(2,1)}, u32[]{:S(2)}, u32[]{:S(2)}) collective-permute-start(bf16[768,1280]{1,0:T(8,128)(2,1)} %concatenate.50.own_in), channel_id=1, source_target_pairs={{0,1},{1,0},{2,3},{3,2},{4,5},{5,4},{6,7},{7,6},{8,9},{9,8},{10,11... | collective-permute-start | bytes 5898248 | tf_op jit(solution)/shard_map/ppermute | solution.py:61
  104.2 46.3 %copy-start.13 = (bf16[128,1536]{1,0:T(8,128)(2,1)}, bf16[128,1536]{1,0:T(8,128)(2,1)S(1)}, u32[]{:S(2)}) copy-start(bf16[128,1536]{1,0:T(8,128)(2,1)S(1)} %multiply_convert_fusion.refs_0_) | copy-start | bytes 1179652
  104.4 46.1 %copy-start.91 = (f32[128]{0:T(128)}, f32[128]{0:T(128)S(1)}, u32[]{:S(2)}) copy-start(f32[128]{0:T(128)S(1)} %get-tuple-element.245) | copy-start | bytes 1540
  104.7 45.8 %copy-start.92 = (f32[128]{0:T(128)}, f32[128]{0:T(128)S(1)}, u32[]{:S(2)}) copy-start(f32[128]{0:T(128)S(1)} %fusion.29) | copy-start | bytes 1540
  150.9 43.0 %copy-start.7 = (f32[2048,1]{1,0:T(8,128)}, f32[2048,1]{1,0:T(8,128)S(1)}, u32[]{:S(2)}) copy-start(f32[2048,1]{1,0:T(8,128)S(1)} %copy.78.gate_ref) | copy-start | bytes 24580
  150.9 19.5 %collective-permute-start.4 = (bf16[256,1536]{1,0:T(8,128)(2,1)}, bf16[256,1536]{1,0:T(8,128)(2,1)}, u32[]{:S(2)}, u32[]{:S(2)}) collective-permute-start(bf16[256,1536]{1,0:T(8,128)(2,1)} %bitcast.188), channel_id=1, source_target_pairs={{0,1},{1,0},{2,3},{3,2},{4,5},{5,4},{6,7},{7,6},{8,9},{9,8},{10,11... | collective-permute-start | bytes 2359304 | tf_op jit(solution)/shard_map/ppermute | solution.py:61
  155.8 82.1 %copy-start.98 = (f32[128]{0:T(128)}, f32[128]{0:T(128)S(1)}, u32[]{:S(2)}) copy-start(f32[128]{0:T(128)S(1)} %broadcast_multiply_fusion) | copy-start | bytes 1540
  193.9 44.0 %copy-start.51 = (f32[128,1536]{1,0:T(8,128)S(1)}, f32[128,1536]{1,0:T(8,128)}, u32[]{:S(2)}) copy-start(f32[128,1536]{1,0:T(8,128)} %copy-done.50) | copy-start | bytes 2359300
  193.9 44.0 %copy-start.71 = (bf16[1,128,1536]{2,1,0:T(8,128)(2,1)S(1)}, bf16[1,128,1536]{2,1,0:T(8,128)(2,1)}, u32[]{:S(2)}) copy-start(bf16[1,128,1536]{2,1,0:T(8,128)(2,1)} %param.37) | copy-start | bytes 1179652
  193.9 44.0 %copy-start.73 = (bf16[1,128,1536]{2,1,0:T(8,128)(2,1)S(1)}, bf16[1,128,1536]{2,1,0:T(8,128)(2,1)}, u32[]{:S(2)}) copy-start(bf16[1,128,1536]{2,1,0:T(8,128)(2,1)} %param.38) | copy-start | bytes 1179652
  193.9 44.0 %copy-start.101 = (f32[128]{0:T(128)S(1)}, f32[128]{0:T(128)}, u32[]{:S(2)}) copy-start(f32[128]{0:T(128)} %get-tuple-element.241) | copy-start | bytes 1540
  237.9 42.1 %copy-start.10 = (f32[128,1536]{1,0:T(8,128)}, f32[128,1536]{1,0:T(8,128)S(1)}, u32[]{:S(2)}) copy-start(f32[128,1536]{1,0:T(8,128)S(1)} %scatter_4.1) | copy-start | bytes 2359300
  329.5 44.1 %copy-start.84 = (pred[128,16]{1,0:T(8,128)(4,1)S(1)}, pred[128,16]{1,0:T(8,128)(4,1)}, u32[]{:S(2)}) copy-start(pred[128,16]{1,0:T(8,128)(4,1)} %copy.77) | copy-start | bytes 6148
  329.5 46.0 %copy-start.14 = (bf16[128,1536]{1,0:T(8,128)(2,1)S(1)}, bf16[128,1536]{1,0:T(8,128)(2,1)}, u32[]{:S(2)}) copy-start(bf16[128,1536]{1,0:T(8,128)(2,1)} %copy-done.13) | copy-start | bytes 1179652
  329.5 51.2 %slice-start = ((s8[4718592]{0:T(1024)(128)(4,1)}), s8[524288]{0:T(1024)(128)(4,1)S(1)}, s32[]{:S(2)}) async-start(s8[4718592]{0:T(1024)(128)(4,1)} %bitcast.182), calls=%async_computation | async-start | bytes 1048576
  514.8 70.6 %copy-start.31 = (bf16[768,512]{1,0:T(8,128)(2,1)}, bf16[768,512]{1,0:T(8,128)(2,1)S(1)}, u32[]{:S(2)}) copy-start(bf16[768,512]{1,0:T(8,128)(2,1)S(1)} %get-tuple-element.211) | copy-start | bytes 2359300
  (88 other events, 670.9 us)

commit v4 on v3

--- a/solution.py
+++ b/solution.py
@@ -399,6 +399,7 @@
 
 MESH = pl.DeviceIdType.MESH
 NZ, NX, NK = 4, 2, 2
+PIECE = 200_000
 VM = pl.BlockSpec(memory_space=pltpu.VMEM)
 HBM = pl.BlockSpec(memory_space=pl.ANY)
 
@@ -547,8 +548,11 @@
         total = v.shape[-2]
         if rows:
             found.append((i, total - rows, rows, True))
-        if rows < total:
-            found.append((i, 0, total - rows, False))
+        straight = total - rows
+        parts = max(1, -(-straight * v.shape[-1] * v.dtype.itemsize // PIECE))
+        step = -(-straight // parts // 16) * 16 if parts > 1 else max(straight, 1)
+        for first in range(0, straight, step):
+            found.append((i, first, min(step, straight - first), False))
     return found
 
 
@@ -561,45 +565,44 @@
     greet(z, x, k, w, made > 0)
     up, down = (slot_of(z + 1, x, k), w), (slot_of(z - 1, x, k), w)
     side, sibling = (slot_of(z, 1 - x, k), w), (slot_of(z, x, 1 - k), w)
-    x_first = any(crosses for *_, crosses in regions)
-
-    def copies(route, slot, way, device, first=False):
-        for r, (i, row, rows, crosses) in enumerate(regions):
-            if route is None or crosses == route:
-                here = pl.ds(row, rows)
-                yield pltpu.make_async_remote_copy(
-                    src_ref=ins[i].at[here] if first else outs[i].at[slot, here],
-                    dst_ref=outs[i].at[slot, here],
-                    send_sem=send_sem.at[r, slot, way],
-                    recv_sem=recv_sem.at[r, slot],
-                    device_id=device,
-                    device_id_type=MESH,
-                )
+
+    every = range(len(regions))
+    straight = [r for r in every if not regions[r][3]]
+    crossing = [r for r in every if regions[r][3]]
+
+    def copy(r, slot, way, device, first=False):
+        i, row, rows, _ = regions[r]
+        here = pl.ds(row, rows)
+        return pltpu.make_async_remote_copy(
+            src_ref=ins[i].at[here] if first else outs[i].at[slot, here],
+            dst_ref=outs[i].at[slot, here],
+            send_sem=send_sem.at[r, slot, way],
+            recv_sem=recv_sem.at[r, slot],
+            device_id=device,
+            device_id_type=MESH,
+        )
 
     def send(*what):
-        for c in copies(*what):
-            c.start()
+        copy(*what).start()
 
     def sent(*what):
-        for c in copies(*what):
-            c.wait_send()
-
-    def arrived(route, slot):
-        for c in copies(route, slot, 0, sibling):
-            c.wait_recv()
-
-    def onward(act, route, slot, sign):
+        copy(*what).wait_send()
+
+    def arrived(r, slot):
+        copy(r, slot, 0, sibling).wait_recv()
+
+    def onward(act, r, slot, sign):
         if sign <= 0:
 
             @pl.when(z < NZ - 1)
             def _():
-                act(route, slot, 0, up)
+                act(r, slot, 0, up)
 
         if sign >= 0:
 
             @pl.when(z > 0)
             def _():
-                act(route, slot, 1, down)
+                act(r, slot, 1, down)
 
     def across(d, act, wait):
         for sign in (-1, 1) if d else (0,):
@@ -608,26 +611,31 @@
             @pl.when((there >= 0) & (there < NZ))
             def _():
                 slot = slot_of(there, 1 - x, k)
-                wait(False, slot)
-                act(False, slot, 3, sibling)
+                for r in straight:
+                    wait(r, slot)
+                    act(r, slot, 3, sibling)
 
     def walk(act, wait):
-        act(None, me, 2, side, True)
+        for r in every:
+            act(r, me, 2, side, True)
 
         @pl.when(z < NZ - 1)
         def _():
-            act(None, me, 0, up, True)
+            for r in every:
+                act(r, me, 0, up, True)
 
         @pl.when(z > 0)
         def _():
-            act(None, me, 1, down, True)
-
-        act(None, me, 3, sibling, True)
-        if x_first:
-            slot = slot_of(z, 1 - x, k)
-            wait(True, slot)
-            onward(act, True, slot, 0)
-            act(True, slot, 3, sibling)
+            for r in every:
+                act(r, me, 1, down, True)
+
+        for r in every:
+            act(r, me, 3, sibling, True)
+        slot = slot_of(z, 1 - x, k)
+        for r in crossing:
+            wait(r, slot)
+            onward(act, r, slot, 0)
+            act(r, slot, 3, sibling)
         for d in range(1, NZ):
             for sign in (-1, 1):
                 there = z + sign * d
@@ -635,18 +643,19 @@
                 @pl.when((there >= 0) & (there < NZ))
                 def _():
                     slot = slot_of(there, x, k)
-                    wait(False, slot)
-                    if d < NZ - 1:
-                        onward(act, False, slot, sign)
-                    act(False, slot, 2, side)
-                    act(False, slot, 3, sibling)
-                    if x_first:
+                    for r in straight:
+                        wait(r, slot)
+                        if d < NZ - 1:
+                            onward(act, r, slot, sign)
+                        act(r, slot, 2, side)
+                        act(r, slot, 3, sibling)
+                    for r in crossing:
                         for column in (x, 1 - x):
                             slot = slot_of(there, column, k)
-                            wait(True, slot)
+                            wait(r, slot)
                             if d < NZ - 1:
-                                onward(act, True, slot, sign)
-                            act(True, slot, 3, sibling)
+                                onward(act, r, slot, sign)
+                            act(r, slot, 3, sibling)
 
             across(d - 1, act, wait)
         across(NZ - 1, act, wait)
@@ -659,8 +668,9 @@
         o.start()
     hand_on()
     for other in range(NZ * NX):
-        arrived(None, other * NK + 1 - k)
-    walk(sent, lambda route, slot: None)
+        for r in every:
+            arrived(r, other * NK + 1 - k)
+    walk(sent, lambda r, slot: None)
     for o in own:
         o.wait()
     finish()
@@ -1016,7 +1026,8 @@
         jnp.concatenate([down_rows_there, down_rows]),
     )
     weight_sdown = jnp.pad(weight_sdown, ((0, lanes - units), (0, 0)))
-    expert_weights = [wide_in, pair_swap(wide_in), down, pair_swap(down), weight_sdown]
+    down_there = pair_swap(down)
+    expert_weights = [wide_in, pair_swap(wide_in), down, down_there, weight_sdown]
     which = jnp.full((1,), side, jnp.int32)
     queries = (query_part[:local_rows] + query_there.astype(jnp.float32)).astype(low)
     key_value_all = key_value_all.reshape(seq_len, 2 * kv_width)
@@ -1025,6 +1036,7 @@
     weight_router = jnp.transpose(router_t, (0, 2, 1)).reshape(width, experts).astype(low)
     attn, lse = attend_forward(queries, key_value_all, query_place, key_place)
     attn_low = attn.astype(low)
+    attn_low, expert_weights[3] = lax.optimization_barrier((attn_low, expert_weights[3]))
     hidden_one = residual + matmul(attn_low, weight_out)
     inverse_two = rms_inverse(hidden_one)
     normed_two = (hidden_one * inverse_two * gain_two).astype(low)

time: 631 us -> 608 us (0.964)
  Pallas kernels: 459 us -> 445 us
  waiting for transfers between devices: 16.6 us -> 3.64 us
  local copies, waits for them, and re-layouts: 57.8 us -> 67.5 us
    ppermute x6, waiting for transfers between devices: 16.6 us -> 3.64 us  [pair_swap(): return lax.ppermute(value, 'wa', [(0, 1), (1, 0)])]
    pallas_call x5, Pallas kernels: 179 us -> 170 us  [ctx_scatter_kernel(): pl.pallas_call(functools.partial(scatter_kernel, count, regions, plan, ma...]
    unnamed x218 -> x216, local copies, waits for them, and re-layouts: 33 us -> 39.9 us
  transfers between devices with their start and end apart: 6 -> 6, of which waited for: 2 -> 1; matrix products, arithmetic and copies ran while one was open for 6% -> 7% of each run, Pallas kernels for 7% -> 9%
where the time goes in v4:
time: 608 us; the launch traced here: 600 us
  Pallas kernels  445 us (73%)
  local copies, waits for them, and re-layouts  67.5 us (11%)
  other arithmetic  47.4 us (8%)
  matrix products  25.4 us (4%)
  between operations  6.38 us (1%)
    pallas_call x4, Pallas kernels, ctx_gather_kernel(): pl.pallas_call(functools.partial(gather_kernel, count, regions, plan, mad...  191 us
    pallas_call x5, Pallas kernels, ctx_scatter_kernel(): pl.pallas_call(functools.partial(scatter_kernel, count, regions, plan, ma...  170 us
    unnamed x216, local copies, waits for them, and re-layouts  39.9 us
    pallas_call x1, Pallas kernels, expert_backward(): pl.pallas_call(expert_backward_kernel, grid=(total // block,), out_shape=...  38.9 us
    pallas_call x1, Pallas kernels, expert_forward(): pl.pallas_call(expert_forward_kernel, grid=(total // block,), out_shape=[...  19.7 us
    pallas_call x1, Pallas kernels, attend_grads(): pl.pallas_call(functools.partial(attend_grads_kernel, min(seq_len, 1024))...  13.9 us
    dot_general x8, matrix products, contract_rows(): lax.dot_general(left, right, (((0,), (0,)), ((), ())), preferred_element_...  12.3 us
  transfers between devices with their start and end apart: 6, of which 1 were waited for; matrix products, arithmetic and copies ran while one was open for 7% of the time, Pallas kernels for 9%

profile of v4, /device:TPU:1, one launch (start us, length us, event | category | flops | bytes accessed | tf_op | source)
XLA Modules:
  0.0 600.3 jit_solution(2165885508335260912)
XLA Ops:
  19.5 4.7 concatenate.50.own_in
  32.6 3.6 collective-permute-done.1
  36.9 44.2 %gather_2.1 = (bf16[16,128,1024]{2,1,0:T(8,128)(2,1)S(1)}, f32[16,8,128]{2,1,0:T(8,128)S(1)}, bf16[128,1536]{1,0:T(8,128)(2,1)S(1)}, bf16[1536,1536]{1,0:T(8,128)(2,1)S(1)}, f32[32,768]{1,0:T(8,128)S(1)}) custom-call(bf16[128,1024]{1,0:T(8,128)(2,1)S(1)} %fusion.10.refs_0_, f32[8,128]{1,0:T(8,128)S(1)} %broadcast_in_dim.69.refs_1_, ...), custom_call_target="tpu_custom_call" | custom-call | tf_op jit(solution)/shard_map/gather_2/pallas_call | solution.py:684
  93.8 11.0 %attend.1 = (f32[128,1536]{1,0:T(8,128)S(1)}, f32[4,1,384]{2,1,0:T(1,128)S(1)}) custom-call(bf16[128,1536]{1,0:T(8,128)(2,1)S(1)} %fusion.5.query_ref, bf16[2048,1024]{1,0:T(8,128)(2,1)S(1)} %bitcast.175, bf16[2048,1024]{1,0:T(8,128)(2,1)S(1)} %bitcast.176, s32[2,128]{1,0:T(2,128)S(1)} %copy-done.48, s32[2048,2]{1,0:T(8,128)S(1)} %copy.73.key_place), custom_call_target="tpu_custom_call" | custom-call | tf_op jit(solution)/shard_map/attend/pallas_call | solution.py:173
  112.0 3.2 multiply_reduce_fusion.4
  117.0 41.0 %gather_3.1 = (bf16[16,128,1536]{2,1,0:T(8,128)(2,1)S(1)}, f32[16,16,128]{2,1,0:T(8,128)S(1)}) custom-call(bf16[128,1536]{1,0:T(8,128)(2,1)S(1)} %multiply_convert_fusion.refs_0_, f32[16,128]{1,0:T(8,128)S(1)} %fusion.55.refs_1_), custom_call_target="tpu_custom_call" | custom-call | tf_op jit(solution)/shard_map/gather_3/pallas_call | solution.py:684
  164.6 2.8 copy-done.5
  168.4 19.7 %expert_forward.1 = (f32[2048,1280]{1,0:T(8,128)}, bf16[2048,1536]{1,0:T(8,128)(2,1)S(1)}) custom-call(s32[1]{0:T(128)} %bitcast.2.side_ref, bf16[2048,1536]{1,0:T(8,128)(2,1)S(1)} %bitcast.180, f32[2048,1]{1,0:T(8,128)S(1)} %copy.78.gate_ref, bf16[768,1280]{1,0:T(8,128)(2,1)} %concatenate.50.own_in, bf16[768,1280]{1,0:T(8,128)(2,1)} %collective-permute-done.4.other_in, ...), custom_call_target="tpu_custom_call" | custom-call | tf_op jit(solution)/shard_map/expert_forward/pallas_call | solution.py:340
  188.1 36.5 %scatter_4.1 = f32[128,1536]{1,0:T(8,128)S(1)} custom-call(bf16[16,128,1536]{2,1,0:T(8,128)(2,1)S(1)} %bitcast.184), custom_call_target="tpu_custom_call" | custom-call | tf_op jit(solution)/shard_map/scatter_4/pallas_call | solution.py:869
  226.3 40.1 %gather_5.1 = bf16[16,128,1536]{2,1,0:T(8,128)(2,1)S(1)} custom-call(bf16[128,1536]{1,0:T(8,128)(2,1)S(1)} %get-tuple-element.229.refs_0_), custom_call_target="tpu_custom_call" | custom-call | tf_op jit(solution)/shard_map/gather_5/pallas_call | solution.py:684
  269.1 38.9 %expert_backward.1 = (bf16[2048,1536]{1,0:T(8,128)(2,1)}, f32[2048,1]{1,0:T(8,128)}, f32[768,512]{1,0:T(8,128)}, f32[768,512]{1,0:T(8,128)}, bf16[768,512]{1,0:T...) custom-call(s32[1]{0:T(128)} %bitcast.2.side_ref, ...), custom_call_target="tpu_custom_call" | custom-call | tf_op jit(solution)/shard_map/expert_backward/pallas_call | solution.py:375
  311.1 2.8 copy-done.11
  316.7 40.5 %scatter_6.1 = (f32[128,1536]{1,0:T(8,128)S(1)}, f32[24,128]{1,0:T(8,128)S(1)}, bf16[128,768]{1,0:T(8,128)(2,1)S(1)}, bf16[128,768]{1,0:T(8,128)(2,1)S(1)}) custom-call(bf16[16,128,1536]{2,1,0:T(8,128)(2,1)S(1)} %bitcast.185, f32[16,24,128]{2,1,0:T(8,128)S(1)} %copy-done.37, bf16[128,768]{1,0:T(8,128)(2,1)S(1)} %copy-done.35, bf16[128,768]{1,0:T(8,128)(2,1)S(1)} %copy-done.34), custom_call_target="tpu_custom_call" | custom-call | tf_op jit(solution)/shard_map/scatter_6/pallas_call | solution.py:869
  369.3 4.7 convolution_convert_fusion.1.grad_ref
  382.7 13.9 %attend_grads.1 = (bf16[128,1536]{1,0:T(8,128)(2,1)S(1)}, bf16[2048,512]{1,0:T(8,128)(2,1)S(1)}, bf16[2048,512]{1,0:T(8,128)(2,1)S(1)}) custom-call(bf16[128,1536]{1,0:T(8,128)(2,1)S(1)} %copy-done.19, bf16[128,1536]{1,0:T(8,128)(2,1)S(1)} %copy-done.20, bf16[2048,1024]{1,0:T(8,128)(2,1)S(1)} %bitcast.177, bf16[2048,1024]{1,0:T(8,128)(2,1)S(1)} %bitcast.178, ...), custom_call_target="tpu_custom_call" | custom-call | tf_op jit(solution)/shard_map/attend_grads/pallas_call | solution.py:190
  397.4 34.8 %scatter_7.1 = (f32[128,512]{1,0:T(8,128)S(1)}, f32[128,512]{1,0:T(8,128)S(1)}, f32[16,128]{1,0:T(8,128)S(1)}, bf16[128,1536]{1,0:T(8,128)(2,1)S(1)}, bf16[128,1...) custom-call(bf16[16,128,512]{2,1,0:T(8,128)(2,1)S(1)} %bitcast.186, ...), custom_call_target="tpu_custom_call" | custom-call | tf_op jit(solution)/shard_map/scatter_7/pallas_call | solution.py:869
  437.0 25.7 %scatter_8.1 = (f32[48,1536]{1,0:T(8,128)S(1)}, f32[8,128]{1,0:T(8,128)S(1)}, bf16[128,1024]{1,0:T(8,128)(2,1)S(1)}, f32[16,128]{1,0:T(8,128)S(1)}, bf16[256,1536]{1,0:T(8,128)(2,1)S(1)}) custom-call(bf16[16,48,1536]{2,1,0:T(8,128)(2,1)S(1)} %bitcast.183, f32[16,8,128]{2,1,0:T(8,128)S(1)} %pad.28.refs_1_, bf16[128,1024]{1,0:T(8,128)(2,1)S(1)} %pad_maximum_fusion.3.refs_2_, ...), custom_call_target="tpu_custom_call" | custom-call | tf_op jit(solution)/shard_map/scatter_8/pallas_call | solution.py:869
  467.8 33.0 %scatter_9.1 = (f32[48,1536]{1,0:T(8,128)S(1)}, f32[48,1024]{1,0:T(8,128)S(1)}, f32[16,128]{1,0:T(8,128)S(1)}, bf16[128,768]{1,0:T(8,128)(2,1)S(1)}, bf16[768,512]{1,0:T(8,128)(2,1)S(1)}) custom-call(bf16[16,48,1536]{2,1,0:T(8,128)(2,1)S(1)} %bitcast.182, bf16[16,48,1024]{2,1,0:T(8,128)(2,1)S(1)} %bitcast.188, f32[16,16,128]{2,1,0:T(8,128)S(1)} %broadcast_in_dim.78.refs_2_, ...), custom_call_target="tpu_custom_call" | custom-call | tf_op jit(solution)/shard_map/scatter_9/pallas_call | solution.py:869
  501.6 65.2 %gather_10.1 = (bf16[16,48,1536]{2,1,0:T(8,128)(2,1)S(1)}, bf16[16,48,1024]{2,1,0:T(8,128)(2,1)S(1)}, bf16[16,48,1536]{2,1,0:T(8,128)(2,1)S(1)}, f32[16,8,128]{2...) custom-call(bf16[48,1536]{1,0:T(8,128)(2,1)S(1)} %convert_element_ty, ...), custom_call_target="tpu_custom_call" | custom-call | tf_op jit(solution)/shard_map/gather_10/pallas_call | solution.py:684
  568.5 3.6 fusion
  572.1 3.6 fusion.1
  578.2 3.0 bitcast_convert_fusion
  581.2 3.0 bitcast_convert_fusion.1
  589.5 2.9 add_bitcast_fusion
  (351 shorter events, 111.4 us)
Async XLA Ops:
  0.7 25.3 %collective-permute-start = (bf16[128,1536]{1,0:T(8,128)(2,1)}, bf16[128,1536]{1,0:T(8,128)(2,1)}, u32[]{:S(2)}, u32[]{:S(2)}) collective-permute-start(bf16[128,1536]{1,0:T(8,128)(2,1)} %bitcast.190), channel_id=1, source_target_pairs={{0,1},{1,0},{2,3},{3,2},{4,5},{5,4},{6,7},{7,6},{8,9},{9,8},{10,11... | collective-permute-start | bytes 1179656 | tf_op jit(solution)/shard_map/ppermute | solution.py:61
  5.4 18.7 %collective-permute-start.2 = (f32[16,128]{1,0:T(8,128)S(1)}, f32[16,128]{1,0:T(8,128)S(1)}, u32[]{:S(2)}, u32[]{:S(2)}) collective-permute-start(f32[16,128]{1,0:T(8,128)S(1)} %scatter.30), channel_id=1, source_target_pairs={{0,1},{1,0},{2,3},{3,2},{4,5},{5,4},{6,7},{7,6},{8,9},{9,8},{10,11... | collective-permute-start | bytes 24584 | tf_op jit(solution)/shard_map/ppermute | solution.py:61
  17.9 73.2 %copy-start.9 = (s32[2048,2]{1,0:T(8,128)}, s32[2048,2]{1,0:T(8,128)S(1)}, u32[]{:S(2)}) copy-start(s32[2048,2]{1,0:T(8,128)S(1)} %copy.73.key_place) | copy-start | bytes 49156
  29.3 6.9 %collective-permute-start.1 = (bf16[128,1024]{1,0:T(8,128)(2,1)S(1)}, bf16[128,1024]{1,0:T(8,128)(2,1)S(1)}, u32[]{:S(2)}, u32[]{:S(2)}) collective-permute-start(bf16[128,1024]{1,0:T(8,128)(2,1)S(1)} %fusion.11), channel_id=1, source_target_pairs={{0,1},{1,0},{2,3},{3,2},{4,5},{5,4},{6,7},{7,6},{8,9},{9,8},{10,11... | collective-permute-start | bytes 786440 | tf_op jit(solution)/shard_map/ppermute | solution.py:61
  86.1 24.0 %collective-permute-start.5 = (bf16[32,1536]{1,0:T(8,128)(2,1)}, bf16[32,1536]{1,0:T(8,128)(2,1)}, u32[]{:S(2)}, u32[]{:S(2)}) collective-permute-start(bf16[32,1536]{1,0:T(8,128)(2,1)} %constant_dynamic-slice_fusion.2), channel_id=1, source_target_pairs={{0,1},{1,0},{2,3},{3,2},{4,5},{5,4},{6,7},{7,6},{8,9},{9,8},{10,11... | collective-permute-start | bytes 294920 | tf_op jit(solution)/shard_map/ppermute | solution.py:61
  86.3 25.7 %collective-permute-start.3 = (bf16[256,1536]{1,0:T(8,128)(2,1)}, bf16[256,1536]{1,0:T(8,128)(2,1)}, u32[]{:S(2)}, u32[]{:S(2)}) collective-permute-start(bf16[256,1536]{1,0:T(8,128)(2,1)} %bitcast.11.own_down), channel_id=1, source_target_pairs={{0,1},{1,0},{2,3},{3,2},{4,5},{5,4},{6,7},{7,6},{8,9},{9,8},{10,11... | collective-permute-start | bytes 2359304 | tf_op jit(solution)/shard_map/ppermute | solution.py:61
  87.6 77.0 %collective-permute-start.4 = (bf16[768,1280]{1,0:T(8,128)(2,1)}, bf16[768,1280]{1,0:T(8,128)(2,1)}, u32[]{:S(2)}, u32[]{:S(2)}) collective-permute-start(bf16[768,1280]{1,0:T(8,128)(2,1)} %concatenate.50.own_in), channel_id=1, source_target_pairs={{0,1},{1,0},{2,3},{3,2},{4,5},{5,4},{6,7},{7,6},{8,9},{9,8},{10,11... | collective-permute-start | bytes 5898248 | tf_op jit(solution)/shard_map/ppermute | solution.py:61
  91.0 133.6 %copy-start.100 = (f32[128]{0:T(128)}, f32[128]{0:T(128)S(1)}, u32[]{:S(2)}) copy-start(f32[128]{0:T(128)S(1)} %broadcast_multiply_fusion) | copy-start | bytes 1540
  116.5 44.2 %copy-start.12 = (bf16[128,1536]{1,0:T(8,128)(2,1)}, bf16[128,1536]{1,0:T(8,128)(2,1)S(1)}, u32[]{:S(2)}) copy-start(bf16[128,1536]{1,0:T(8,128)(2,1)S(1)} %multiply_convert_fusion.refs_0_) | copy-start | bytes 1179652
  116.7 44.0 %copy-start.93 = (f32[128]{0:T(128)}, f32[128]{0:T(128)S(1)}, u32[]{:S(2)}) copy-start(f32[128]{0:T(128)S(1)} %get-tuple-element.249) | copy-start | bytes 1540
  116.8 43.9 %copy-start.83 = (f32[128,16]{1,0:T(8,128)}, f32[128,16]{1,0:T(8,128)S(1)}, u32[]{:S(2)}) copy-start(f32[128,16]{1,0:T(8,128)S(1)} %copy.76) | copy-start | bytes 24580
  117.0 41.0 %copy-start.94 = (f32[128]{0:T(128)}, f32[128]{0:T(128)S(1)}, u32[]{:S(2)}) copy-start(f32[128]{0:T(128)S(1)} %fusion.28) | copy-start | bytes 1540
  188.1 36.5 %copy-start.53 = (f32[128,1536]{1,0:T(8,128)S(1)}, f32[128,1536]{1,0:T(8,128)}, u32[]{:S(2)}) copy-start(f32[128,1536]{1,0:T(8,128)} %copy-done.52) | copy-start | bytes 2359300
  188.1 36.5 %copy-start.73 = (bf16[1,128,1536]{2,1,0:T(8,128)(2,1)S(1)}, bf16[1,128,1536]{2,1,0:T(8,128)(2,1)}, u32[]{:S(2)}) copy-start(bf16[1,128,1536]{2,1,0:T(8,128)(2,1)} %param.37) | copy-start | bytes 1179652
  188.1 36.5 %copy-start.75 = (bf16[1,128,1536]{2,1,0:T(8,128)(2,1)S(1)}, bf16[1,128,1536]{2,1,0:T(8,128)(2,1)}, u32[]{:S(2)}) copy-start(bf16[1,128,1536]{2,1,0:T(8,128)(2,1)} %param.38) | copy-start | bytes 1179652
  188.1 36.5 %copy-start.103 = (f32[128]{0:T(128)S(1)}, f32[128]{0:T(128)}, u32[]{:S(2)}) copy-start(f32[128]{0:T(128)} %get-tuple-element.245) | copy-start | bytes 1540
  316.7 43.9 %copy-start.85 = (f32[256,1536]{1,0:T(8,128)S(1)}, f32[256,1536]{1,0:T(8,128)}, u32[]{:S(2)}) copy-start(f32[256,1536]{1,0:T(8,128)} %get-tuple-element.184) | copy-start | bytes 4718596
  316.7 48.5 %copy-start.13 = (bf16[128,1536]{1,0:T(8,128)(2,1)S(1)}, bf16[128,1536]{1,0:T(8,128)(2,1)}, u32[]{:S(2)}) copy-start(bf16[128,1536]{1,0:T(8,128)(2,1)} %copy-done.12) | copy-start | bytes 1179652
  396.7 35.6 %copy-start.25 = (bf16[128,1536]{1,0:T(8,128)(2,1)}, bf16[128,1536]{1,0:T(8,128)(2,1)S(1)}, u32[]{:S(2)}) copy-start(bf16[128,1536]{1,0:T(8,128)(2,1)S(1)} %get-tuple-element.183.refs_5_) | copy-start | bytes 1179652
  397.4 36.2 %copy-start.42 = (bf16[128,768]{1,0:T(8,128)(2,1)S(1)}, bf16[128,768]{1,0:T(8,128)(2,1)}, u32[]{:S(2)}) copy-start(bf16[128,768]{1,0:T(8,128)(2,1)} %copy-done.41) | copy-start | bytes 589828
  397.4 36.2 %copy-start.87 = (f32[16,768]{1,0:T(8,128)S(1)}, f32[16,768]{1,0:T(8,128)}, u32[]{:S(2)}) copy-start(f32[16,768]{1,0:T(8,128)} %fusion.19) | copy-start | bytes 147460
  467.8 33.8 %copy-start.80 = (f32[64,1536]{1,0:T(8,128)S(1)}, f32[64,1536]{1,0:T(8,128)}, u32[]{:S(2)}) copy-start(f32[64,1536]{1,0:T(8,128)} %copy-done.79) | copy-start | bytes 1179652
  467.8 33.9 %copy-start.28 = (bf16[768,512]{1,0:T(8,128)(2,1)S(1)}, bf16[768,512]{1,0:T(8,128)(2,1)}, u32[]{:S(2)}) copy-start(bf16[768,512]{1,0:T(8,128)(2,1)} %get-tuple-element.206.refs_6_) | copy-start | bytes 2359300
  500.8 66.1 %copy-start.30 = (bf16[768,512]{1,0:T(8,128)(2,1)}, bf16[768,512]{1,0:T(8,128)(2,1)S(1)}, u32[]{:S(2)}) copy-start(bf16[768,512]{1,0:T(8,128)(2,1)S(1)} %get-tuple-element.215) | copy-start | bytes 2359300
  (87 other events, 400.8 us)

commit v5 on v4

--- a/solution.py
+++ b/solution.py
@@ -327,7 +327,9 @@
 
 
 def whole(value):
-    return pl.BlockSpec(value.shape, lambda i: (0,) * len(value.shape))
+    return pl.BlockSpec(
+        value.shape, lambda i: (0,) * len(value.shape), pipeline_mode=pl.Buffered(1)
+    )
 
 
 def by_rows(block, columns):
@@ -336,7 +338,7 @@
 
 def expert_forward(side, rows, gate, weights):
     total, width = rows.shape
-    block, acts = min(total, 256), weights[0].shape[1]
+    block, acts = min(total, 512), weights[0].shape[1]
     return pl.pallas_call(
         expert_forward_kernel,
         grid=(total // block,),

time: 608 us -> 607 us (level)
  no operation moved by 1% of the time
where the time goes in v5:
time: 607 us; the launch traced here: 599 us
  Pallas kernels  443 us (73%)
  local copies, waits for them, and re-layouts  67.5 us (11%)
  other arithmetic  47.4 us (8%)
  matrix products  25.4 us (4%)
  between operations  6.38 us (1%)
    pallas_call x4, Pallas kernels, ctx_gather_kernel(): pl.pallas_call(functools.partial(gather_kernel, count, regions, plan, mad...  191 us
    pallas_call x5, Pallas kernels, ctx_scatter_kernel(): pl.pallas_call(functools.partial(scatter_kernel, count, regions, plan, ma...  170 us
    unnamed x216, local copies, waits for them, and re-layouts  39.9 us
    pallas_call x1, Pallas kernels, expert_backward(): pl.pallas_call(expert_backward_kernel, grid=(total // block,), out_shape=...  38.9 us
    pallas_call x1, Pallas kernels, expert_forward(): pl.pallas_call(expert_forward_kernel, grid=(total // block,), out_shape=[...  18.3 us
    pallas_call x1, Pallas kernels, attend_grads(): pl.pallas_call(functools.partial(attend_grads_kernel, min(seq_len, 1024))...  13.9 us
    dot_general x8, matrix products, contract_rows(): lax.dot_general(left, right, (((0,), (0,)), ((), ())), preferred_element_...  12.3 us
  transfers between devices with their start and end apart: 6, of which 1 were waited for; matrix products, arithmetic and copies ran while one was open for 7% of the time, Pallas kernels for 9%

profile of v5, /device:TPU:1, one launch (start us, length us, event | category | flops | bytes accessed | tf_op | source)
XLA Modules:
  0.0 598.9 jit_solution(2797696695530029306)
XLA Ops:
  19.5 4.7 concatenate.50.own_in
  32.6 3.6 collective-permute-done.1
  36.9 44.2 %gather_2.1 = (bf16[16,128,1024]{2,1,0:T(8,128)(2,1)S(1)}, f32[16,8,128]{2,1,0:T(8,128)S(1)}, bf16[128,1536]{1,0:T(8,128)(2,1)S(1)}, bf16[1536,1536]{1,0:T(8,128)(2,1)S(1)}, f32[32,768]{1,0:T(8,128)S(1)}) custom-call(bf16[128,1024]{1,0:T(8,128)(2,1)S(1)} %fusion.10.refs_0_, f32[8,128]{1,0:T(8,128)S(1)} %broadcast_in_dim.69.refs_1_, ...), custom_call_target="tpu_custom_call" | custom-call | tf_op jit(solution)/shard_map/gather_2/pallas_call | solution.py:686
  93.8 11.0 %attend.1 = (f32[128,1536]{1,0:T(8,128)S(1)}, f32[4,1,384]{2,1,0:T(1,128)S(1)}) custom-call(bf16[128,1536]{1,0:T(8,128)(2,1)S(1)} %fusion.5.query_ref, bf16[2048,1024]{1,0:T(8,128)(2,1)S(1)} %bitcast.175, bf16[2048,1024]{1,0:T(8,128)(2,1)S(1)} %bitcast.176, s32[2,128]{1,0:T(2,128)S(1)} %copy-done.48, s32[2048,2]{1,0:T(8,128)S(1)} %copy.73.key_place), custom_call_target="tpu_custom_call" | custom-call | tf_op jit(solution)/shard_map/attend/pallas_call | solution.py:173
  112.0 3.2 multiply_reduce_fusion.4
  117.0 41.0 %gather_3.1 = (bf16[16,128,1536]{2,1,0:T(8,128)(2,1)S(1)}, f32[16,16,128]{2,1,0:T(8,128)S(1)}) custom-call(bf16[128,1536]{1,0:T(8,128)(2,1)S(1)} %multiply_convert_fusion.refs_0_, f32[16,128]{1,0:T(8,128)S(1)} %fusion.55.refs_1_), custom_call_target="tpu_custom_call" | custom-call | tf_op jit(solution)/shard_map/gather_3/pallas_call | solution.py:686
  164.6 2.8 copy-done.5
  168.4 18.3 %expert_forward.1 = (f32[2048,1280]{1,0:T(8,128)}, bf16[2048,1536]{1,0:T(8,128)(2,1)S(1)}) custom-call(s32[1]{0:T(128)} %bitcast.2.side_ref, bf16[2048,1536]{1,0:T(8,128)(2,1)S(1)} %bitcast.180, f32[2048,1]{1,0:T(8,128)S(1)} %copy.78.gate_ref, bf16[768,1280]{1,0:T(8,128)(2,1)} %concatenate.50.own_in, bf16[768,1280]{1,0:T(8,128)(2,1)} %collective-permute-done.4.other_in, ...), custom_call_target="tpu_custom_call" | custom-call | tf_op jit(solution)/shard_map/expert_forward/pallas_call | solution.py:342
  186.7 36.5 %scatter_4.1 = f32[128,1536]{1,0:T(8,128)S(1)} custom-call(bf16[16,128,1536]{2,1,0:T(8,128)(2,1)S(1)} %bitcast.184), custom_call_target="tpu_custom_call" | custom-call | tf_op jit(solution)/shard_map/scatter_4/pallas_call | solution.py:871
  224.9 40.1 %gather_5.1 = bf16[16,128,1536]{2,1,0:T(8,128)(2,1)S(1)} custom-call(bf16[128,1536]{1,0:T(8,128)(2,1)S(1)} %get-tuple-element.229.refs_0_), custom_call_target="tpu_custom_call" | custom-call | tf_op jit(solution)/shard_map/gather_5/pallas_call | solution.py:686
  267.7 38.9 %expert_backward.1 = (bf16[2048,1536]{1,0:T(8,128)(2,1)}, f32[2048,1]{1,0:T(8,128)}, f32[768,512]{1,0:T(8,128)}, f32[768,512]{1,0:T(8,128)}, bf16[768,512]{1,0:T...) custom-call(s32[1]{0:T(128)} %bitcast.2.side_ref, ...), custom_call_target="tpu_custom_call" | custom-call | tf_op jit(solution)/shard_map/expert_backward/pallas_call | solution.py:377
  309.7 2.8 copy-done.11
  315.3 40.6 %scatter_6.1 = (f32[128,1536]{1,0:T(8,128)S(1)}, f32[24,128]{1,0:T(8,128)S(1)}, bf16[128,768]{1,0:T(8,128)(2,1)S(1)}, bf16[128,768]{1,0:T(8,128)(2,1)S(1)}) custom-call(bf16[16,128,1536]{2,1,0:T(8,128)(2,1)S(1)} %bitcast.185, f32[16,24,128]{2,1,0:T(8,128)S(1)} %copy-done.37, bf16[128,768]{1,0:T(8,128)(2,1)S(1)} %copy-done.35, bf16[128,768]{1,0:T(8,128)(2,1)S(1)} %copy-done.34), custom_call_target="tpu_custom_call" | custom-call | tf_op jit(solution)/shard_map/scatter_6/pallas_call | solution.py:871
  367.9 4.7 convolution_convert_fusion.1.grad_ref
  381.3 13.9 %attend_grads.1 = (bf16[128,1536]{1,0:T(8,128)(2,1)S(1)}, bf16[2048,512]{1,0:T(8,128)(2,1)S(1)}, bf16[2048,512]{1,0:T(8,128)(2,1)S(1)}) custom-call(bf16[128,1536]{1,0:T(8,128)(2,1)S(1)} %copy-done.19, bf16[128,1536]{1,0:T(8,128)(2,1)S(1)} %copy-done.20, bf16[2048,1024]{1,0:T(8,128)(2,1)S(1)} %bitcast.177, bf16[2048,1024]{1,0:T(8,128)(2,1)S(1)} %bitcast.178, ...), custom_call_target="tpu_custom_call" | custom-call | tf_op jit(solution)/shard_map/attend_grads/pallas_call | solution.py:190
  396.1 34.8 %scatter_7.1 = (f32[128,512]{1,0:T(8,128)S(1)}, f32[128,512]{1,0:T(8,128)S(1)}, f32[16,128]{1,0:T(8,128)S(1)}, bf16[128,1536]{1,0:T(8,128)(2,1)S(1)}, bf16[128,1...) custom-call(bf16[16,128,512]{2,1,0:T(8,128)(2,1)S(1)} %bitcast.186, ...), custom_call_target="tpu_custom_call" | custom-call | tf_op jit(solution)/shard_map/scatter_7/pallas_call | solution.py:871
  435.7 25.6 %scatter_8.1 = (f32[48,1536]{1,0:T(8,128)S(1)}, f32[8,128]{1,0:T(8,128)S(1)}, bf16[128,1024]{1,0:T(8,128)(2,1)S(1)}, f32[16,128]{1,0:T(8,128)S(1)}, bf16[256,1536]{1,0:T(8,128)(2,1)S(1)}) custom-call(bf16[16,48,1536]{2,1,0:T(8,128)(2,1)S(1)} %bitcast.183, f32[16,8,128]{2,1,0:T(8,128)S(1)} %pad.28.refs_1_, bf16[128,1024]{1,0:T(8,128)(2,1)S(1)} %pad_maximum_fusion.3.refs_2_, ...), custom_call_target="tpu_custom_call" | custom-call | tf_op jit(solution)/shard_map/scatter_8/pallas_call | solution.py:871
  466.4 33.1 %scatter_9.1 = (f32[48,1536]{1,0:T(8,128)S(1)}, f32[48,1024]{1,0:T(8,128)S(1)}, f32[16,128]{1,0:T(8,128)S(1)}, bf16[128,768]{1,0:T(8,128)(2,1)S(1)}, bf16[768,512]{1,0:T(8,128)(2,1)S(1)}) custom-call(bf16[16,48,1536]{2,1,0:T(8,128)(2,1)S(1)} %bitcast.182, bf16[16,48,1024]{2,1,0:T(8,128)(2,1)S(1)} %bitcast.188, f32[16,16,128]{2,1,0:T(8,128)S(1)} %broadcast_in_dim.78.refs_2_, ...), custom_call_target="tpu_custom_call" | custom-call | tf_op jit(solution)/shard_map/scatter_9/pallas_call | solution.py:871
  500.3 65.2 %gather_10.1 = (bf16[16,48,1536]{2,1,0:T(8,128)(2,1)S(1)}, bf16[16,48,1024]{2,1,0:T(8,128)(2,1)S(1)}, bf16[16,48,1536]{2,1,0:T(8,128)(2,1)S(1)}, f32[16,8,128]{2...) custom-call(bf16[48,1536]{1,0:T(8,128)(2,1)S(1)} %convert_element_ty, ...), custom_call_target="tpu_custom_call" | custom-call | tf_op jit(solution)/shard_map/gather_10/pallas_call | solution.py:686
  567.2 3.6 fusion
  570.8 3.6 fusion.1
  576.9 3.0 bitcast_convert_fusion
  579.9 3.0 bitcast_convert_fusion.1
  588.1 2.9 add_bitcast_fusion
  (351 shorter events, 111.4 us)
Async XLA Ops:
  0.7 25.3 %collective-permute-start = (bf16[128,1536]{1,0:T(8,128)(2,1)}, bf16[128,1536]{1,0:T(8,128)(2,1)}, u32[]{:S(2)}, u32[]{:S(2)}) collective-permute-start(bf16[128,1536]{1,0:T(8,128)(2,1)} %bitcast.190), channel_id=1, source_target_pairs={{0,1},{1,0},{2,3},{3,2},{4,5},{5,4},{6,7},{7,6},{8,9},{9,8},{10,11... | collective-permute-start | bytes 1179656 | tf_op jit(solution)/shard_map/ppermute | solution.py:61
  5.4 18.7 %collective-permute-start.2 = (f32[16,128]{1,0:T(8,128)S(1)}, f32[16,128]{1,0:T(8,128)S(1)}, u32[]{:S(2)}, u32[]{:S(2)}) collective-permute-start(f32[16,128]{1,0:T(8,128)S(1)} %scatter.30), channel_id=1, source_target_pairs={{0,1},{1,0},{2,3},{3,2},{4,5},{5,4},{6,7},{7,6},{8,9},{9,8},{10,11... | collective-permute-start | bytes 24584 | tf_op jit(solution)/shard_map/ppermute | solution.py:61
  17.9 73.2 %copy-start.9 = (s32[2048,2]{1,0:T(8,128)}, s32[2048,2]{1,0:T(8,128)S(1)}, u32[]{:S(2)}) copy-start(s32[2048,2]{1,0:T(8,128)S(1)} %copy.73.key_place) | copy-start | bytes 49156
  29.3 6.9 %collective-permute-start.1 = (bf16[128,1024]{1,0:T(8,128)(2,1)S(1)}, bf16[128,1024]{1,0:T(8,128)(2,1)S(1)}, u32[]{:S(2)}, u32[]{:S(2)}) collective-permute-start(bf16[128,1024]{1,0:T(8,128)(2,1)S(1)} %fusion.11), channel_id=1, source_target_pairs={{0,1},{1,0},{2,3},{3,2},{4,5},{5,4},{6,7},{7,6},{8,9},{9,8},{10,11... | collective-permute-start | bytes 786440 | tf_op jit(solution)/shard_map/ppermute | solution.py:61
  86.1 24.0 %collective-permute-start.5 = (bf16[32,1536]{1,0:T(8,128)(2,1)}, bf16[32,1536]{1,0:T(8,128)(2,1)}, u32[]{:S(2)}, u32[]{:S(2)}) collective-permute-start(bf16[32,1536]{1,0:T(8,128)(2,1)} %constant_dynamic-slice_fusion.2), channel_id=1, source_target_pairs={{0,1},{1,0},{2,3},{3,2},{4,5},{5,4},{6,7},{7,6},{8,9},{9,8},{10,11... | collective-permute-start | bytes 294920 | tf_op jit(solution)/shard_map/ppermute | solution.py:61
  86.3 25.7 %collective-permute-start.3 = (bf16[256,1536]{1,0:T(8,128)(2,1)}, bf16[256,1536]{1,0:T(8,128)(2,1)}, u32[]{:S(2)}, u32[]{:S(2)}) collective-permute-start(bf16[256,1536]{1,0:T(8,128)(2,1)} %bitcast.11.own_down), channel_id=1, source_target_pairs={{0,1},{1,0},{2,3},{3,2},{4,5},{5,4},{6,7},{7,6},{8,9},{9,8},{10,11... | collective-permute-start | bytes 2359304 | tf_op jit(solution)/shard_map/ppermute | solution.py:61
  87.6 77.0 %collective-permute-start.4 = (bf16[768,1280]{1,0:T(8,128)(2,1)}, bf16[768,1280]{1,0:T(8,128)(2,1)}, u32[]{:S(2)}, u32[]{:S(2)}) collective-permute-start(bf16[768,1280]{1,0:T(8,128)(2,1)} %concatenate.50.own_in), channel_id=1, source_target_pairs={{0,1},{1,0},{2,3},{3,2},{4,5},{5,4},{6,7},{7,6},{8,9},{9,8},{10,11... | collective-permute-start | bytes 5898248 | tf_op jit(solution)/shard_map/ppermute | solution.py:61
  91.0 132.1 %copy-start.100 = (f32[128]{0:T(128)}, f32[128]{0:T(128)S(1)}, u32[]{:S(2)}) copy-start(f32[128]{0:T(128)S(1)} %broadcast_multiply_fusion) | copy-start | bytes 1540
  116.5 44.2 %copy-start.12 = (bf16[128,1536]{1,0:T(8,128)(2,1)}, bf16[128,1536]{1,0:T(8,128)(2,1)S(1)}, u32[]{:S(2)}) copy-start(bf16[128,1536]{1,0:T(8,128)(2,1)S(1)} %multiply_convert_fusion.refs_0_) | copy-start | bytes 1179652
  116.7 44.0 %copy-start.93 = (f32[128]{0:T(128)}, f32[128]{0:T(128)S(1)}, u32[]{:S(2)}) copy-start(f32[128]{0:T(128)S(1)} %get-tuple-element.249) | copy-start | bytes 1540
  116.8 43.9 %copy-start.83 = (f32[128,16]{1,0:T(8,128)}, f32[128,16]{1,0:T(8,128)S(1)}, u32[]{:S(2)}) copy-start(f32[128,16]{1,0:T(8,128)S(1)} %copy.76) | copy-start | bytes 24580
  117.0 41.0 %copy-start.94 = (f32[128]{0:T(128)}, f32[128]{0:T(128)S(1)}, u32[]{:S(2)}) copy-start(f32[128]{0:T(128)S(1)} %fusion.28) | copy-start | bytes 1540
  186.7 36.5 %copy-start.53 = (f32[128,1536]{1,0:T(8,128)S(1)}, f32[128,1536]{1,0:T(8,128)}, u32[]{:S(2)}) copy-start(f32[128,1536]{1,0:T(8,128)} %copy-done.52) | copy-start | bytes 2359300
  186.7 36.5 %copy-start.73 = (bf16[1,128,1536]{2,1,0:T(8,128)(2,1)S(1)}, bf16[1,128,1536]{2,1,0:T(8,128)(2,1)}, u32[]{:S(2)}) copy-start(bf16[1,128,1536]{2,1,0:T(8,128)(2,1)} %param.37) | copy-start | bytes 1179652
  186.7 36.5 %copy-start.75 = (bf16[1,128,1536]{2,1,0:T(8,128)(2,1)S(1)}, bf16[1,128,1536]{2,1,0:T(8,128)(2,1)}, u32[]{:S(2)}) copy-start(bf16[1,128,1536]{2,1,0:T(8,128)(2,1)} %param.38) | copy-start | bytes 1179652
  186.7 36.5 %copy-start.103 = (f32[128]{0:T(128)S(1)}, f32[128]{0:T(128)}, u32[]{:S(2)}) copy-start(f32[128]{0:T(128)} %get-tuple-element.245) | copy-start | bytes 1540
  315.3 43.9 %copy-start.85 = (f32[256,1536]{1,0:T(8,128)S(1)}, f32[256,1536]{1,0:T(8,128)}, u32[]{:S(2)}) copy-start(f32[256,1536]{1,0:T(8,128)} %get-tuple-element.184) | copy-start | bytes 4718596
  315.3 48.6 %copy-start.13 = (bf16[128,1536]{1,0:T(8,128)(2,1)S(1)}, bf16[128,1536]{1,0:T(8,128)(2,1)}, u32[]{:S(2)}) copy-start(bf16[128,1536]{1,0:T(8,128)(2,1)} %copy-done.12) | copy-start | bytes 1179652
  395.3 35.6 %copy-start.25 = (bf16[128,1536]{1,0:T(8,128)(2,1)}, bf16[128,1536]{1,0:T(8,128)(2,1)S(1)}, u32[]{:S(2)}) copy-start(bf16[128,1536]{1,0:T(8,128)(2,1)S(1)} %get-tuple-element.183.refs_5_) | copy-start | bytes 1179652
  396.1 36.2 %copy-start.42 = (bf16[128,768]{1,0:T(8,128)(2,1)S(1)}, bf16[128,768]{1,0:T(8,128)(2,1)}, u32[]{:S(2)}) copy-start(bf16[128,768]{1,0:T(8,128)(2,1)} %copy-done.41) | copy-start | bytes 589828
  396.1 36.2 %copy-start.87 = (f32[16,768]{1,0:T(8,128)S(1)}, f32[16,768]{1,0:T(8,128)}, u32[]{:S(2)}) copy-start(f32[16,768]{1,0:T(8,128)} %fusion.19) | copy-start | bytes 147460
  466.4 33.9 %copy-start.80 = (f32[64,1536]{1,0:T(8,128)S(1)}, f32[64,1536]{1,0:T(8,128)}, u32[]{:S(2)}) copy-start(f32[64,1536]{1,0:T(8,128)} %copy-done.79) | copy-start | bytes 1179652
  466.4 34.0 %copy-start.28 = (bf16[768,512]{1,0:T(8,128)(2,1)S(1)}, bf16[768,512]{1,0:T(8,128)(2,1)}, u32[]{:S(2)}) copy-start(bf16[768,512]{1,0:T(8,128)(2,1)} %get-tuple-element.206.refs_6_) | copy-start | bytes 2359300
  499.5 66.1 %copy-start.30 = (bf16[768,512]{1,0:T(8,128)(2,1)}, bf16[768,512]{1,0:T(8,128)(2,1)S(1)}, u32[]{:S(2)}) copy-start(bf16[768,512]{1,0:T(8,128)(2,1)S(1)} %get-tuple-element.215) | copy-start | bytes 2359300
  (87 other events, 399.4 us)
